TPU v7x, 256 devices: a whole 4x4x8 slice. The times are simulated.
256 devices in a mesh: inst: 16 (over z, core), tp: 16 (over y, x).
Axes of the slice: x: 4, y: 4, z: 8, core: 2. Of those that a mesh axis runs over, the one named last changes fastest.
Arguments:
- queries: bfloat16 [3, 128, 8192], P(None, 'inst', 'tp'), may hold values from -8 to 8
- new_kv: bfloat16 [3, 128, 2, 1024], P(None, 'inst'), may hold values from -5 to 5
- page_cache: bfloat16 [2048, 2, 256, 1024], P('inst', None, 'tp'), may hold values from -6 to 6
- range_owner: int32 [16, 16], replicated, may hold values from 0 to 127, as said below
- range_start: int32 [16, 16], replicated, may hold values from 0 to 127, as said below
- range_tokens: int32 [16, 16], replicated, may hold values from 1 to 28928, as said below
Outputs:
- attention: bfloat16 [3, 128, 8192], P(None, 'inst', 'tp')
Inputs may be any that keep to these rules, and one draw needn't show every extreme that they name: `range_owner`: every request is homed at instance request // 8. Of the ranges one instance lends, at most 2 belong to requests of one home instance; in every draw one home instance receives exactly 2 ranges from every lender. `range_start`: the ranges of one lender tile its pool without gaps, in order of k: the first starts at page 0 and each next one starts where the previous one's pages end. `range_tokens`: A range of c pages holds more than 256 * (c - 1) positions.
All inputs are finite; a program needn't handle non-finite values.
Results may differ from a plain program's by a relative error of at most 0.003.
Values may be sent and summed in bfloat16 or wider, within the bound.
No kernel may reach another device: no remote copies, remote signals or barrier semaphores. Data moves between devices by JAX's collectives and lax.ppermute only.
A program may use at most 128 MiB of HBM per device.

v0:
```python
import math

import jax
import jax.numpy as jnp
from jax import lax
from jax.sharding import PartitionSpec as P

HEAD_DIM = 128
PAGE = 256
CAP = 2
REQ_INST = 8


VERY_LOW = -1e30


def slot_ranks(homes):
    count = homes.shape[1]
    earlier = jnp.arange(count)[None, :] < jnp.arange(count)[:, None]
    matches = homes[:, :, None] == homes[:, None, :]
    return jnp.sum(matches & earlier[None], axis=2)


def on_device(queries, new_kv, page_cache, range_owner, range_start, range_tokens):
    step_count, local_requests, local_columns = queries.shape
    lenders = lax.axis_size("inst")
    tp_count = lax.axis_size("tp")
    my_inst = lax.axis_index("inst")
    my_tp = lax.axis_index("tp")
    pool_pages, _, slice_tokens, kv_columns = page_cache.shape
    kv_heads = kv_columns // HEAD_DIM
    local_heads = local_columns // HEAD_DIM
    all_heads = local_heads * tp_count
    group_size = all_heads // kv_heads
    score_scale = 1.0 / math.sqrt(HEAD_DIM)
    slot_total = lenders * CAP
    highest = lax.Precision.HIGHEST
    homes = range_owner // REQ_INST
    ranks = slot_ranks(homes)
    local_owner = range_owner - my_inst * REQ_INST
    claim = (
        (homes == my_inst)[:, :, None, None]
        & (ranks[:, :, None, None] == jnp.arange(CAP)[None, None, :, None])
        & (local_owner[:, :, None, None] == jnp.arange(local_requests)[None, None, None, :])
    )
    claim = jnp.sum(claim.astype(jnp.float32), axis=1)
    my_owner = lax.dynamic_index_in_dim(range_owner, my_inst, 0, keepdims=False)
    my_start = lax.dynamic_index_in_dim(range_start, my_inst, 0, keepdims=False)
    my_tokens = lax.dynamic_index_in_dim(range_tokens, my_inst, 0, keepdims=False)
    my_slot = lax.dynamic_index_in_dim(homes * CAP + ranks, my_inst, 0, keepdims=False)
    page_span = (my_tokens + PAGE - 1) // PAGE
    page_ids = jnp.arange(pool_pages)
    page_hot = (page_ids[:, None] >= my_start[None, :]) & (
        page_ids[:, None] < (my_start + page_span)[None, :]
    )
    page_first = jnp.sum(jnp.where(page_hot, my_start[None, :], 0), axis=1)
    page_limit = jnp.sum(jnp.where(page_hot, my_tokens[None, :], 0), axis=1)
    page_slot = jnp.sum(jnp.where(page_hot, my_slot[None, :], 0), axis=1)
    position = (
        (page_ids - page_first)[:, None] * PAGE
        + my_tp * slice_tokens
        + jnp.arange(slice_tokens)[None, :]
    )
    usable = position < page_limit[:, None]
    slot_hot = page_slot[:, None] == jnp.arange(slot_total)[None, :]
    range_slot_hot = my_slot[:, None] == jnp.arange(slot_total)[None, :]
    full_queries = lax.all_gather(queries, "tp", axis=2, tiled=True)
    every_query = lax.all_gather(full_queries, "inst", axis=1, tiled=True)
    page_owner = jnp.sum(jnp.where(page_hot, my_owner[None, :], 0), axis=1)
    picker = (page_owner[:, None] == jnp.arange(lenders * local_requests)[None, :]).astype(
        jnp.bfloat16
    )
    page_queries = jnp.einsum(
        "pr,srx->spx", picker, every_query, preferred_element_type=jnp.float32
    ).astype(jnp.bfloat16)
    query_blocks = page_queries.reshape(step_count, pool_pages, kv_heads, group_size, HEAD_DIM)
    key_rows = page_cache[:, 0].reshape(pool_pages, slice_tokens, kv_heads, HEAD_DIM)
    value_rows = page_cache[:, 1].reshape(pool_pages, slice_tokens, kv_heads, HEAD_DIM)
    scores = (
        jnp.einsum("spkgd,pikd->spkgi", query_blocks, key_rows, preferred_element_type=jnp.float32)
        * score_scale
    )
    usable_mask = usable[None, :, None, None, :]
    scores = jnp.where(usable_mask, scores, VERY_LOW)
    page_max = jnp.max(scores, axis=4)
    range_max = jnp.max(
        jnp.where(page_hot.T[None, :, :, None, None], page_max[:, None], VERY_LOW), axis=2
    )
    page_ref = jnp.max(
        jnp.where(page_hot[None, :, :, None, None], range_max[:, None], VERY_LOW), axis=2
    )
    weights = jnp.where(usable_mask, jnp.exp(scores - page_ref[..., None]), 0.0)
    page_sums = jnp.sum(weights, axis=4)
    page_outs = jnp.einsum(
        "spkgi,pikd->spkgd",
        weights.astype(jnp.bfloat16),
        value_rows,
        preferred_element_type=jnp.float32,
    )
    slot_shape = (lenders, CAP, step_count, all_heads)
    slot_float = slot_hot.astype(jnp.float32)
    slot_outs = jnp.einsum("pl,spkgd->lskgd", slot_float, page_outs, precision=highest)
    slot_sums = jnp.einsum("pl,spkg->lskg", slot_float, page_sums, precision=highest)
    slot_max = jnp.max(
        jnp.where(range_slot_hot[None, :, :, None, None], range_max[:, :, None], VERY_LOW), axis=1
    )
    slot_max = jnp.transpose(slot_max, (1, 0, 2, 3))
    slot_outs = slot_outs.reshape(slot_shape + (HEAD_DIM,))
    slot_sums = slot_sums.reshape(slot_shape)
    slot_max = slot_max.reshape(slot_shape)
    outs, maxima, totals = (
        lax.all_to_all(
            lax.all_to_all(slot_outs, "inst", split_axis=0, concat_axis=0, tiled=True),
            "tp",
            split_axis=3,
            concat_axis=0,
            tiled=True,
        ),
        lax.all_to_all(
            lax.all_to_all(slot_max, "inst", split_axis=0, concat_axis=0, tiled=True),
            "tp",
            split_axis=3,
            concat_axis=0,
            tiled=True,
        ),
        lax.all_to_all(
            lax.all_to_all(slot_sums, "inst", split_axis=0, concat_axis=0, tiled=True),
            "tp",
            split_axis=3,
            concat_axis=0,
            tiled=True,
        ),
    )
    entries = outs.reshape(-1, step_count, local_heads, HEAD_DIM)
    entry_max = maxima.reshape(-1, step_count, local_heads)
    entry_sum = totals.reshape(-1, step_count, local_heads)
    owner_hot = jnp.tile(claim.reshape(slot_total, local_requests), (tp_count, 1)) > 0.5
    local_queries = queries.reshape(step_count, local_requests, local_heads, HEAD_DIM)
    head_group = (my_tp * local_heads + jnp.arange(local_heads)) // group_size
    group_pick = (head_group[:, None] == jnp.arange(kv_heads)[None, :]).astype(jnp.bfloat16)
    fresh_keys = new_kv[:, :, 0].reshape(step_count, local_requests, kv_heads, HEAD_DIM)
    fresh_values = new_kv[:, :, 1].reshape(step_count, local_requests, kv_heads, HEAD_DIM)
    head_keys = jnp.einsum(
        "hk,srkd->srhd", group_pick, fresh_keys, preferred_element_type=jnp.float32
    ).astype(jnp.bfloat16)
    head_values = jnp.einsum(
        "hk,srkd->srhd", group_pick, fresh_values, preferred_element_type=jnp.float32
    ).astype(jnp.bfloat16)
    fresh_scores = (
        jnp.einsum("srhd,trhd->srht", local_queries, head_keys, preferred_element_type=jnp.float32)
        * score_scale
    )
    causal = (jnp.arange(step_count)[None, :] <= jnp.arange(step_count)[:, None])[:, None, None, :]
    fresh_scores = jnp.where(causal, fresh_scores, VERY_LOW)
    fresh_max = jnp.max(fresh_scores, axis=3)
    fresh_weights = jnp.where(causal, jnp.exp(fresh_scores - fresh_max[..., None]), 0.0)
    fresh_sum = jnp.sum(fresh_weights, axis=3)
    fresh_out = jnp.einsum(
        "srht,trhd->srhd",
        fresh_weights.astype(jnp.bfloat16),
        head_values,
        preferred_element_type=jnp.float32,
    )
    owner_mask = owner_hot[:, None, :, None]
    spread_max = jnp.where(owner_mask, entry_max[:, :, None, :], VERY_LOW)
    row_max = jnp.maximum(fresh_max, jnp.max(spread_max, axis=0))
    factor_all = jnp.where(
        owner_mask, jnp.exp(jnp.minimum(entry_max[:, :, None, :] - row_max[None], 0.0)), 0.0
    )
    numerator = jnp.einsum("esrh,eshd->srhd", factor_all, entries, precision=highest)
    denominator = jnp.einsum("esrh,esh->srh", factor_all, entry_sum, precision=highest)
    fresh_factor = jnp.exp(fresh_max - row_max)
    numerator = numerator + fresh_factor[..., None] * fresh_out
    denominator = denominator + fresh_factor * fresh_sum
    result = numerator / denominator[..., None]
    return result.reshape(step_count, local_requests, local_heads * HEAD_DIM).astype(jnp.bfloat16)


def solution(mesh):
    placed = (
        P(None, "inst", "tp"),
        P(None, "inst", None, None),
        P("inst", None, "tp", None),
        P(),
        P(),
        P(),
    )
    return jax.shard_map(
        on_device, mesh=mesh, in_specs=placed, out_specs=P(None, "inst", "tp"), check_vma=False
    )
```

profile of v0, /device:TPU:1, one launch (start us, length us, event | category | flops | bytes accessed | tf_op | source)
XLA Modules:
  0.0 318.7 jit_solution(2001754022968398413)
XLA Ops:
  6.5 22.7 %all_gather.6 = bf16[3,8,8192]{2,1,0:T(8,128)(2,1)} all-gather(bf16[3,8,512]{2,1,0:T(8,128)(2,1)} %param.6), channel_id=1, replica_groups=mesh['inst'=16,'tp'=16] {'tp'}, dimensions={2}, use_global_device_ids=true | all-gather | bytes 417792 | tf_op jit(solution)/shard_map/all_gather | solution.py:67
  29.2 6.3 %fusion.78 = (bf16[128,1,16,1024]{3,2,1,0:T(8,128)(2,1)}, bf16[128,1,16,1024]{3,2,1,0:T(8,128)(2,1)}) fusion(bf16[128,2,16,1024]{3,2,1,0:T(8,128)(2,1)} %param.8), kind=kLoop, calls=%fused_computation.133 | loop fusion | bytes 16777216 | tf_op jit(solution)/shard_map/slice | solution.py:77
  35.6 6.6 %copy.192 = bf16[128,1,16,1024]{0,3,2,1:T(8,128)(2,1)} copy(bf16[128,1,16,1024]{3,2,1,0:T(8,128)(2,1)} %get-tuple-element.15) | data formatting | bytes 8388608
  42.2 6.8 %copy.179 = bf16[128,16,8,128,1]{3,1,4,2,0:T(8,128)(2,1)} copy(bf16[128,16,8,128,1]{0,3,2,1,4:T(8,128)(2,1)} %bitcast.151) | data formatting | bytes 8388608 | tf_op jit(solution)/shard_map/reshape;squeeze | solution.py:77
  49.0 6.6 %copy.193 = bf16[128,1,16,1024]{0,3,2,1:T(8,128)(2,1)} copy(bf16[128,1,16,1024]{3,2,1,0:T(8,128)(2,1)} %get-tuple-element.16) | data formatting | bytes 8388608
  55.6 6.9 %copy.180 = bf16[128,16,8,128,1]{3,1,4,2,0:T(8,128)(2,1)} copy(bf16[128,16,8,128,1]{0,3,2,1,4:T(8,128)(2,1)} %bitcast.152) | data formatting | bytes 8388608 | tf_op jit(solution)/shard_map/reshape;squeeze | solution.py:78
  62.5 0.4 convert_reduce_fusion.1
  63.0 0.7 fusion.72
  64.2 16.8 %all-gather.2.cloned.1.call-done = bf16[3,128,8192]{2,1,0:T(8,128)(2,1)} async-done(((bf16[3,8,8192]{2,1,0:T(8,128)(2,1)}), bf16[3,128,8192]{2,1,0:T(8,128)(2,1)}) %all-gather.2.cloned.1.call-update) | async-done | bytes 6291472 | tf_op jit(solution)/shard_map/all_gather | solution.py:68
  80.9 4.6 %convolution_convert_fusion = bf16[128,3,8192]{2,0,1:T(8,128)(2,1)S(1)} fusion(bf16[3,128,8192]{2,1,0:T(8,128)(2,1)} %all-gather.2.cloned.1.call-done, s32[128]{0:T(128)S(1)} %get-tuple-element.10), kind=kOutput, calls=%fused_computation.7 | convolution fusion | flops 808468480 | bytes 12583424 | tf_op jit(solution)/shard_map/pr,srx->spx/dot_general | solution.py:73
  85.6 1.9 copy.194
  87.5 0.3 copy-done
  87.8 7.0 %bitcast_reduce_fusion = (f32[3,128,8,8]{3,0,2,1:T(4,128)S(1)}, f32[128,8,3,8,16]{4,3,2,1,0:T(8,128)}) fusion(pred[128,16]{1,0:T(8,128)(4,1)S(1)} %add_compare_fusion, bf16[128,16,8,128,1]{3,1,4,2,0:T(8,128)(2,1)S(1)} %copy-done, bf16[3,128,8,8,128]{4,3,2,1,0:T(8,128)(2,1)S(1)} %bitcast.150), kind=kOutput, calls=%fused_computation.1 | convolution fusion | flops 101818368 | bytes 12158976 | tf_op jit(solution)/shard_map/spkgd,pikd->spkgi/dot_general | solution.py:80
  94.7 0.7 copy.147
  95.5 0.5 select_reduce_fusion.2
  96.0 0.5 select_reduce_fusion.1
  96.4 1.5 copy.148
  98.0 12.6 %fusion.4 = f32[3,128,8,8]{3,0,2,1:T(4,128)} fusion(f32[128,8,3,8,16]{4,3,2,1,0:T(8,128)} %get-tuple-element.23, f32[3,128,8,8]{3,0,2,1:T(4,128)S(1)} %copy.148, pred[128,16]{1,0:T(8,128)(4,1)S(1)} %add_compare_fusion), kind=kLoop, calls=%fused_computation.8 | loop fusion | flops 1941504 | bytes 1771520 | tf_op jit(solution)/shard_map/reduce_sum | solution.py:93
  110.5 1.9 copy.172
  112.4 0.3 fusion.26
  112.7 0.7 reshape.320
  113.4 4.7 %all-to-all-start.4 = ((f32[16,1,384]{2,1,0:T(1,128)}), f32[16,1,384]{2,1,0:T(1,128)S(1)}, u32[]{:S(2)}, u32[]{:S(2)}) async-start(f32[16,1,384]{2,1,0:T(1,128)} %reshape.320), calls=%async_computation.4 | async-start | bytes 49152 | tf_op jit(solution)/shard_map/all_to_all | solution.py:127
  118.0 0.5 select_reduce_fusion
  118.5 0.2 copy.156
  118.7 0.2 reshape.302
  118.9 0.7 reshape.316
  119.6 5.7 %all-to-all-done.4 = f32[16,1,384]{2,1,0:T(1,128)S(1)} async-done(((f32[16,1,384]{2,1,0:T(1,128)}), f32[16,1,384]{2,1,0:T(1,128)S(1)}, u32[]{:S(2)}, u32[]{:S(2)}) %all-to-all-start.4) | async-done | bytes 24608 | tf_op jit(solution)/shard_map/all_to_all | solution.py:127
  125.4 3.7 %all-to-all-start.2 = ((f32[16,1,384]{2,1,0:T(1,128)}), f32[16,1,384]{2,1,0:T(1,128)S(1)}, u32[]{:S(2)}, u32[]{:S(2)}) async-start(f32[16,1,384]{2,1,0:T(1,128)} %reshape.316), calls=%async_computation.2 | async-start | bytes 49152 | tf_op jit(solution)/shard_map/all_to_all | solution.py:120
  129.1 13.1 %fusion.16 = f32[3,128,8,8,128]{4,3,0,2,1:T(8,128)} fusion(bf16[128,16,8,128,1]{3,1,4,2,0:T(8,128)(2,1)} %copy.180, f32[128,8,3,8,16]{4,3,2,1,0:T(8,128)} %get-tuple-element.23, f32[3,128,8,8]{3,0,2,1:T(4,128)S(1)} %copy.148, pred[128,16]{1,0:T(8,128)(4,1)S(1)} %add_compare_fusion), kind=kOutput, calls=%fused_computation.19 | convolution fusion | flops 102629376 | bytes 18450432 | tf_op jit(solution)/shard_map/spkgi,pikd->spkgd/dot_general | solution.py:94
  142.1 0.6 broadcast.279
  142.7 0.7 reduce.6
  143.5 0.2 copy.174
  143.6 0.8 reshape.322
  144.5 6.6 %all-to-all-start.5 = ((f32[16,1,384]{2,1,0:T(1,128)}), f32[16,1,384]{2,1,0:T(1,128)S(1)}, u32[]{:S(2)}, u32[]{:S(2)}) async-start(f32[16,1,384]{2,1,0:T(1,128)} %reshape.322), calls=%async_computation.5 | async-start | bytes 49152 | tf_op jit(solution)/shard_map/all_to_all | solution.py:126
  151.1 15.6 %fusion.2 = f32[32,3,8,8,128]{4,0,3,2,1:T(8,128)S(1)} fusion(f32[3,128,8,8,128]{4,3,0,2,1:T(8,128)} %fusion.16, s32[128]{0:T(128)S(1)} %get-tuple-element.7), kind=kOutput, calls=%fused_computation.4 | convolution fusion | flops 1207963648 | bytes 15729152 | tf_op jit(solution)/shard_map/pl,spkgd->lskgd/dot_general | solution.py:102
  166.7 3.4 %copy.152 = f32[16,2,3,64,128]{4,1,3,2,0:T(2,128)} copy(f32[16,2,3,64,128]{4,1,0,3,2:T(2,128)S(1)} %bitcast.155) | data formatting | bytes 6291456 | tf_op jit(solution)/shard_map/reshape | solution.py:108
  170.1 7.5 %all-to-all-start = ((f32[16,2,3,64,128]{4,1,3,2,0:T(2,128)}), f32[16,2,3,64,128]{4,1,3,2,0:T(2,128)S(1)}, u32[]{:S(2)}, u32[]{:S(2)}) async-start(f32[16,2,3,64,128]{4,1,3,2,0:T(2,128)} %copy.152), calls=%async_computation | async-start | bytes 6291456 | tf_op jit(solution)/shard_map/all_to_all | solution.py:113
  177.7 0.7 reduce.4
  178.4 0.2 copy.158
  178.6 0.9 reshape.318
  179.5 69.2 %all-to-all-done = f32[16,2,3,64,128]{4,1,3,2,0:T(2,128)S(1)} async-done(((f32[16,2,3,64,128]{4,1,3,2,0:T(2,128)}), f32[16,2,3,64,128]{4,1,3,2,0:T(2,128)S(1)}, u32[]{:S(2)}, u32[]{:S(2)}) %all-to-all-start) | async-done | bytes 3145760 | tf_op jit(solution)/shard_map/all_to_all | solution.py:113
  248.6 6.9 %all-to-all-start.3 = ((f32[16,1,384]{2,1,0:T(1,128)}), f32[16,1,384]{2,1,0:T(1,128)S(1)}, u32[]{:S(2)}, u32[]{:S(2)}) async-start(f32[16,1,384]{2,1,0:T(1,128)} %reshape.318), calls=%async_computation.3 | async-start | bytes 49152 | tf_op jit(solution)/shard_map/all_to_all | solution.py:119
  255.6 3.5 %copy.153 = f32[16,2,3,64,128]{4,1,0,2,3:T(2,128)} copy(f32[16,2,3,64,128]{4,1,3,2,0:T(2,128)S(1)} %all-to-all-done) | data formatting | bytes 6291456 | tf_op jit(solution)/shard_map/all_to_all | solution.py:113
  259.1 2.9 all-to-all-done.3
  262.0 3.7 %all-to-all-start.1 = ((f32[16,2,3,64,128]{4,1,0,2,3:T(2,128)}), f32[16,2,3,64,128]{4,1,0,2,3:T(2,128)S(1)}, u32[]{:S(2)}, u32[]{:S(2)}) async-start(f32[16,2,3,64,128]{4,1,0,2,3:T(2,128)} %copy.153), calls=%async_computation.1 | async-start | bytes 6291456 | tf_op jit(solution)/shard_map/all_to_all | solution.py:112
  266.2 0.4 slice_reduce_fusion
  266.6 0.2 fusion.23
  267.3 0.7 fusion.60
  268.0 0.2 copy.170
  268.1 0.2 fusion.24
  268.3 0.8 fusion.42
  269.1 0.7 reduce.7
  269.8 0.3 reshape.323
  270.1 1.5 copy.176
  271.6 2.0 copy.184
  273.6 1.4 reduce.5
  275.0 0.3 reshape.319
  275.3 1.5 copy.160
  276.8 1.4 copy.161
  278.4 1.2 fusion.25
  279.6 0.7 multiply_add_fusion
  280.3 27.8 %all-to-all-done.1 = f32[16,2,3,64,128]{4,1,0,2,3:T(2,128)S(1)} async-done(((f32[16,2,3,64,128]{4,1,0,2,3:T(2,128)}), f32[16,2,3,64,128]{4,1,0,2,3:T(2,128)S(1)}, u32[]{:S(2)}, u32[]{:S(2)}) %all-to-all-start.1) | async-done | bytes 3145760 | tf_op jit(solution)/shard_map/all_to_all | solution.py:112
  308.1 1.4 copy.154
  309.4 2.4 fusion.22
  (46 shorter events, 1.7 us)
Async XLA Ops:
  6.5 74.4 %all-gather.2.cloned.1.call-start = ((), (), s32[]{:S(2)}) async-start(), calls=%async_computation.6 | async-start | bytes 6684672 | tf_op jit(solution)/shard_map/all_gather | solution.py:68
  55.6 6.9 %copy-start.4 = (s32[16,16]{1,0:T(8,128)S(1)}, s32[16,16]{1,0:T(8,128)}, u32[]{:S(2)}) copy-start(s32[16,16]{1,0:T(8,128)} %param.9) | copy-start | bytes 3076
  85.6 2.2 copy-start
  113.4 12.0 %all-to-all-start.4 = ((f32[16,1,384]{2,1,0:T(1,128)}), f32[16,1,384]{2,1,0:T(1,128)S(1)}, u32[]{:S(2)}, u32[]{:S(2)}) async-start(f32[16,1,384]{2,1,0:T(1,128)} %reshape.320), calls=%async_computation.4 | async-start | bytes 49152 | tf_op jit(solution)/shard_map/all_to_all | solution.py:127
  125.4 19.1 %all-to-all-start.2 = ((f32[16,1,384]{2,1,0:T(1,128)}), f32[16,1,384]{2,1,0:T(1,128)S(1)}, u32[]{:S(2)}, u32[]{:S(2)}) async-start(f32[16,1,384]{2,1,0:T(1,128)} %reshape.316), calls=%async_computation.2 | async-start | bytes 49152 | tf_op jit(solution)/shard_map/all_to_all | solution.py:120
  144.5 25.6 %all-to-all-start.5 = ((f32[16,1,384]{2,1,0:T(1,128)}), f32[16,1,384]{2,1,0:T(1,128)S(1)}, u32[]{:S(2)}, u32[]{:S(2)}) async-start(f32[16,1,384]{2,1,0:T(1,128)} %reshape.322), calls=%async_computation.5 | async-start | bytes 49152 | tf_op jit(solution)/shard_map/all_to_all | solution.py:126
  170.1 78.5 %all-to-all-start = ((f32[16,2,3,64,128]{4,1,3,2,0:T(2,128)}), f32[16,2,3,64,128]{4,1,3,2,0:T(2,128)S(1)}, u32[]{:S(2)}, u32[]{:S(2)}) async-start(f32[16,2,3,64,128]{4,1,3,2,0:T(2,128)} %copy.152), calls=%async_computation | async-start | bytes 6291456 | tf_op jit(solution)/shard_map/all_to_all | solution.py:113
  248.6 13.4 %all-to-all-start.3 = ((f32[16,1,384]{2,1,0:T(1,128)}), f32[16,1,384]{2,1,0:T(1,128)S(1)}, u32[]{:S(2)}, u32[]{:S(2)}) async-start(f32[16,1,384]{2,1,0:T(1,128)} %reshape.318), calls=%async_computation.3 | async-start | bytes 49152 | tf_op jit(solution)/shard_map/all_to_all | solution.py:119
  255.6 10.6 %copy-start.1 = (bf16[3,8,2,1024]{3,2,1,0:T(2,128)(2,1)S(1)}, bf16[3,8,2,1024]{3,2,1,0:T(2,128)(2,1)}, u32[]{:S(2)}) copy-start(bf16[3,8,2,1024]{3,2,1,0:T(2,128)(2,1)} %param.7) | copy-start | bytes 294916
  255.6 11.2 %copy-start.5 = (bf16[3,8,512]{2,1,0:T(8,128)(2,1)S(1)}, bf16[3,8,512]{2,1,0:T(8,128)(2,1)}, u32[]{:S(2)}) copy-start(bf16[3,8,512]{2,1,0:T(8,128)(2,1)} %param.6) | copy-start | bytes 73732
  262.0 7.1 %copy-start.3 = (f32[16,1,384]{2,1,0:T(1,128)}, f32[16,1,384]{2,1,0:T(1,128)S(1)}, u32[]{:S(2)}) copy-start(f32[16,1,384]{2,1,0:T(1,128)S(1)} %all-to-all-done.3) | copy-start | bytes 73732
  262.0 46.0 %all-to-all-start.1 = ((f32[16,2,3,64,128]{4,1,0,2,3:T(2,128)}), f32[16,2,3,64,128]{4,1,0,2,3:T(2,128)S(1)}, u32[]{:S(2)}, u32[]{:S(2)}) async-start(f32[16,2,3,64,128]{4,1,0,2,3:T(2,128)} %copy.153), calls=%async_computation.1 | async-start | bytes 6291456 | tf_op jit(solution)/shard_map/all_to_all | solution.py:112
  275.3 34.1 %copy-start.2 = (f32[8,4,128,3]{2,3,1,0:T(4,128)S(1)}, f32[8,4,128,3]{2,3,1,0:T(4,128)}, u32[]{:S(2)}) copy-start(f32[8,4,128,3]{2,3,1,0:T(4,128)} %fusion.42) | copy-start | bytes 147460
Sparse Core Ops, SparseCore 0:
  29.4 51.5 all-gather.1
where the time goes:
time: 322 us; the launch traced here: 319 us
  waiting for transfers between devices  122 us (38%)
  local copies, waits for them, and re-layouts  60.4 us (19%)
  matrix products  45.5 us (14%)
  starting transfers between devices  33.1 us (10%)
  blocking collectives  22.7 us (7%)
  other arithmetic  20.8 us (6%)
  between operations  13.8 us (4%)
    all_to_all x1, waiting for transfers between devices, on_device(): lax.all_to_all(slot_outs, 'inst', split_axis=0, concat_axis=0, tiled=True)  69.2 us
    all_to_all x1, waiting for transfers between devices, on_device(): lax.all_to_all(lax.all_to_all(slot_outs, 'inst', split_axis=0, concat_axi...  27.8 us
    all_gather x1, blocking collectives, on_device(): full_queries = lax.all_gather(queries, 'tp', axis=2, tiled=True)  22.7 us
    unnamed x23, local copies, waits for them, and re-layouts  19.3 us
    all_gather x1, waiting for transfers between devices, on_device(): every_query = lax.all_gather(full_queries, 'inst', axis=1, tiled=True)  16.8 us
    dot_general x1, matrix products, on_device(): jnp.einsum('pl,spkgd->lskgd', slot_float, page_outs, precision=highest)  15.6 us
    dot_general x1, matrix products, on_device(): jnp.einsum('spkgi,pikd->spkgd', weights.astype(jnp.bfloat16), value_rows,...  13.1 us
    reduce_sum x1, other arithmetic, on_device(): page_sums = jnp.sum(weights, axis=4)  12.6 us
  transfers between devices with their start and end apart: 7, of which 5 were waited for; matrix products, arithmetic and copies ran while one was open for 28% of the time, Pallas kernels for 0%

commit v1 on v0

v1 whole, which is shorter than its diff:
```python
import functools
import math

import jax
import jax.numpy as jnp
from jax import lax
from jax.experimental import pallas as pl
from jax.experimental.pallas import tpu as pltpu
from jax.sharding import PartitionSpec as P

HEAD_DIM = 128
PAGE = 256
CAP = 2
REQ_INST = 8
CHUNK = 16
VERY_LOW = -1e30
FLOOR = -1e29

f32 = jnp.float32
bf16 = jnp.bfloat16


def attend(groups, slice_tokens, meta, q_ref, k_ref, v_ref, out_ref, slot, qf, of, mf, lf):
    sources, ranges = q_ref.shape[0], q_ref.shape[1]
    rows = sources * groups
    half = rows // 2
    pages = k_ref.shape[0]
    extra = (pages - ranges) // CHUNK
    chunk_tokens = CHUNK * slice_tokens
    scale = 1.0 / math.sqrt(HEAD_DIM)
    exp2_scale = scale * math.log2(math.e)
    my_tp = meta[2, 0]

    for e in range(extra):
        slot[0, e] = 0
        slot[1, e] = 0
        slot[2, e] = 0
        slot[3, e] = 0

    def fill(r, count):
        start = meta[0, r]
        tokens = meta[1, r]
        span = (tokens + PAGE - 1) // PAGE
        more = (span - 1) // CHUNK
        tail = jnp.clip(tokens % PAGE - my_tp * slice_tokens, 0, slice_tokens)
        high = start * slice_tokens + (tokens // PAGE) * slice_tokens + tail
        slot[4, r] = high

        def one(j, carry):
            first = start + (j + 1) * CHUNK
            slot[0, count + j] = jnp.minimum(first, pages - CHUNK)
            slot[1, count + j] = first * slice_tokens
            slot[2, count + j] = high
            slot[3, count + j] = r
            return carry

        lax.fori_loop(0, more, one, 0)
        return count + more

    lax.fori_loop(0, ranges, fill, 0)

    for x in range(sources):
        for g in range(groups):
            qf[pl.ds((x * groups + g) * ranges, ranges), :] = q_ref[
                x, :, g * HEAD_DIM : (g + 1) * HEAD_DIM
            ].astype(f32)

    row_id = lax.broadcasted_iota(jnp.int32, (rows, HEAD_DIM), 0)
    lane_id = lax.broadcasted_iota(jnp.int32, (rows, chunk_tokens), 1)
    top = row_id < half

    def chunk(r, page, low, high):
        q = qf[pl.ds(r, rows, stride=ranges), :]
        zero = jnp.zeros_like(q)
        wide = jnp.concatenate(
            [jnp.where(top, q, zero), jnp.where(top, zero, q)], axis=1
        ).astype(bf16)
        k = k_ref[pl.ds(page, CHUNK), 0].reshape(chunk_tokens, 2 * HEAD_DIM)
        v = v_ref[pl.ds(page, CHUNK), 0].reshape(chunk_tokens, 2 * HEAD_DIM)
        s = lax.dot_general(wide, k, (((1,), (1,)), ((), ())), preferred_element_type=f32)
        place = lane_id + page * slice_tokens
        s = jnp.where((place >= low) & (place < high), s, VERY_LOW)
        m = jnp.maximum(jnp.max(s, axis=1, keepdims=True), FLOOR)
        p = jnp.exp2((s - m) * exp2_scale)
        total = jnp.sum(p, axis=1, keepdims=True)
        o = jnp.dot(p.astype(bf16), v, preferred_element_type=f32)
        o = jnp.where(top, o[:, :HEAD_DIM], o[:, HEAD_DIM:])
        shape = (rows, HEAD_DIM)
        return o, jnp.broadcast_to(m, shape), jnp.broadcast_to(total, shape)

    for r in range(ranges):
        start = meta[0, r]
        o, m, total = chunk(
            r, jnp.minimum(start, pages - CHUNK), start * slice_tokens, slot[4, r]
        )
        of[pl.ds(r, rows, stride=ranges), :] = o
        mf[pl.ds(r, rows, stride=ranges), :] = m
        lf[pl.ds(r, rows, stride=ranges), :] = total

    more = [chunk(slot[3, e], slot[0, e], slot[1, e], slot[2, e]) for e in range(extra)]
    for e in range(extra):
        o, m, total = more[e]
        at = pl.ds(slot[3, e], rows, stride=ranges)
        m_old = mf[at, :]
        m_new = jnp.maximum(m_old, m)
        a_old = jnp.exp2((m_old - m_new) * exp2_scale)
        a = jnp.exp2((m - m_new) * exp2_scale)
        of[at, :] = of[at, :] * a_old + o * a
        lf[at, :] = lf[at, :] * a_old + total * a
        mf[at, :] = m_new

    lane = lax.broadcasted_iota(jnp.int32, (ranges, HEAD_DIM), 1)
    for x in range(sources):
        stats = jnp.zeros((ranges, HEAD_DIM), f32)
        for g in range(groups):
            at = pl.ds((x * groups + g) * ranges, ranges)
            total = lf[at, :]
            some = total > 0.0
            safe = jnp.where(some, total, 1.0)
            out_ref[x, :, g * HEAD_DIM : (g + 1) * HEAD_DIM] = (of[at, :] / safe).astype(bf16)
            lse = jnp.where(some, mf[at, :] * scale + jnp.log(safe), VERY_LOW)
            mine = (lane == g) | (lane == g + groups) | (lane == g + 2 * groups)
            stats = jnp.where(mine, lse, stats)
        out_ref[x, :, groups * HEAD_DIM :] = split3(stats, lane, groups)


def split3(stats, lane, groups):
    high = stats.astype(bf16).astype(f32)
    rest = stats - high
    mid = rest.astype(bf16).astype(f32)
    low = rest - mid
    return jnp.where(lane < groups, high, jnp.where(lane < 2 * groups, mid, low)).astype(bf16)


def join3(parts, groups):
    parts = parts.astype(f32)
    return (
        parts
        + pltpu.roll(parts, HEAD_DIM - groups, 1)
        + pltpu.roll(parts, HEAD_DIM - 2 * groups, 1)
    )


def merge_sources(groups, in_ref, pick_ref, out_ref):
    sources, ranges = in_ref.shape[0], in_ref.shape[1]
    lane = lax.broadcasted_iota(jnp.int32, (ranges, HEAD_DIM), 1)
    lses = [join3(in_ref[i, :, groups * HEAD_DIM :], groups) for i in range(sources)]
    top = functools.reduce(jnp.maximum, lses)
    shares = [jnp.exp(l - top) for l in lses]
    total = functools.reduce(jnp.add, shares)
    lse = top + jnp.log(total)
    inverse = 1.0 / total
    shares = [s * inverse for s in shares]
    pick = pick_ref[...]
    stats = jnp.zeros((ranges, HEAD_DIM), f32)
    for g in range(groups):
        cols = slice(g * HEAD_DIM, (g + 1) * HEAD_DIM)
        acc = jnp.zeros((ranges, HEAD_DIM), f32)
        for i in range(sources):
            acc = acc + shares[i][:, g : g + 1] * in_ref[i, :, cols].astype(f32)
        out_ref[:, cols] = jnp.dot(pick, acc.astype(bf16), preferred_element_type=f32).astype(bf16)
        mine = (lane == g) | (lane == g + groups) | (lane == g + 2 * groups)
        stats = jnp.where(mine, jnp.broadcast_to(lse[:, g : g + 1], stats.shape), stats)
    parts = split3(stats, lane, groups)
    out_ref[:, groups * HEAD_DIM :] = jnp.dot(pick, parts, preferred_element_type=f32).astype(bf16)


def finish(steps, heads, in_ref, owner_ref, q_ref, k_ref, v_ref, out_ref):
    groups = steps * heads
    requests = q_ref.shape[1]
    scale = 1.0 / math.sqrt(HEAD_DIM)
    stats = join3(in_ref[:, groups * HEAD_DIM :], groups)
    lses = jnp.transpose(stats, (1, 0))
    owned = owner_ref[...] == lax.broadcasted_iota(jnp.int32, owner_ref.shape, 0)
    keys = [k_ref[t].astype(f32) for t in range(steps)]
    values = [v_ref[t].astype(f32) for t in range(steps)]
    for s in range(steps):
        for h in range(heads):
            g = s * heads + h
            cols = slice(h * HEAD_DIM, (h + 1) * HEAD_DIM)
            q = q_ref[s, :, cols].astype(f32)
            scores = [
                jnp.sum(q * keys[t], axis=1, keepdims=True) * scale for t in range(s + 1)
            ]
            lent = jnp.where(owned, jnp.broadcast_to(lses[g : g + 1, :], owned.shape), VERY_LOW)
            top = functools.reduce(jnp.maximum, scores)
            top = jnp.maximum(top, jnp.max(lent, axis=1, keepdims=True))
            share = jnp.where(owned, jnp.exp(lent - top), 0.0)
            total = jnp.sum(share, axis=1, keepdims=True)
            acc = jnp.dot(
                share,
                in_ref[:, g * HEAD_DIM : (g + 1) * HEAD_DIM].astype(f32),
                preferred_element_type=f32,
                precision=lax.Precision.HIGHEST,
            )
            for t in range(s + 1):
                weight = jnp.exp(scores[t] - top)
                total = total + weight
                acc = acc + weight.astype(bf16).astype(f32) * values[t]
            out_ref[s, :, cols] = (acc / total).astype(bf16)


def slot_ranks(homes):
    count = homes.shape[1]
    earlier = jnp.arange(count)[None, :] < jnp.arange(count)[:, None]
    matches = homes[:, :, None] == homes[:, None, :]
    return jnp.sum(matches & earlier[None], axis=2)


def on_device(queries, new_kv, page_cache, range_owner, range_start, range_tokens):
    steps, requests, columns = queries.shape
    lenders = lax.axis_size("inst")
    tp_count = lax.axis_size("tp")
    my_inst = lax.axis_index("inst")
    my_tp = lax.axis_index("tp")
    pages, _, slice_tokens, kv_columns = page_cache.shape
    ranges = range_owner.shape[1]
    heads = columns // HEAD_DIM
    groups = steps * heads
    kv_heads = kv_columns // HEAD_DIM
    group_size = heads * tp_count // kv_heads
    slots = lenders * CAP
    wide = (groups + 1) * HEAD_DIM
    pairs = kv_heads // 2
    sources = tp_count // pairs

    homes = range_owner // REQ_INST
    ranks = slot_ranks(homes)
    hit = (homes == my_inst)[:, :, None] & (ranks[:, :, None] == jnp.arange(CAP))
    slot_owner = (
        jnp.sum(jnp.where(hit, (range_owner - my_inst * REQ_INST + 1)[:, :, None], 0), axis=1) - 1
    ).reshape(slots)
    my_slot = lax.dynamic_index_in_dim(homes * CAP + ranks, my_inst, 0, keepdims=False)
    slot_pick = (jnp.arange(slots)[:, None] == my_slot[None, :]).astype(bf16)
    owner_pick = (slot_owner[:, None] == jnp.arange(requests)[None, :]).astype(bf16)

    sent = jnp.einsum("lr,srx->lsx", owner_pick, queries, preferred_element_type=f32).astype(bf16)
    sent = sent.reshape(lenders, CAP, groups * HEAD_DIM)
    got = lax.all_to_all(sent, "inst", split_axis=0, concat_axis=0, tiled=True)
    mine = jnp.einsum(
        "lr,lx->rx", slot_pick, got.reshape(slots, -1), preferred_element_type=f32
    ).astype(bf16)
    every = lax.all_gather(mine, "tp", axis=0, tiled=False)

    meta = jnp.stack(
        [
            lax.dynamic_index_in_dim(range_start, my_inst, 0, keepdims=False),
            lax.dynamic_index_in_dim(range_tokens, my_inst, 0, keepdims=False),
            jnp.full((ranges,), my_tp, jnp.int32),
        ]
    )
    pair_columns = 2 * HEAD_DIM
    partial = pl.pallas_call(
        functools.partial(attend, groups, slice_tokens),
        grid=(pairs,),
        in_specs=[
            pl.BlockSpec(memory_space=pltpu.SMEM),
            pl.BlockSpec((sources, ranges, groups * HEAD_DIM), lambda i: (i, 0, 0)),
            pl.BlockSpec((pages, 1, slice_tokens, pair_columns), lambda i: (0, 0, 0, i)),
            pl.BlockSpec((pages, 1, slice_tokens, pair_columns), lambda i: (0, 1, 0, i)),
        ],
        out_specs=pl.BlockSpec((sources, ranges, wide), lambda i: (i, 0, 0)),
        out_shape=jax.ShapeDtypeStruct((tp_count, ranges, wide), bf16),
        scratch_shapes=[pltpu.SMEM((5, ranges), jnp.int32)]
        + [pltpu.VMEM((sources * groups * ranges, HEAD_DIM), f32)] * 4,
        compiler_params=pltpu.CompilerParams(vmem_limit_bytes=48 * 2**20),
        name="attend",
    )(meta, every, page_cache, page_cache)

    parts = lax.all_to_all(partial, "tp", split_axis=0, concat_axis=0, tiled=True)
    vmem = pl.BlockSpec(memory_space=pltpu.VMEM)
    lent = pl.pallas_call(
        functools.partial(merge_sources, groups),
        in_specs=[vmem] * 2,
        out_specs=vmem,
        out_shape=jax.ShapeDtypeStruct((slots, wide), bf16),
        compiler_params=pltpu.CompilerParams(vmem_limit_bytes=32 * 2**20),
        name="merge_sources",
    )(parts, slot_pick)
    back = lax.all_to_all(
        lent.reshape(lenders, CAP, wide), "inst", split_axis=0, concat_axis=0, tiled=True
    ).reshape(slots, wide)

    head = my_tp * heads // group_size
    fresh = lax.dynamic_slice_in_dim(new_kv, head * HEAD_DIM, HEAD_DIM, axis=3)
    owner_rows = jnp.broadcast_to(slot_owner[None, :], (requests, slots))
    return pl.pallas_call(
        functools.partial(finish, steps, heads),
        in_specs=[vmem] * 5,
        out_specs=vmem,
        out_shape=jax.ShapeDtypeStruct((steps, requests, columns), bf16),
        compiler_params=pltpu.CompilerParams(vmem_limit_bytes=32 * 2**20),
        name="finish",
    )(back, owner_rows, queries, fresh[:, :, 0], fresh[:, :, 1])


def solution(mesh):
    placed = (
        P(None, "inst", "tp"),
        P(None, "inst", None, None),
        P("inst", None, "tp", None),
        P(),
        P(),
        P(),
    )
    return jax.shard_map(
        on_device, mesh=mesh, in_specs=placed, out_specs=P(None, "inst", "tp"), check_vma=False
    )
```

time: 322 us -> 111 us (0.34)
  waiting for transfers between devices: 122 us -> 26.6 us
  local copies, waits for them, and re-layouts: 60.4 us -> 3.42 us
  matrix products: 45.5 us -> 1.15 us
  Pallas kernels: 0 us -> 33.6 us
  other arithmetic: 20.8 us -> 2.04 us
  between operations: 13.8 us -> 0.12 us
  starting transfers between devices: 33.1 us -> 24.1 us
    all_to_all x6 -> x3, waiting for transfers between devices: 106 us -> 26.6 us  [the longest x1 10.3 us: on_device(): lax.all_to_all(partial, 'tp', split_axis=0, concat_axis=0, tiled=True)]
    dot_general x11 -> x2, matrix products: 45.5 us -> 1.15 us  [the longest x1 0.95 us: on_device(): jnp.einsum('lr,srx->lsx', owner_pick, queries, preferred_element_type=f32)]
    pallas_call x0 -> x3, Pallas kernels: none -> 33.6 us  [the longest x1 31.7 us: on_device(): pl.pallas_call(functools.partial(attend, groups, slice_tokens), grid=(pai...]
    unnamed x23 -> x2, local copies, waits for them, and re-layouts: 19.3 us -> 0.01 us
    all_gather x1 -> x0, waiting for transfers between devices: 16.8 us -> none  [on_device(): every_query = lax.all_gather(full_queries, 'inst', axis=1, tiled=True)]
    another operation x3 -> x1, local copies, waits for them, and re-layouts: 13.7 us -> 0.08 us  [on_device(): jnp.stack([lax.dynamic_index_in_dim(range_start, my_inst, 0, keepdims=Fal...]
    reduce_sum x4 -> x1, other arithmetic: 13.5 us -> 0.12 us  [on_device(): jnp.sum(jnp.where(hit, (range_owner - my_inst * REQ_INST + 1)[:, :, None]...]
    all_to_all x6 -> x3, starting transfers between devices: 33.1 us -> 24.1 us  [the longest x1 9.98 us: on_device(): got = lax.all_to_all(sent, 'inst', split_axis=0, concat_axis=0, tiled=True)]
  transfers between devices with their start and end apart: 7 -> 3, of which waited for: 5 -> 3; matrix products, arithmetic and copies ran while one was open for 28% -> 2% of each run, Pallas kernels for 0% -> 0%
where the time goes in v1:
time: 111 us
  Pallas kernels  33.6 us (30%)
  waiting for transfers between devices  26.6 us (24%)
  starting transfers between devices  24.1 us (22%)
  blocking collectives  19.8 us (18%)
  local copies, waits for them, and re-layouts  3.42 us (3%)
  other arithmetic  2.04 us (2%)
  matrix products  1.15 us (1%)
    pallas_call x1, Pallas kernels, on_device(): pl.pallas_call(functools.partial(attend, groups, slice_tokens), grid=(pai...  31.7 us
    all_gather x1, blocking collectives, on_device(): every = lax.all_gather(mine, 'tp', axis=0, tiled=False)  19.8 us
    all_to_all x1, waiting for transfers between devices, on_device(): lax.all_to_all(partial, 'tp', split_axis=0, concat_axis=0, tiled=True)  10.3 us
    all_to_all x1, starting transfers between devices, on_device(): got = lax.all_to_all(sent, 'inst', split_axis=0, concat_axis=0, tiled=True)  9.98 us
    all_to_all x1, starting transfers between devices, on_device(): lax.all_to_all(lent.reshape(lenders, CAP, wide), 'inst', split_axis=0, co...  9.13 us
    all_to_all x1, waiting for transfers between devices, on_device(): lax.all_to_all(lent.reshape(lenders, CAP, wide), 'inst', split_axis=0, co...  8.68 us
    all_to_all x1, waiting for transfers between devices, on_device(): got = lax.all_to_all(sent, 'inst', split_axis=0, concat_axis=0, tiled=True)  7.61 us
    all_to_all x1, starting transfers between devices, on_device(): lax.all_to_all(partial, 'tp', split_axis=0, concat_axis=0, tiled=True)  4.99 us
  transfers between devices with their start and end apart: 3, of which 3 were waited for; matrix products, arithmetic and copies ran while one was open for 2% of the time, Pallas kernels for 0%

profile of v1, /device:TPU:1, one launch (start us, length us, event | category | flops | bytes accessed | tf_op | source)
XLA Modules:
  0.0 110.8 jit_solution(15490621531510148052)
XLA Ops:
  0.0 0.7 broadcast_compare_fusion
  0.7 0.7 subtract_add_fusion
  1.4 0.4 convert_reduce_fusion
  1.8 0.1 select_reduce_fusion
  2.0 0.1 copy.10
  2.1 0.1 sub.26
  2.2 1.0 convolution_convert_fusion.1
  3.1 0.1 copy.11
  3.2 0.7 reshape.41
  3.9 10.0 %all-to-all-start = ((bf16[16,2,1536]{2,1,0:T(2,128)(2,1)}), bf16[16,2,1536]{2,1,0:T(2,128)(2,1)S(1)}, u32[]{:S(2)}, u32[]{:S(2)}) async-start(bf16[16,2,1536]{2,1,0:T(2,128)(2,1)} %reshape.41), calls=%async_computation | async-start | bytes 196608 | tf_op jit(solution)/shard_map/all_to_all | solution.py:239
  13.9 0.1 pad.2.clone
  14.0 0.7 constant_dynamic-slice_fusion.4
  14.7 0.1 add_add_fusion.meta
  14.8 7.6 %all-to-all-done = bf16[16,2,1536]{2,1,0:T(2,128)(2,1)S(1)} async-done(((bf16[16,2,1536]{2,1,0:T(2,128)(2,1)}), bf16[16,2,1536]{2,1,0:T(2,128)(2,1)S(1)}, u32[]{:S(2)}, u32[]{:S(2)}) %all-to-all-start) | async-done | bytes 98336 | tf_op jit(solution)/shard_map/all_to_all | solution.py:239
  22.4 0.2 convolution_convert_fusion
  22.6 19.8 %all-gather = bf16[256,1536]{1,0:T(8,128)(2,1)S(1)} all-gather(bf16[16,1536]{1,0:T(8,128)(2,1)S(1)} %convolution_convert_fusion), channel_id=2, replica_groups=mesh['inst'=16,'tp'=16] {'tp'}, dimensions={0}, use_global_device_ids=true | all-gather | bytes 835584 | tf_op jit(solution)/shard_map/all_gather | solution.py:243
  42.4 0.0 copy-start
  42.4 31.7 %attend.1 = bf16[16,16,1664]{2,1,0:T(8,128)(2,1)} custom-call(s32[3,16]{1,0:T(4,128)S(1)} %add_add_fusion.meta, bf16[16,16,1536]{2,1,0:T(8,128)(2,1)S(1)} %bitcast.13, bf16[128,2,16,1024]{3,2,1,0:T(8,128)(2,1)} %v_ref.1, bf16[128,2,16,1024]{3,2,1,0:T(8,128)(2,1)} %v_ref.1), custom_call_target="tpu_custom_call" | custom-call | tf_op jit(solution)/shard_map/attend/pallas_call | solution.py:253
  74.1 5.0 %all-to-all-start.1 = ((bf16[16,16,1664]{2,1,0:T(8,128)(2,1)}), bf16[16,16,1664]{2,1,0:T(8,128)(2,1)S(1)}, u32[]{:S(2)}, u32[]{:S(2)}) async-start(bf16[16,16,1664]{2,1,0:T(8,128)(2,1)} %attend.1), calls=%async_computation.1 | async-start | bytes 1703936 | tf_op jit(solution)/shard_map/all_to_all | solution.py:270
  79.1 0.9 constant_dynamic-slice_fusion.2
  80.0 10.3 %all-to-all-done.1.in_ref = bf16[16,16,1664]{2,1,0:T(8,128)(2,1)S(1)} async-done(((bf16[16,16,1664]{2,1,0:T(8,128)(2,1)}), bf16[16,16,1664]{2,1,0:T(8,128)(2,1)S(1)}, u32[]{:S(2)}, u32[]{:S(2)}) %all-to-all-start.1) | async-done | bytes 852000 | tf_op jit(solution)/shard_map/all_to_all | solution.py:270
  90.3 0.8 merge_sources.1
  91.1 0.7 reshape.43
  91.7 9.1 %all-to-all-start.2 = ((bf16[16,2,1664]{2,1,0:T(2,128)(2,1)}), bf16[16,2,1664]{2,1,0:T(2,128)(2,1)S(1)}, u32[]{:S(2)}, u32[]{:S(2)}) async-start(bf16[16,2,1664]{2,1,0:T(2,128)(2,1)} %reshape.43), calls=%async_computation.2 | async-start | bytes 212992 | tf_op jit(solution)/shard_map/all_to_all | solution.py:280
  100.9 8.7 %all-to-all-done.2 = bf16[16,2,1664]{2,1,0:T(2,128)(2,1)S(1)} async-done(((bf16[16,2,1664]{2,1,0:T(2,128)(2,1)}), bf16[16,2,1664]{2,1,0:T(2,128)(2,1)S(1)}, u32[]{:S(2)}, u32[]{:S(2)}) %all-to-all-start.2) | async-done | bytes 106528 | tf_op jit(solution)/shard_map/all_to_all | solution.py:280
  109.6 0.0 copy-done
  109.6 1.1 %finish.1 = bf16[3,8,512]{2,1,0:T(8,128)(2,1)} custom-call(bf16[32,1664]{1,0:T(8,128)(2,1)S(1)} %reshape.44.in_ref, s32[8,32]{1,0:T(8,128)S(1)} %broadcast_in_dim.12.owner_ref, bf16[3,8,512]{2,1,0:T(8,128)(2,1)S(1)} %copy-done, bf16[3,8,128]{2,1,0:T(8,128)(2,1)S(1)} %get-tuple-element.13.k_ref, bf16[3,8,128]{2,1,0:T(8,128)(2,1)S(1)} %get-tuple-element.12.v_ref), custom_call_target="tpu_custom_call" | custom-call | tf_op jit(solution)/shard_map/finish/pallas_call | solution.py:287
  (7 shorter events, 0.1 us)
Async XLA Ops:
  3.9 18.5 %all-to-all-start = ((bf16[16,2,1536]{2,1,0:T(2,128)(2,1)}), bf16[16,2,1536]{2,1,0:T(2,128)(2,1)S(1)}, u32[]{:S(2)}, u32[]{:S(2)}) async-start(bf16[16,2,1536]{2,1,0:T(2,128)(2,1)} %reshape.41), calls=%async_computation | async-start | bytes 196608 | tf_op jit(solution)/shard_map/all_to_all | solution.py:239
  42.4 67.2 %copy-start = (bf16[3,8,512]{2,1,0:T(8,128)(2,1)S(1)}, bf16[3,8,512]{2,1,0:T(8,128)(2,1)}, u32[]{:S(2)}) copy-start(bf16[3,8,512]{2,1,0:T(8,128)(2,1)} %q_ref.1) | copy-start | bytes 73732
  74.1 16.2 %all-to-all-start.1 = ((bf16[16,16,1664]{2,1,0:T(8,128)(2,1)}), bf16[16,16,1664]{2,1,0:T(8,128)(2,1)S(1)}, u32[]{:S(2)}, u32[]{:S(2)}) async-start(bf16[16,16,1664]{2,1,0:T(8,128)(2,1)} %attend.1), calls=%async_computation.1 | async-start | bytes 1703936 | tf_op jit(solution)/shard_map/all_to_all | solution.py:270
  91.7 17.8 %all-to-all-start.2 = ((bf16[16,2,1664]{2,1,0:T(2,128)(2,1)}), bf16[16,2,1664]{2,1,0:T(2,128)(2,1)S(1)}, u32[]{:S(2)}, u32[]{:S(2)}) async-start(bf16[16,2,1664]{2,1,0:T(2,128)(2,1)} %reshape.43), calls=%async_computation.2 | async-start | bytes 212992 | tf_op jit(solution)/shard_map/all_to_all | solution.py:280

commit v2 on v1

v2 whole, which is shorter than its diff:
```python
import functools
import math

import jax
import jax.numpy as jnp
from jax import lax
from jax.experimental import pallas as pl
from jax.experimental.pallas import tpu as pltpu
from jax.sharding import PartitionSpec as P

HEAD_DIM = 128
PAGE = 256
CAP = 2
REQ_INST = 8
SIDE = 4
SHIFTS = (1, 3, 2)
CHUNK = 16
BATCH = 8
MORE = 4
VERY_LOW = -1e30
FLOOR = -1e29
PAD = 16
PAGE_ROW, LOW_ROW, HIGH_ROW, RANGE_ROW, END_ROW, PLACE_ROW, START_ROW, SLOT_ROW = range(8)

f32 = jnp.float32
bf16 = jnp.bfloat16


def iota(shape, dim):
    return lax.broadcasted_iota(jnp.int32, shape, dim)


def split3(stats, lane, groups):
    high = stats.astype(bf16).astype(f32)
    rest = stats - high
    mid = rest.astype(bf16).astype(f32)
    low = rest - mid
    return jnp.where(lane < groups, high, jnp.where(lane < 2 * groups, mid, low)).astype(bf16)


def join3(parts, groups):
    parts = parts.astype(f32)
    return (
        parts
        + pltpu.roll(parts, HEAD_DIM - groups, 1)
        + pltpu.roll(parts, HEAD_DIM - 2 * groups, 1)
    )


def prepare(q_ref, owner_ref, sent_ref, mine_ref, stage):
    steps, requests, columns = q_ref.shape
    heads = columns // HEAD_DIM
    groups = steps * heads
    lenders, ranges = owner_ref.shape
    owner = owner_ref[...]
    hit = owner // REQ_INST == lax.axis_index("inst")
    earlier = (iota((ranges, ranges), 0) < iota((ranges, ranges), 1)).astype(f32)
    rank = jnp.dot(hit.astype(f32), earlier, preferred_element_type=f32)
    local = (owner % REQ_INST + 1).astype(f32)
    owners = []
    for c in range(CAP):
        chosen = jnp.where(hit & (jnp.abs(rank - c) < 0.5), local, 0.0)
        mine = jnp.sum(chosen, axis=1, keepdims=True) - 1.0
        owners.append(jnp.broadcast_to(mine, (lenders, HEAD_DIM)))
        pick = (mine.astype(jnp.int32) == iota((lenders, requests), 1)).astype(f32)
        for s in range(steps):
            value = jnp.dot(pick, q_ref[s].astype(f32), preferred_element_type=f32)
            for h in range(heads):
                at = pl.ds(c * groups + s * heads + h, lenders, stride=CAP * groups)
                stage[at, :] = value[:, h * HEAD_DIM : (h + 1) * HEAD_DIM]
    sent_ref[...] = stage[...].astype(bf16)
    mine_ref[...] = jnp.transpose(jnp.concatenate(owners, axis=0), (1, 0))[: mine_ref.shape[0], :]


def make_plan(slice_tokens, pages, owner_ref, start_ref, tokens_ref, plan):
    ranges = owner_ref.shape[1]
    me = lax.axis_index("inst")
    my_tp = lax.axis_index("tp")
    for i in range(plan.shape[0]):
        for r in range(ranges):
            plan[i, r] = 0
    plan[PLACE_ROW, 1] = my_tp % SIDE
    plan[PLACE_ROW, 2] = my_tp // SIDE

    def fill(r, count):
        start = start_ref[me, r]
        tokens = tokens_ref[me, r]
        span = (tokens + PAGE - 1) // PAGE
        more = (span - 1) // CHUNK
        tail = jnp.clip(tokens % PAGE - my_tp * slice_tokens, 0, slice_tokens)
        high = (start + tokens // PAGE) * slice_tokens + tail
        plan[END_ROW, r] = high
        plan[START_ROW, r] = start

        def one(j, carry):
            first = start + (j + 1) * CHUNK
            plan[PAGE_ROW, count + j] = jnp.minimum(first, pages - CHUNK)
            plan[LOW_ROW, count + j] = first * slice_tokens
            plan[HIGH_ROW, count + j] = high
            plan[RANGE_ROW, count + j] = r
            return carry

        lax.fori_loop(0, more, one, 0)
        return count + more

    plan[PLACE_ROW, 0] = lax.fori_loop(0, ranges, fill, 0)
    homes = [owner_ref[me, r] // REQ_INST for r in range(ranges)]
    for r in range(ranges):
        rank = sum([(homes[e] == homes[r]).astype(jnp.int32) for e in range(r)], jnp.int32(0))
        plan[SLOT_ROW, r] = homes[r] * CAP + rank


def slot_matrix(plan, shape, range_dim):
    ranges = shape[range_dim]
    matrix = jnp.zeros(shape, f32)
    for r in range(ranges):
        here = (iota(shape, range_dim) == r) & (iota(shape, 1 - range_dim) == plan[SLOT_ROW, r])
        matrix = jnp.where(here, 1.0, matrix)
    return matrix


def pick_ranges(groups, plan, got_ref, out_ref, stage):
    ranges = out_ref.shape[0]
    slots = got_ref.shape[0] // groups
    stage[...] = got_ref[...].astype(f32)
    matrix = slot_matrix(plan, (ranges, slots), 0)
    for g in range(groups):
        value = stage[pl.ds(g, slots, stride=groups), :]
        out_ref[:, g * HEAD_DIM : (g + 1) * HEAD_DIM] = jnp.dot(
            matrix, value, preferred_element_type=f32
        ).astype(bf16)


def attend_row(groups, ranges, plan, chunks, k_ref, v_ref, out_ref, qf, of, mf, lf):
    rows = SIDE * groups
    half = rows // 2
    pages, _, slice_tokens, _ = k_ref.shape
    chunk_tokens = CHUNK * slice_tokens
    scale = 1.0 / math.sqrt(HEAD_DIM)
    exp2_scale = scale * math.log2(math.e)
    place = plan[PLACE_ROW, 1]
    sources = [(place + SIDE - k) % SIDE for k in (0,) + SHIFTS]

    for x, chunk in zip(sources, chunks):
        base = pl.multiple_of(x * (groups * ranges), groups * ranges)
        for g in range(groups):
            qf[pl.ds(base + g * ranges, ranges), :] = chunk[
                :, g * HEAD_DIM : (g + 1) * HEAD_DIM
            ].astype(f32)

    top = iota((rows, HEAD_DIM), 0) < half
    lane = iota((1, chunk_tokens), 1)

    def load(ref, page):
        return ref[pl.ds(page, CHUNK), 0].reshape(chunk_tokens, 2 * HEAD_DIM)

    def scores(r, page, low, high):
        q = qf[pl.ds(r, rows, stride=ranges), :]
        zero = jnp.zeros_like(q)
        wide = jnp.concatenate(
            [jnp.where(top, q, zero), jnp.where(top, zero, q)], axis=1
        ).astype(bf16)
        s = lax.dot_general(
            wide, load(k_ref, page), (((1,), (1,)), ((), ())), preferred_element_type=f32
        )
        at = lane + page * slice_tokens
        return s + jnp.where((at >= low) & (at < high), 0.0, VERY_LOW)

    def softmax(s):
        m = jnp.maximum(jnp.max(s, axis=1, keepdims=True), FLOOR)
        p = jnp.exp2((s - m) * exp2_scale)
        return p, m, jnp.sum(p, axis=1, keepdims=True)

    def values(p, page):
        o = jnp.dot(p.astype(bf16), load(v_ref, page), preferred_element_type=f32)
        return jnp.where(top, o[:, :HEAD_DIM], o[:, HEAD_DIM:])

    def many(work):
        s = [scores(*w) for w in work]
        s = [softmax(one) for one in s]
        o = [values(one[0], w[1]) for one, w in zip(s, work)]
        return [(one, m, total) for one, (_, m, total) in zip(o, s)]

    def first(b, carry):
        work = []
        for j in range(BATCH):
            r = b * BATCH + j
            start = plan[START_ROW, r]
            page = jnp.minimum(start, pages - CHUNK)
            work.append((r, page, start * slice_tokens, plan[END_ROW, r]))
        for w, (o, m, total) in zip(work, many(work)):
            at = pl.ds(w[0], rows, stride=ranges)
            of[at, :] = o
            mf[at, :] = jnp.broadcast_to(m, o.shape)
            lf[at, :] = jnp.broadcast_to(total, o.shape)
        return carry

    lax.fori_loop(0, ranges // BATCH, first, 0)

    def more(b, carry):
        work = []
        for j in range(MORE):
            e = b * MORE + j
            work.append((plan[RANGE_ROW, e], plan[PAGE_ROW, e], plan[LOW_ROW, e], plan[HIGH_ROW, e]))
        for w, (o, m, total) in zip(work, many(work)):
            at = pl.ds(w[0], rows, stride=ranges)
            m_old = mf[at, :]
            m_new = jnp.maximum(m_old, m)
            a_old = jnp.exp2((m_old - m_new) * exp2_scale)
            a = jnp.exp2((m - m_new) * exp2_scale)
            of[at, :] = of[at, :] * a_old + o * a
            lf[at, :] = lf[at, :] * a_old + total * a
            mf[at, :] = m_new
        return carry

    lax.fori_loop(0, (plan[PLACE_ROW, 0] + MORE - 1) // MORE, more, 0)

    lanes = iota((ranges, HEAD_DIM), 1)
    for x in range(SIDE):
        m = jnp.zeros((ranges, HEAD_DIM), f32)
        totals = jnp.zeros((ranges, HEAD_DIM), f32)
        for g in range(groups):
            at = pl.ds((x * groups + g) * ranges, ranges)
            total = lf[at, :]
            safe = jnp.where(total > 0.0, total, 1.0)
            out_ref[x, :, g * HEAD_DIM : (g + 1) * HEAD_DIM] = (of[at, :] / safe).astype(bf16)
            mine = (lanes == g) | (lanes == g + groups) | (lanes == g + 2 * groups)
            m = jnp.where(mine, mf[at, :], m)
            totals = jnp.where(mine, total, totals)
        some = totals > 0.0
        lse = jnp.where(some, m * scale + jnp.log(jnp.where(some, totals, 1.0)), VERY_LOW)
        out_ref[x, :, groups * HEAD_DIM :] = split3(lse, lanes, groups)


def attend_own(groups, plan, c0, c1, c2, c3, k_ref, v_ref, out_ref, *scratch):
    attend_row(groups, c0.shape[0], plan, [c0, c1, c2, c3], k_ref, v_ref, out_ref, *scratch)


def attend_others(groups, plan, b0, b1, b2, k_ref, v_ref, held, out_ref, q, *scratch):
    for i, block in enumerate((b0, b1, b2)):

        @pl.when(pl.program_id(0) == i)
        def _():
            q[...] = block[...]

    chunks = [q.at[j] for j in range(SIDE)]
    attend_row(groups, q.shape[1], plan, chunks, k_ref, v_ref, out_ref, *scratch)


def merge_sources(groups, plan, in_ref, out_ref, stage):
    sources, ranges = in_ref.shape[0], in_ref.shape[1]
    slots = out_ref.shape[0] // PAD
    lane = iota((ranges, HEAD_DIM), 1)
    lses = [join3(in_ref[i, :, groups * HEAD_DIM :], groups) for i in range(sources)]
    top = functools.reduce(jnp.maximum, lses)
    shares = [jnp.exp(l - top) for l in lses]
    total = functools.reduce(jnp.add, shares)
    lse = top + jnp.log(total)
    inverse = 1.0 / total
    shares = [s * inverse for s in shares]
    matrix = slot_matrix(plan, (slots, ranges), 1).astype(bf16)
    stats = jnp.zeros((ranges, HEAD_DIM), f32)
    for g in range(groups):
        cols = slice(g * HEAD_DIM, (g + 1) * HEAD_DIM)
        acc = jnp.zeros((ranges, HEAD_DIM), f32)
        for i in range(sources):
            acc = acc + shares[i][:, g : g + 1] * in_ref[i, :, cols].astype(f32)
        stage[pl.ds(g, slots, stride=PAD), :] = jnp.dot(
            matrix, acc.astype(bf16), preferred_element_type=f32
        )
        mine = (lane == g) | (lane == g + groups) | (lane == g + 2 * groups)
        stats = jnp.where(mine, jnp.broadcast_to(lse[:, g : g + 1], stats.shape), stats)
    parts = split3(stats, lane, groups)
    stage[pl.ds(groups, slots, stride=PAD), :] = jnp.dot(matrix, parts, preferred_element_type=f32)
    for g in range(groups + 1, PAD):
        stage[pl.ds(g, slots, stride=PAD), :] = jnp.zeros((slots, HEAD_DIM), f32)
    out_ref[...] = stage[...].astype(bf16)


def finish(steps, heads, in_ref, owner_ref, q_ref, k_ref, v_ref, out_ref, stage):
    groups = steps * heads
    lenders = in_ref.shape[0] // (CAP * PAD)
    scale = 1.0 / math.sqrt(HEAD_DIM)
    stage[...] = in_ref[...].astype(f32)

    def group(g):
        return jnp.concatenate(
            [stage[pl.ds(c * PAD + g, lenders, stride=CAP * PAD), :] for c in range(CAP)], axis=0
        )

    lses = jnp.transpose(join3(group(groups), groups), (1, 0))
    owned = owner_ref[...].astype(jnp.int32) == iota(owner_ref.shape, 0)
    keys = [k_ref[t].astype(f32) for t in range(steps)]
    values = [v_ref[t].astype(f32) for t in range(steps)]
    for s in range(steps):
        for h in range(heads):
            g = s * heads + h
            cols = slice(h * HEAD_DIM, (h + 1) * HEAD_DIM)
            q = q_ref[s, :, cols].astype(f32)
            scores = [
                jnp.sum(q * keys[t], axis=1, keepdims=True) * scale for t in range(s + 1)
            ]
            lent = jnp.where(owned, jnp.broadcast_to(lses[g : g + 1, :], owned.shape), VERY_LOW)
            top = functools.reduce(jnp.maximum, scores)
            top = jnp.maximum(top, jnp.max(lent, axis=1, keepdims=True))
            share = jnp.where(owned, jnp.exp(lent - top), 0.0)
            total = jnp.sum(share, axis=1, keepdims=True)
            acc = jnp.dot(
                share, group(g), preferred_element_type=f32, precision=lax.Precision.HIGHEST
            )
            for t in range(s + 1):
                weight = jnp.exp(scores[t] - top)
                total = total + weight
                acc = acc + weight.astype(bf16).astype(f32) * values[t]
            out_ref[s, :, cols] = (acc / total).astype(bf16)


def x_shift(k):
    return [(SIDE * y + x, SIDE * y + (x + k) % SIDE) for y in range(SIDE) for x in range(SIDE)]


def y_shift(k):
    return [(SIDE * y + x, SIDE * ((y + k) % SIDE) + x) for y in range(SIDE) for x in range(SIDE)]


def on_device(queries, new_kv, page_cache, range_owner, range_start, range_tokens):
    steps, requests, columns = queries.shape
    lenders = lax.axis_size("inst")
    tp_count = lax.axis_size("tp")
    my_tp = lax.axis_index("tp")
    pages, _, slice_tokens, kv_columns = page_cache.shape
    ranges = range_owner.shape[1]
    heads = columns // HEAD_DIM
    groups = steps * heads
    kv_heads = kv_columns // HEAD_DIM
    group_size = heads * tp_count // kv_heads
    slots = lenders * CAP
    wide = (groups + 1) * HEAD_DIM
    vmem = pl.BlockSpec(memory_space=pltpu.VMEM)
    smem = pl.BlockSpec(memory_space=pltpu.SMEM)
    small = pltpu.CompilerParams(vmem_limit_bytes=16 * 2**20)
    large = pltpu.CompilerParams(vmem_limit_bytes=32 * 2**20)

    sent, slot_owner = pl.pallas_call(
        prepare,
        in_specs=[vmem] * 2,
        out_specs=[vmem] * 2,
        out_shape=[
            jax.ShapeDtypeStruct((slots * groups, HEAD_DIM), bf16),
            jax.ShapeDtypeStruct((requests, slots), f32),
        ],
        scratch_shapes=[pltpu.VMEM((slots * groups, HEAD_DIM), f32)],
        compiler_params=small,
        name="prepare",
    )(queries, range_owner)
    got = lax.all_to_all(sent, "inst", split_axis=0, concat_axis=0, tiled=True)

    plan = pl.pallas_call(
        functools.partial(make_plan, slice_tokens, pages),
        in_specs=[smem] * 3,
        out_specs=smem,
        out_shape=jax.ShapeDtypeStruct((8, ranges), jnp.int32),
        name="make_plan",
    )(range_owner, range_start, range_tokens)
    head = my_tp * heads // group_size
    fresh = lax.dynamic_slice_in_dim(new_kv, head * HEAD_DIM, HEAD_DIM, axis=3)

    own = pl.pallas_call(
        functools.partial(pick_ranges, groups),
        in_specs=[smem, vmem],
        out_specs=vmem,
        out_shape=jax.ShapeDtypeStruct((ranges, groups * HEAD_DIM), bf16),
        scratch_shapes=[pltpu.VMEM((slots * groups, HEAD_DIM), f32)],
        compiler_params=small,
        name="pick_ranges",
    )(plan, got)
    chunks = [own] + [lax.ppermute(own, "tp", x_shift(k)) for k in SHIFTS]
    block = jnp.stack(chunks)
    blocks = [lax.ppermute(block, "tp", y_shift(k)) for k in SHIFTS]

    pair = 2 * HEAD_DIM
    scratch = [pltpu.VMEM((SIDE * groups * ranges, HEAD_DIM), f32)] * 4
    cost = dict(transcendentals=0)
    chunk_spec = pl.BlockSpec((ranges, groups * HEAD_DIM), lambda i, p: (0, 0))
    partial = pl.pallas_call(
        functools.partial(attend_own, groups),
        grid_spec=pltpu.PrefetchScalarGridSpec(
            num_scalar_prefetch=1,
            grid=(1,),
            in_specs=[chunk_spec] * SIDE
            + [
                pl.BlockSpec(
                    (pages, 1, slice_tokens, pair), lambda i, p, w=w: (0, w, 0, p[PLACE_ROW, 2])
                )
                for w in range(2)
            ],
            out_specs=pl.BlockSpec((SIDE, ranges, wide), lambda i, p: (p[PLACE_ROW, 2], 0, 0)),
            scratch_shapes=scratch,
        ),
        out_shape=jax.ShapeDtypeStruct((tp_count, ranges, wide), bf16),
        compiler_params=large,
        cost_estimate=pl.CostEstimate(flops=10**9, bytes_accessed=2**23, **cost),
        name="attend_own",
    )(plan, *chunks, page_cache, page_cache)

    def row_of(i, p):
        shift = jnp.where(i == 0, SHIFTS[0], jnp.where(i == 1, SHIFTS[1], SHIFTS[2]))
        return (p[PLACE_ROW, 2] + SIDE - shift) % SIDE

    block_spec = pl.BlockSpec((SIDE, ranges, groups * HEAD_DIM), lambda i, p: (0, 0, 0))
    partial = pl.pallas_call(
        functools.partial(attend_others, groups),
        grid_spec=pltpu.PrefetchScalarGridSpec(
            num_scalar_prefetch=1,
            grid=(len(SHIFTS),),
            in_specs=[block_spec] * len(SHIFTS)
            + [
                pl.BlockSpec(
                    (pages, 1, slice_tokens, pair), lambda i, p, w=w: (0, w, 0, row_of(i, p))
                )
                for w in range(2)
            ]
            + [pl.BlockSpec(memory_space=pl.ANY)],
            out_specs=pl.BlockSpec((SIDE, ranges, wide), lambda i, p: (row_of(i, p), 0, 0)),
            scratch_shapes=[pltpu.VMEM((SIDE, ranges, groups * HEAD_DIM), bf16)] + scratch,
        ),
        out_shape=jax.ShapeDtypeStruct((tp_count, ranges, wide), bf16),
        input_output_aliases={6: 0},
        compiler_params=large,
        cost_estimate=pl.CostEstimate(flops=3 * 10**9, bytes_accessed=3 * 2**23, **cost),
        name="attend_others",
    )(plan, *blocks, page_cache, page_cache, partial)

    parts = lax.all_to_all(partial, "tp", split_axis=0, concat_axis=0, tiled=True)
    lent = pl.pallas_call(
        functools.partial(merge_sources, groups),
        in_specs=[smem, vmem],
        out_specs=vmem,
        out_shape=jax.ShapeDtypeStruct((slots * PAD, HEAD_DIM), bf16),
        scratch_shapes=[pltpu.VMEM((slots * PAD, HEAD_DIM), f32)],
        compiler_params=small,
        name="merge_sources",
    )(plan, parts)
    back = lax.all_to_all(lent, "inst", split_axis=0, concat_axis=0, tiled=True)
    return pl.pallas_call(
        functools.partial(finish, steps, heads),
        in_specs=[vmem] * 5,
        out_specs=vmem,
        out_shape=jax.ShapeDtypeStruct((steps, requests, columns), bf16),
        scratch_shapes=[pltpu.VMEM((slots * PAD, HEAD_DIM), f32)],
        compiler_params=small,
        name="finish",
    )(back, slot_owner, queries, fresh[:, :, 0], fresh[:, :, 1])


def solution(mesh):
    placed = (
        P(None, "inst", "tp"),
        P(None, "inst", None, None),
        P("inst", None, "tp", None),
        P(),
        P(),
        P(),
    )
    return jax.shard_map(
        on_device, mesh=mesh, in_specs=placed, out_specs=P(None, "inst", "tp"), check_vma=False
    )
```

time: 111 us -> 87 us (0.78)
  blocking collectives: 19.8 us -> 0 us
  Pallas kernels: 33.6 us -> 19.9 us
  starting transfers between devices: 24.1 us -> 31.8 us
  local copies, waits for them, and re-layouts: 3.42 us -> 6.39 us
  other arithmetic: 2.04 us -> 0.03 us
  waiting for transfers between devices: 26.6 us -> 28.2 us
  matrix products: 1.15 us -> 0 us
    all_gather x1 -> x0, blocking collectives: 19.8 us -> none  [on_device(): every = lax.all_gather(mine, 'tp', axis=0, tiled=False)]
    pallas_call x2 -> x6, Pallas kernels: 32.5 us -> 18.7 us  [the longest x1 8.75 us: on_device(): pl.pallas_call(functools.partial(attend_others, groups), grid_spec=pltpu....]
    ppermute x0 -> x6, starting transfers between devices: none -> 8.75 us  [the longest x3 4.46 us: on_device(): blocks = [lax.ppermute(block, 'tp', y_shift(k)) for k in SHIFTS]]
    unnamed x2 -> x14, local copies, waits for them, and re-layouts: 0.01 us -> 5.51 us
    ppermute x0 -> x6, waiting for transfers between devices: none -> 2.92 us  [the longest x3 2.91 us: on_device(): chunks = [own] + [lax.ppermute(own, 'tp', x_shift(k)) for k in SHIFTS]]
    all_to_all x1, waiting for transfers between devices: 7.61 us -> 6.01 us  [on_device(): got = lax.all_to_all(sent, 'inst', split_axis=0, concat_axis=0, tiled=True)]
    reshape x4 -> x0, local copies, waits for them, and re-layouts: 1.48 us -> none  [the longest x1 0.72 us: on_device(): sent = sent.reshape(lenders, CAP, groups * HEAD_DIM)]
    dot_general x2 -> x0, matrix products: 1.15 us -> none  [the longest x1 0.95 us: on_device(): jnp.einsum('lr,srx->lsx', owner_pick, queries, preferred_element_type=f32)]
  transfers between devices with their start and end apart: 3 -> 9, of which waited for: 3 -> 5; matrix products, arithmetic and copies ran while one was open for 2% -> 1% of each run, Pallas kernels for 0% -> 7%
where the time goes in v2:
time: 87 us; the launch traced here: 86.4 us
  starting transfers between devices  31.8 us (37%)
  waiting for transfers between devices  28.2 us (32%)
  Pallas kernels  19.9 us (23%)
  local copies, waits for them, and re-layouts  6.39 us (7%)
    all_to_all x1, waiting for transfers between devices, on_device(): lax.all_to_all(partial, 'tp', split_axis=0, concat_axis=0, tiled=True)  11 us
    all_to_all x1, starting transfers between devices, on_device(): got = lax.all_to_all(sent, 'inst', split_axis=0, concat_axis=0, tiled=True)  9.98 us
    all_to_all x1, starting transfers between devices, on_device(): back = lax.all_to_all(lent, 'inst', split_axis=0, concat_axis=0, tiled=True)  9.02 us
    pallas_call x1, Pallas kernels, on_device(): pl.pallas_call(functools.partial(attend_others, groups), grid_spec=pltpu....  8.75 us
    all_to_all x1, waiting for transfers between devices, on_device(): back = lax.all_to_all(lent, 'inst', split_axis=0, concat_axis=0, tiled=True)  8.33 us
    all_to_all x1, waiting for transfers between devices, on_device(): got = lax.all_to_all(sent, 'inst', split_axis=0, concat_axis=0, tiled=True)  6.01 us
    unnamed x14, local copies, waits for them, and re-layouts  5.51 us
    ppermute x3, starting transfers between devices, on_device(): blocks = [lax.ppermute(block, 'tp', y_shift(k)) for k in SHIFTS]  4.46 us
  transfers between devices with their start and end apart: 9, of which 5 were waited for; matrix products, arithmetic and copies ran while one was open for 1% of the time, Pallas kernels for 7%

profile of v2, /device:TPU:1, one launch (start us, length us, event | category | flops | bytes accessed | tf_op | source)
XLA Modules:
  0.0 86.4 jit_solution(9815643034425853854)
XLA Ops:
  0.0 0.0 copy-start.4
  0.0 0.7 copy-done.4
  0.7 0.0 copy-start.6
  0.7 0.7 copy-done.6
  1.4 1.0 %prepare.1 = (bf16[384,128]{1,0:T(8,128)(2,1)}, f32[8,32]{1,0:T(8,128)S(1)}) custom-call(bf16[3,8,512]{2,1,0:T(8,128)(2,1)S(1)} %copy-done.4, s32[16,16]{1,0:T(8,128)S(1)} %copy-done.6), custom_call_target="tpu_custom_call" | custom-call | tf_op jit(solution)/shard_map/prepare/pallas_call | solution.py:344
  2.4 10.0 %all-to-all-start = ((bf16[16,24,128]{2,1,0:T(8,128)(2,1)}), bf16[16,24,128]{2,1,0:T(8,128)(2,1)S(1)}, u32[]{:S(2)}, u32[]{:S(2)}) async-start(bf16[16,24,128]{2,1,0:T(8,128)(2,1)} %bitcast), calls=%async_computation | async-start | bytes 196608 | tf_op jit(solution)/shard_map/all_to_all | solution.py:356
  12.4 2.5 %make_plan.1.plan = s32[8,16]{1,0:T(8,128)} custom-call(s32[16,16]{1,0:T(8,128)} %owner_ref.3, s32[16,16]{1,0:T(8,128)} %start_ref.1, s32[16,16]{1,0:T(8,128)} %tokens_ref.1), custom_call_target="tpu_custom_call" | custom-call | tf_op jit(solution)/shard_map/make_plan/pallas_call | solution.py:358
  14.9 6.0 %all-to-all-done = bf16[16,24,128]{2,1,0:T(8,128)(2,1)S(1)} async-done(((bf16[16,24,128]{2,1,0:T(8,128)(2,1)}), bf16[16,24,128]{2,1,0:T(8,128)(2,1)S(1)}, u32[]{:S(2)}, u32[]{:S(2)}) %all-to-all-start) | async-done | bytes 98336 | tf_op jit(solution)/shard_map/all_to_all | solution.py:356
  20.9 0.0 copy-start.2
  20.9 0.7 copy-done.2
  21.6 0.8 pick_ranges.1.c0
  22.4 1.3 %collective-permute-start = (bf16[16,1536]{1,0:T(8,128)(2,1)S(1)}, bf16[16,1536]{1,0:T(8,128)(2,1)S(1)}, u32[]{:S(2)}, u32[]{:S(2)}) collective-permute-start(bf16[16,1536]{1,0:T(8,128)(2,1)S(1)} %pick_ranges.1.c0), channel_id=1, source_target_pairs={{0,1},{1,2},{2,3},{3,0},{4,5},{5,6},{6,7},{7,4},{8,9},{9,10},{10,1... | collective-permute-start | bytes 147464 | tf_op jit(solution)/shard_map/ppermute | solution.py:377
  23.7 1.5 %collective-permute-start.1 = (bf16[16,1536]{1,0:T(8,128)(2,1)S(1)}, bf16[16,1536]{1,0:T(8,128)(2,1)S(1)}, u32[]{:S(2)}, u32[]{:S(2)}) collective-permute-start(bf16[16,1536]{1,0:T(8,128)(2,1)S(1)} %pick_ranges.1.c0), channel_id=1, source_target_pairs={{0,3},{1,0},{2,1},{3,2},{4,7},{5,4},{6,5},{7,6},{8,11},{9,8},{10,9... | collective-permute-start | bytes 147464 | tf_op jit(solution)/shard_map/ppermute | solution.py:377
  25.1 1.5 %collective-permute-start.2 = (bf16[16,1536]{1,0:T(8,128)(2,1)S(1)}, bf16[16,1536]{1,0:T(8,128)(2,1)S(1)}, u32[]{:S(2)}, u32[]{:S(2)}) collective-permute-start(bf16[16,1536]{1,0:T(8,128)(2,1)S(1)} %pick_ranges.1.c0), channel_id=1, source_target_pairs={{0,2},{1,3},{2,0},{3,1},{4,6},{5,7},{6,4},{7,5},{8,10},{9,11},{10,... | collective-permute-start | bytes 147464 | tf_op jit(solution)/shard_map/ppermute | solution.py:377
  26.7 0.5 collective-permute-done.c1
  27.1 0.0 collective-permute-done.1.c2
  27.1 2.4 %collective-permute-done.2.c3 = bf16[16,1536]{1,0:T(8,128)(2,1)S(1)} collective-permute-done((bf16[16,1536]{1,0:T(8,128)(2,1)S(1)}, bf16[16,1536]{1,0:T(8,128)(2,1)S(1)}, u32[]{:S(2)}, u32[]{:S(2)}) %collective-permute-start.2) | collective-permute-done | bytes 49184 | tf_op jit(solution)/shard_map/ppermute | solution.py:377
  29.6 1.4 %collective-permute-start.3 = (bf16[4,16,1536]{2,1,0:T(8,128)(2,1)S(1)}, bf16[4,16,1536]{2,1,0:T(8,128)(2,1)S(1)}, u32[]{:S(2)}, u32[]{:S(2)}) collective-permute-start(bf16[4,16,1536]{2,1,0:T(8,128)(2,1)S(1)} %pad_maximum_fusion), channel_id=1, source_target_pairs={{0,4},{1,5},{2,6},{3,7},{4,8},{5,9},{6,10},{7,11},{8,12},{9,13},{1... | collective-permute-start | bytes 589832 | tf_op jit(solution)/shard_map/ppermute | solution.py:379
  31.0 1.5 %collective-permute-start.4 = (bf16[4,16,1536]{2,1,0:T(8,128)(2,1)S(1)}, bf16[4,16,1536]{2,1,0:T(8,128)(2,1)S(1)}, u32[]{:S(2)}, u32[]{:S(2)}) collective-permute-start(bf16[4,16,1536]{2,1,0:T(8,128)(2,1)S(1)} %pad_maximum_fusion), channel_id=1, source_target_pairs={{0,12},{1,13},{2,14},{3,15},{4,0},{5,1},{6,2},{7,3},{8,4},{9,5},{1... | collective-permute-start | bytes 589832 | tf_op jit(solution)/shard_map/ppermute | solution.py:379
  32.5 1.6 %collective-permute-start.5 = (bf16[4,16,1536]{2,1,0:T(8,128)(2,1)S(1)}, bf16[4,16,1536]{2,1,0:T(8,128)(2,1)S(1)}, u32[]{:S(2)}, u32[]{:S(2)}) collective-permute-start(bf16[4,16,1536]{2,1,0:T(8,128)(2,1)S(1)} %pad_maximum_fusion), channel_id=1, source_target_pairs={{0,8},{1,9},{2,10},{3,11},{4,12},{5,13},{6,14},{7,15},{8,0},{9,1},... | collective-permute-start | bytes 589832 | tf_op jit(solution)/shard_map/ppermute | solution.py:379
  34.1 0.0 copy-start
  34.1 3.4 %copy-done = bf16[128,2,16,1024]{3,2,1,0:T(8,128)(2,1)S(1)} copy-done((bf16[128,2,16,1024]{3,2,1,0:T(8,128)(2,1)S(1)}, bf16[128,2,16,1024]{3,2,1,0:T(8,128)(2,1)}, u32[]{:S(2)}) %copy-start) | copy-done | bytes 8388632
  37.4 0.0 copy-start.1
  37.4 3.7 %attend_own.1.held = bf16[16,16,1664]{2,1,0:T(8,128)(2,1)} custom-call(s32[8,16]{1,0:T(8,128)S(1)} %copy-done.2, bf16[16,1536]{1,0:T(8,128)(2,1)S(1)} %pick_ranges.1.c0, bf16[16,1536]{1,0:T(8,128)(2,1)S(1)} %collective-permute-done.c1, bf16[16,1536]{1,0:T(8,128)(2,1)S(1)} %collective-permute-done.1.c2, bf16[16,1536]{1,0:T(8,128)(2,1)S(1)} %collective-permute-done.2.c3, ...), custom_call_target="tpu_custom_call" | custom-call | flops 1000000000 | bytes 8388608 | tf_op jit(solution)/shard_map/attend_own/pallas_call | solution.py:385
  41.1 0.0 copy-start.3
  41.1 0.0 copy-start.5
  41.1 0.0 collective-permute-done.3.b0
  41.1 0.0 collective-permute-done.4.b1
  41.1 0.0 collective-permute-done.5.b2
  41.1 0.0 copy-done.1
  41.1 8.8 %attend_others.1 = bf16[16,16,1664]{2,1,0:T(8,128)(2,1)} custom-call(s32[8,16]{1,0:T(8,128)S(1)} %copy-done.2, bf16[4,16,1536]{2,1,0:T(8,128)(2,1)S(1)} %collective-permute-done.3.b0, bf16[4,16,1536]{2,1,0:T(8,128)(2,1)S(1)} %collective-permute-done.4.b1, bf16[4,16,1536]{2,1,0:T(8,128)(2,1)S(1)} %collective-permute-done.5.b2, ...), custom_call_target="tpu_custom_call", output_to_operand_aliasing={{}: (6, {})} | custom-call | flops 3000000000 | bytes 25165824 | tf_op jit(solution)/shard_map/attend_others/pallas_call | solution.py:411
  49.9 4.0 %all-to-all-start.1 = ((bf16[16,16,1664]{2,1,0:T(8,128)(2,1)}), bf16[16,16,1664]{2,1,0:T(8,128)(2,1)S(1)}, u32[]{:S(2)}, u32[]{:S(2)}) async-start(bf16[16,16,1664]{2,1,0:T(8,128)(2,1)} %attend_others.1), calls=%async_computation.1 | async-start | bytes 1703936 | tf_op jit(solution)/shard_map/all_to_all | solution.py:434
  54.0 11.0 %all-to-all-done.1.in_ref = bf16[16,16,1664]{2,1,0:T(8,128)(2,1)S(1)} async-done(((bf16[16,16,1664]{2,1,0:T(8,128)(2,1)}), bf16[16,16,1664]{2,1,0:T(8,128)(2,1)S(1)}, u32[]{:S(2)}, u32[]{:S(2)}) %all-to-all-start.1) | async-done | bytes 852000 | tf_op jit(solution)/shard_map/all_to_all | solution.py:434
  64.9 0.0 copy-done.3
  64.9 2.1 %merge_sources.1 = bf16[512,128]{1,0:T(8,128)(2,1)} custom-call(s32[8,16]{1,0:T(8,128)S(1)} %copy-done.3, bf16[16,16,1664]{2,1,0:T(8,128)(2,1)S(1)} %all-to-all-done.1.in_ref), custom_call_target="tpu_custom_call" | custom-call | tf_op jit(solution)/shard_map/merge_sources/pallas_call | solution.py:435
  67.0 9.0 %all-to-all-start.2 = ((bf16[16,32,128]{2,1,0:T(8,128)(2,1)}), bf16[16,32,128]{2,1,0:T(8,128)(2,1)S(1)}, u32[]{:S(2)}, u32[]{:S(2)}) async-start(bf16[16,32,128]{2,1,0:T(8,128)(2,1)} %bitcast.6), calls=%async_computation.2 | async-start | bytes 262144 | tf_op jit(solution)/shard_map/all_to_all | solution.py:444
  76.0 0.9 %constant_dynamic-slice_fusion.1 = (bf16[3,8,1,128]{3,2,1,0:T(2,128)(2,1)S(1)}, bf16[3,8,1,128]{3,2,1,0:T(2,128)(2,1)S(1)}) fusion(bf16[3,8,2,1024]{3,2,1,0:T(2,128)(2,1)} %param.7, s32[]{:T(128)S(6)} %add.5, s32[]{:T(128)S(6)} %select_n.9), kind=kLoop, calls=%fused_computation.4 | loop fusion | bytes 24584 | tf_op jit(solution)/shard_map/slice | solution.py:453
  76.9 8.3 %all-to-all-done.2 = bf16[16,32,128]{2,1,0:T(8,128)(2,1)S(1)} async-done(((bf16[16,32,128]{2,1,0:T(8,128)(2,1)}), bf16[16,32,128]{2,1,0:T(8,128)(2,1)S(1)}, u32[]{:S(2)}, u32[]{:S(2)}) %all-to-all-start.2) | async-done | bytes 131104 | tf_op jit(solution)/shard_map/all_to_all | solution.py:444
  85.2 0.0 copy-done.5
  85.2 1.2 %finish.1 = bf16[3,8,512]{2,1,0:T(8,128)(2,1)} custom-call(bf16[512,128]{1,0:T(8,128)(2,1)S(1)} %bitcast.12, f32[8,32]{1,0:T(8,128)S(1)} %get-tuple-element.8.owner_ref, bf16[3,8,512]{2,1,0:T(8,128)(2,1)S(1)} %copy-done.5, bf16[3,8,128]{2,1,0:T(8,128)(2,1)S(1)} %get-tuple-element.12.k_ref, bf16[3,8,128]{2,1,0:T(8,128)(2,1)S(1)} %get-tuple-element.11.v_ref), custom_call_target="tpu_custom_call" | custom-call | tf_op jit(solution)/shard_map/finish/pallas_call | solution.py:445
  (2 shorter events, 0.0 us)
Async XLA Ops:
  0.0 0.7 copy-start.4
  0.7 0.7 copy-start.6
  2.4 18.5 %all-to-all-start = ((bf16[16,24,128]{2,1,0:T(8,128)(2,1)}), bf16[16,24,128]{2,1,0:T(8,128)(2,1)S(1)}, u32[]{:S(2)}, u32[]{:S(2)}) async-start(bf16[16,24,128]{2,1,0:T(8,128)(2,1)} %bitcast), calls=%async_computation | async-start | bytes 196608 | tf_op jit(solution)/shard_map/all_to_all | solution.py:356
  20.9 0.7 copy-start.2
  22.4 4.7 %collective-permute-start = (bf16[16,1536]{1,0:T(8,128)(2,1)S(1)}, bf16[16,1536]{1,0:T(8,128)(2,1)S(1)}, u32[]{:S(2)}, u32[]{:S(2)}) collective-permute-start(bf16[16,1536]{1,0:T(8,128)(2,1)S(1)} %pick_ranges.1.c0), channel_id=1, source_target_pairs={{0,1},{1,2},{2,3},{3,0},{4,5},{5,6},{6,7},{7,4},{8,9},{9,10},{10,1... | collective-permute-start | bytes 147464 | tf_op jit(solution)/shard_map/ppermute | solution.py:377
  23.7 3.5 %collective-permute-start.1 = (bf16[16,1536]{1,0:T(8,128)(2,1)S(1)}, bf16[16,1536]{1,0:T(8,128)(2,1)S(1)}, u32[]{:S(2)}, u32[]{:S(2)}) collective-permute-start(bf16[16,1536]{1,0:T(8,128)(2,1)S(1)} %pick_ranges.1.c0), channel_id=1, source_target_pairs={{0,3},{1,0},{2,1},{3,2},{4,7},{5,4},{6,5},{7,6},{8,11},{9,8},{10,9... | collective-permute-start | bytes 147464 | tf_op jit(solution)/shard_map/ppermute | solution.py:377
  25.1 4.4 %collective-permute-start.2 = (bf16[16,1536]{1,0:T(8,128)(2,1)S(1)}, bf16[16,1536]{1,0:T(8,128)(2,1)S(1)}, u32[]{:S(2)}, u32[]{:S(2)}) collective-permute-start(bf16[16,1536]{1,0:T(8,128)(2,1)S(1)} %pick_ranges.1.c0), channel_id=1, source_target_pairs={{0,2},{1,3},{2,0},{3,1},{4,6},{5,7},{6,4},{7,5},{8,10},{9,11},{10,... | collective-permute-start | bytes 147464 | tf_op jit(solution)/shard_map/ppermute | solution.py:377
  29.6 11.5 %collective-permute-start.3 = (bf16[4,16,1536]{2,1,0:T(8,128)(2,1)S(1)}, bf16[4,16,1536]{2,1,0:T(8,128)(2,1)S(1)}, u32[]{:S(2)}, u32[]{:S(2)}) collective-permute-start(bf16[4,16,1536]{2,1,0:T(8,128)(2,1)S(1)} %pad_maximum_fusion), channel_id=1, source_target_pairs={{0,4},{1,5},{2,6},{3,7},{4,8},{5,9},{6,10},{7,11},{8,12},{9,13},{1... | collective-permute-start | bytes 589832 | tf_op jit(solution)/shard_map/ppermute | solution.py:379
  31.0 10.1 %collective-permute-start.4 = (bf16[4,16,1536]{2,1,0:T(8,128)(2,1)S(1)}, bf16[4,16,1536]{2,1,0:T(8,128)(2,1)S(1)}, u32[]{:S(2)}, u32[]{:S(2)}) collective-permute-start(bf16[4,16,1536]{2,1,0:T(8,128)(2,1)S(1)} %pad_maximum_fusion), channel_id=1, source_target_pairs={{0,12},{1,13},{2,14},{3,15},{4,0},{5,1},{6,2},{7,3},{8,4},{9,5},{1... | collective-permute-start | bytes 589832 | tf_op jit(solution)/shard_map/ppermute | solution.py:379
  32.5 8.6 %collective-permute-start.5 = (bf16[4,16,1536]{2,1,0:T(8,128)(2,1)S(1)}, bf16[4,16,1536]{2,1,0:T(8,128)(2,1)S(1)}, u32[]{:S(2)}, u32[]{:S(2)}) collective-permute-start(bf16[4,16,1536]{2,1,0:T(8,128)(2,1)S(1)} %pad_maximum_fusion), channel_id=1, source_target_pairs={{0,8},{1,9},{2,10},{3,11},{4,12},{5,13},{6,14},{7,15},{8,0},{9,1},... | collective-permute-start | bytes 589832 | tf_op jit(solution)/shard_map/ppermute | solution.py:379
  34.1 3.4 %copy-start = (bf16[128,2,16,1024]{3,2,1,0:T(8,128)(2,1)S(1)}, bf16[128,2,16,1024]{3,2,1,0:T(8,128)(2,1)}, u32[]{:S(2)}) copy-start(bf16[128,2,16,1024]{3,2,1,0:T(8,128)(2,1)} %v_ref.3) | copy-start | bytes 25165828
  37.4 3.7 %copy-start.1 = (bf16[128,2,16,1024]{3,2,1,0:T(8,128)(2,1)S(1)}, bf16[128,2,16,1024]{3,2,1,0:T(8,128)(2,1)}, u32[]{:S(2)}) copy-start(bf16[128,2,16,1024]{3,2,1,0:T(8,128)(2,1)} %v_ref.3) | copy-start | bytes 25165828
  41.1 23.8 %copy-start.3 = (s32[8,16]{1,0:T(8,128)S(1)}, s32[8,16]{1,0:T(8,128)}, u32[]{:S(2)}) copy-start(s32[8,16]{1,0:T(8,128)} %make_plan.1.plan) | copy-start | bytes 1540
  41.1 44.1 %copy-start.5 = (bf16[3,8,512]{2,1,0:T(8,128)(2,1)S(1)}, bf16[3,8,512]{2,1,0:T(8,128)(2,1)}, u32[]{:S(2)}) copy-start(bf16[3,8,512]{2,1,0:T(8,128)(2,1)} %q_ref.3) | copy-start | bytes 73732
  49.9 15.0 %all-to-all-start.1 = ((bf16[16,16,1664]{2,1,0:T(8,128)(2,1)}), bf16[16,16,1664]{2,1,0:T(8,128)(2,1)S(1)}, u32[]{:S(2)}, u32[]{:S(2)}) async-start(bf16[16,16,1664]{2,1,0:T(8,128)(2,1)} %attend_others.1), calls=%async_computation.1 | async-start | bytes 1703936 | tf_op jit(solution)/shard_map/all_to_all | solution.py:434
  67.0 18.2 %all-to-all-start.2 = ((bf16[16,32,128]{2,1,0:T(8,128)(2,1)}), bf16[16,32,128]{2,1,0:T(8,128)(2,1)S(1)}, u32[]{:S(2)}, u32[]{:S(2)}) async-start(bf16[16,32,128]{2,1,0:T(8,128)(2,1)} %bitcast.6), calls=%async_computation.2 | async-start | bytes 262144 | tf_op jit(solution)/shard_map/all_to_all | solution.py:444

commit v3 on v2

v3 whole, which is shorter than its diff:
```python
import functools
import math

import jax
import jax.numpy as jnp
from jax import lax
from jax.experimental import pallas as pl
from jax.experimental.pallas import tpu as pltpu
from jax.sharding import PartitionSpec as P

HEAD_DIM = 128
PAGE = 256
CAP = 2
REQ_INST = 8
SIDE = 4
SHIFTS = (1, 3, 2)
FIRST = 8
CHUNK = 16
MORE = 8
VERY_LOW = -1e30
FLOOR = -1e29
PAD = 16
PAGE_ROW, LOW_ROW, HIGH_ROW, RANGE_ROW, END_ROW, COUNT_ROW, START_ROW = range(7)

f32 = jnp.float32
bf16 = jnp.bfloat16


def iota(shape, dim):
    return lax.broadcasted_iota(jnp.int32, shape, dim)


def split3(stats, lane, groups):
    high = stats.astype(bf16).astype(f32)
    rest = stats - high
    mid = rest.astype(bf16).astype(f32)
    low = rest - mid
    return jnp.where(lane < groups, high, jnp.where(lane < 2 * groups, mid, low)).astype(bf16)


def join3(parts, groups):
    parts = parts.astype(f32)
    return (
        parts
        + pltpu.roll(parts, HEAD_DIM - groups, 1)
        + pltpu.roll(parts, HEAD_DIM - 2 * groups, 1)
    )


def prepare(q_hbm, owner_hbm, sent_ref, mine_ref, q_ref, owner_ref, stage, sems):
    copies = [
        pltpu.make_async_copy(owner_hbm, owner_ref, sems.at[0]),
        pltpu.make_async_copy(q_hbm, q_ref, sems.at[1]),
    ]
    for copy in copies:
        copy.start()
    steps, requests, columns = q_ref.shape
    heads = columns // HEAD_DIM
    groups = steps * heads
    lenders, ranges = owner_ref.shape
    earlier = (iota((ranges, ranges), 0) < iota((ranges, ranges), 1)).astype(f32)
    copies[0].wait()
    owner = owner_ref[...]
    hit = owner // REQ_INST == lax.axis_index("inst")
    rank = jnp.dot(hit.astype(f32), earlier, preferred_element_type=f32)
    local = (owner % REQ_INST + 1).astype(f32)
    owners = []
    for c in range(CAP):
        chosen = jnp.where(hit & (jnp.abs(rank - c) < 0.5), local, 0.0)
        owners.append(jnp.sum(chosen, axis=1, keepdims=True) - 1.0)
    copies[1].wait()
    for c in range(CAP):
        pick = (owners[c].astype(jnp.int32) == iota((lenders, requests), 1)).astype(f32)
        for s in range(steps):
            value = jnp.dot(pick, q_ref[s].astype(f32), preferred_element_type=f32)
            for h in range(heads):
                at = pl.ds(c * groups + s * heads + h, lenders, stride=CAP * groups)
                stage[at, :] = value[:, h * HEAD_DIM : (h + 1) * HEAD_DIM]
    sent_ref[...] = stage[...].astype(bf16)
    spread = [jnp.broadcast_to(mine, (lenders, HEAD_DIM)) for mine in owners]
    mine_ref[...] = jnp.transpose(jnp.concatenate(spread, axis=0), (1, 0))[: mine_ref.shape[0], :]


def make_plan(slice_tokens, pages, owner_ref, start_ref, tokens_ref, plan, pick_ref, put_ref):
    ranges = owner_ref.shape[1]
    me = lax.axis_index("inst")
    my_tp = lax.axis_index("tp")
    for i in range(RANGE_ROW + 1):
        for r in range(ranges):
            plan[i, r] = 0

    def fill(r, count):
        start = start_ref[me, r]
        tokens = tokens_ref[me, r]
        span = (tokens + PAGE - 1) // PAGE
        more = jnp.maximum(span - FIRST + CHUNK - 1, 0) // CHUNK
        tail = jnp.clip(tokens % PAGE - my_tp * slice_tokens, 0, slice_tokens)
        high = (start + tokens // PAGE) * slice_tokens + tail
        plan[END_ROW, r] = high
        plan[START_ROW, r] = start

        def one(j, carry):
            first = start + FIRST + j * CHUNK
            plan[PAGE_ROW, count + j] = jnp.minimum(first, pages - CHUNK)
            plan[LOW_ROW, count + j] = first * slice_tokens
            plan[HIGH_ROW, count + j] = high
            plan[RANGE_ROW, count + j] = r
            return carry

        lax.fori_loop(0, more, one, 0)
        return count + more

    plan[COUNT_ROW, 0] = lax.fori_loop(0, ranges, fill, 0)
    homes = [owner_ref[me, r] // REQ_INST for r in range(ranges)]
    pick = jnp.zeros(pick_ref.shape, f32)
    put = jnp.zeros(put_ref.shape, f32)
    for r in range(ranges):
        rank = sum([(homes[e] == homes[r]).astype(jnp.int32) for e in range(r)], jnp.int32(0))
        slot = homes[r] * CAP + rank
        pick = jnp.where((iota(pick.shape, 0) == r) & (iota(pick.shape, 1) == slot), 1.0, pick)
        put = jnp.where((iota(put.shape, 1) == r) & (iota(put.shape, 0) == slot), 1.0, put)
    pick_ref[...] = pick
    put_ref[...] = put


def pick_ranges(groups, pick_ref, got_ref, out_ref, stage):
    slots = got_ref.shape[0] // groups
    stage[...] = got_ref[...].astype(f32)
    pick = pick_ref[...]
    for g in range(groups):
        value = stage[pl.ds(g, slots, stride=groups), :]
        out_ref[:, g * HEAD_DIM : (g + 1) * HEAD_DIM] = jnp.dot(
            pick, value, preferred_element_type=f32
        ).astype(bf16)


def place_before(shift):
    return (lax.axis_index("tp") // SIDE + SIDE - shift) % SIDE


def spread_queries(groups, chunks, qf, base):
    ranges = chunks[0].shape[0]
    for k, chunk in zip((0,) + SHIFTS, chunks):
        x = (lax.axis_index("tp") + SIDE - k) % SIDE
        at = pl.multiple_of(x * (groups * ranges) + base, groups * ranges)
        for g in range(groups):
            cols = slice(g * HEAD_DIM, (g + 1) * HEAD_DIM)
            qf[pl.ds(at + g * ranges, ranges), :] = chunk[:, cols].astype(f32)


def attend_row(groups, ranges, plan, k_ref, v_ref, wait_k, wait_v, out_ref, qf, base, of, lf):
    rows = SIDE * groups
    half = rows // 2
    pages, slice_tokens, pair = k_ref.shape
    scale = 1.0 / math.sqrt(HEAD_DIM)
    exp2_scale = scale * math.log2(math.e)
    top = iota((rows, HEAD_DIM), 0) < half

    def load(ref, page, span):
        return ref[pl.ds(page, span)].reshape(span * slice_tokens, pair)

    def scores(span, r, page, low, high):
        q = qf[pl.ds(base + r, rows, stride=ranges), :]
        zero = jnp.zeros_like(q)
        wide = jnp.concatenate(
            [jnp.where(top, q, zero), jnp.where(top, zero, q)], axis=1
        ).astype(bf16)
        k = load(k_ref, page, span)
        s = lax.dot_general(wide, k, (((1,), (1,)), ((), ())), preferred_element_type=f32)
        at = iota((1, span * slice_tokens), 1) + page * slice_tokens
        return s + jnp.where((at >= low) & (at < high), 0.0, VERY_LOW)

    def softmax(s):
        m = jnp.maximum(jnp.max(s, axis=1, keepdims=True), FLOOR)
        p = jnp.exp2((s - m) * exp2_scale)
        total = jnp.sum(p, axis=1, keepdims=True)
        some = total > 0.0
        safe = jnp.where(some, total, 1.0)
        lse = jnp.where(some, m * scale + jnp.log(safe), VERY_LOW)
        return p.astype(bf16), 1.0 / safe, jnp.broadcast_to(lse, (rows, HEAD_DIM))

    def values(span, page, p, inverse):
        o = jnp.dot(p, load(v_ref, page, span), preferred_element_type=f32)
        return jnp.where(top, o[:, :HEAD_DIM], o[:, HEAD_DIM:]) * inverse

    def many(span, work, wait=None):
        s = [scores(span, *w) for w in work]
        s = [softmax(one) for one in s]
        if wait is not None:
            wait()
        o = [values(span, w[1], one[0], one[1]) for one, w in zip(s, work)]
        return [(one, lse) for one, (_, _, lse) in zip(o, s)]

    def place(r):
        return pl.ds(pl.multiple_of(r * rows, 8), rows)

    work = []
    for r in range(ranges):
        start = plan[START_ROW, r]
        page = jnp.minimum(start, pages - FIRST)
        work.append((r, page, start * slice_tokens, plan[END_ROW, r]))
    wait_k()
    for w, (o, lse) in zip(work, many(FIRST, work, wait_v)):
        of[place(w[0]), :] = o
        lf[place(w[0]), :] = lse

    def more(b, carry):
        work = []
        for j in range(MORE):
            e = b * MORE + j
            work.append((plan[RANGE_ROW, e], plan[PAGE_ROW, e], plan[LOW_ROW, e], plan[HIGH_ROW, e]))
        for w, (o, lse) in zip(work, many(CHUNK, work)):
            at = place(w[0])
            old = lf[at, :]
            high = jnp.maximum(old, lse)
            share_old = jnp.exp(old - high)
            share = jnp.exp(lse - high)
            total = share_old + share
            of[at, :] = (of[at, :] * share_old + o * share) / total
            lf[at, :] = high + jnp.log(total)
        return carry

    lax.fori_loop(0, (plan[COUNT_ROW, 0] + MORE - 1) // MORE, more, 0)

    lanes = iota((ranges, HEAD_DIM), 1)
    for x in range(SIDE):
        lse = jnp.zeros((ranges, HEAD_DIM), f32)
        for g in range(groups):
            at = pl.ds(x * groups + g, ranges, stride=rows)
            out_ref[x, :, g * HEAD_DIM : (g + 1) * HEAD_DIM] = of[at, :].astype(bf16)
            mine = (lanes == g) | (lanes == g + groups) | (lanes == g + 2 * groups)
            lse = jnp.where(mine, lf[at, :], lse)
        out_ref[x, :, groups * HEAD_DIM :] = split3(lse, lanes, groups)


def cache_copies(cache, target, shift, sems, first):
    pair = target.shape[-1]
    y = place_before(shift)
    columns = pl.ds(pl.multiple_of(y * pair, pair), pair)
    return [
        pltpu.make_async_copy(cache.at[:, w, :, columns], target.at[w], sems.at[first + w])
        for w in range(2)
    ]


def row_copy(row, held, shift, sem):
    y = place_before(shift)
    return pltpu.make_async_copy(row, held.at[pl.ds(y * SIDE, SIDE)], sem)


def attend_own(groups, plan_hbm, block, cache, held, plan, chunks, kv, row, qf, of, lf, sems):
    rows = cache_copies(cache, kv, 0, sems, 0)
    small = [pltpu.make_async_copy(plan_hbm, plan, sems.at[2])]
    small.append(pltpu.make_async_copy(block, chunks, sems.at[3]))
    for copy in small + rows:
        copy.start()
    for copy in small:
        copy.wait()
    spread_queries(groups, [chunks.at[i] for i in range(SIDE)], qf, 0)
    attend_row(
        groups, block.shape[1], plan, kv.at[0], kv.at[1], rows[0].wait, rows[1].wait, row, qf, 0, of, lf
    )
    out = row_copy(row, held, 0, sems.at[4])
    out.start()
    out.wait()


def attend_others(groups, shifts, plan_hbm, *refs):
    count = len(shifts)
    given = refs[:count]
    cache, held_in, held, plan, blocks, kv, row, qf, of, lf, sems = refs[count:]
    ranges = given[0].shape[1]
    size = SIDE * groups * ranges
    small = [pltpu.make_async_copy(plan_hbm, plan, sems.at[0])]
    for i, block in enumerate(given):
        small.append(pltpu.make_async_copy(block, blocks.at[i], sems.at[1 + i]))
    rows = [
        cache_copies(cache, kv.at[i], k, sems, 1 + count + 2 * i) for i, k in enumerate(shifts)
    ]
    for copy in small + sum(rows, []):
        copy.start()
    for copy in small:
        copy.wait()
    for i in range(count):
        spread_queries(groups, [blocks.at[i, j] for j in range(SIDE)], qf, i * size)
    out = 1 + 3 * count

    def one(i, carry):
        def wait(w):
            for k in range(count):

                @pl.when(i == k)
                def _():
                    rows[k][w].wait()

        wait_k, wait_v = functools.partial(wait, 0), functools.partial(wait, 1)
        keys, values = kv.at[i, 0], kv.at[i, 1]
        base = pl.multiple_of(i * size, size)
        attend_row(groups, ranges, plan, keys, values, wait_k, wait_v, row.at[i], qf, base, of, lf)
        shift = jnp.where(i == 0, shifts[0], shifts[-1])
        row_copy(row.at[i], held, shift, sems.at[out + i]).start()
        return carry

    lax.fori_loop(0, count, one, 0)
    for i, shift in enumerate(shifts):
        row_copy(row.at[i], held, shift, sems.at[out + i]).wait()


def merge_sources(groups, put_ref, in_ref, out_ref, stage):
    sources, ranges = in_ref.shape[0], in_ref.shape[1]
    slots = out_ref.shape[0] // PAD
    lane = iota((ranges, HEAD_DIM), 1)
    lses = [join3(in_ref[i, :, groups * HEAD_DIM :], groups) for i in range(sources)]
    top = functools.reduce(jnp.maximum, lses)
    shares = [jnp.exp(l - top) for l in lses]
    total = functools.reduce(jnp.add, shares)
    lse = top + jnp.log(total)
    inverse = 1.0 / total
    shares = [s * inverse for s in shares]
    put = put_ref[...].astype(bf16)
    stats = jnp.zeros((ranges, HEAD_DIM), f32)
    for g in range(groups):
        cols = slice(g * HEAD_DIM, (g + 1) * HEAD_DIM)
        acc = jnp.zeros((ranges, HEAD_DIM), f32)
        for i in range(sources):
            acc = acc + shares[i][:, g : g + 1] * in_ref[i, :, cols].astype(f32)
        stage[pl.ds(g, slots, stride=PAD), :] = jnp.dot(
            put, acc.astype(bf16), preferred_element_type=f32
        )
        mine = (lane == g) | (lane == g + groups) | (lane == g + 2 * groups)
        stats = jnp.where(mine, jnp.broadcast_to(lse[:, g : g + 1], stats.shape), stats)
    parts = split3(stats, lane, groups)
    stage[pl.ds(groups, slots, stride=PAD), :] = jnp.dot(put, parts, preferred_element_type=f32)
    for g in range(groups + 1, PAD):
        stage[pl.ds(g, slots, stride=PAD), :] = jnp.zeros((slots, HEAD_DIM), f32)
    out_ref[...] = stage[...].astype(bf16)


def finish(steps, heads, in_ref, owner_ref, q_ref, k_ref, v_ref, out_ref, stage):
    groups = steps * heads
    lenders = in_ref.shape[0] // (CAP * PAD)
    scale = 1.0 / math.sqrt(HEAD_DIM)
    stage[...] = in_ref[...].astype(f32)

    def group(g):
        return jnp.concatenate(
            [stage[pl.ds(c * PAD + g, lenders, stride=CAP * PAD), :] for c in range(CAP)], axis=0
        )

    lses = jnp.transpose(join3(group(groups), groups), (1, 0))
    owned = owner_ref[...].astype(jnp.int32) == iota(owner_ref.shape, 0)
    keys = [k_ref[t].astype(f32) for t in range(steps)]
    values = [v_ref[t].astype(f32) for t in range(steps)]
    for s in range(steps):
        for h in range(heads):
            g = s * heads + h
            cols = slice(h * HEAD_DIM, (h + 1) * HEAD_DIM)
            q = q_ref[s, :, cols].astype(f32)
            scores = [
                jnp.sum(q * keys[t], axis=1, keepdims=True) * scale for t in range(s + 1)
            ]
            lent = jnp.where(owned, jnp.broadcast_to(lses[g : g + 1, :], owned.shape), VERY_LOW)
            top = functools.reduce(jnp.maximum, scores)
            top = jnp.maximum(top, jnp.max(lent, axis=1, keepdims=True))
            share = jnp.where(owned, jnp.exp(lent - top), 0.0)
            total = jnp.sum(share, axis=1, keepdims=True)
            acc = jnp.dot(
                share, group(g), preferred_element_type=f32, precision=lax.Precision.HIGHEST
            )
            for t in range(s + 1):
                weight = jnp.exp(scores[t] - top)
                total = total + weight
                acc = acc + weight.astype(bf16).astype(f32) * values[t]
            out_ref[s, :, cols] = (acc / total).astype(bf16)


def x_shift(k):
    return [(SIDE * y + x, SIDE * y + (x + k) % SIDE) for y in range(SIDE) for x in range(SIDE)]


def y_shift(k):
    return [(SIDE * y + x, SIDE * ((y + k) % SIDE) + x) for y in range(SIDE) for x in range(SIDE)]


def on_device(queries, new_kv, page_cache, range_owner, range_start, range_tokens):
    steps, requests, columns = queries.shape
    lenders = lax.axis_size("inst")
    tp_count = lax.axis_size("tp")
    my_tp = lax.axis_index("tp")
    pages, _, slice_tokens, kv_columns = page_cache.shape
    ranges = range_owner.shape[1]
    heads = columns // HEAD_DIM
    groups = steps * heads
    kv_heads = kv_columns // HEAD_DIM
    group_size = heads * tp_count // kv_heads
    slots = lenders * CAP
    wide = (groups + 1) * HEAD_DIM
    vmem = pl.BlockSpec(memory_space=pltpu.VMEM)
    smem = pl.BlockSpec(memory_space=pltpu.SMEM)
    hbm = pl.BlockSpec(memory_space=pltpu.HBM)
    params = pltpu.CompilerParams(vmem_limit_bytes=24 * 2**20)
    whole = pltpu.CompilerParams(vmem_limit_bytes=64 * 2**20 - 2**17)
    dma = pltpu.SemaphoreType.DMA

    sent, slot_owner = pl.pallas_call(
        prepare,
        in_specs=[hbm] * 2,
        out_specs=[vmem] * 2,
        out_shape=[
            jax.ShapeDtypeStruct((slots * groups, HEAD_DIM), bf16),
            jax.ShapeDtypeStruct((requests, slots), f32),
        ],
        scratch_shapes=[
            pltpu.VMEM(queries.shape, bf16),
            pltpu.VMEM(range_owner.shape, jnp.int32),
            pltpu.VMEM((slots * groups, HEAD_DIM), f32),
            dma((2,)),
        ],
        compiler_params=whole,
        name="prepare",
    )(queries, range_owner)
    got = lax.all_to_all(sent, "inst", split_axis=0, concat_axis=0, tiled=True)

    plan, pick, put = pl.pallas_call(
        functools.partial(make_plan, slice_tokens, pages),
        in_specs=[smem] * 3,
        out_specs=[smem, vmem, vmem],
        out_shape=[
            jax.ShapeDtypeStruct((8, ranges), jnp.int32),
            jax.ShapeDtypeStruct((ranges, slots), f32),
            jax.ShapeDtypeStruct((slots, ranges), f32),
        ],
        name="make_plan",
    )(range_owner, range_start, range_tokens)
    head = my_tp * heads // group_size
    fresh = lax.dynamic_slice_in_dim(new_kv, head * HEAD_DIM, HEAD_DIM, axis=3)

    own = pl.pallas_call(
        functools.partial(pick_ranges, groups),
        in_specs=[vmem] * 2,
        out_specs=vmem,
        out_shape=jax.ShapeDtypeStruct((ranges, groups * HEAD_DIM), bf16),
        scratch_shapes=[pltpu.VMEM((slots * groups, HEAD_DIM), f32)],
        compiler_params=params,
        name="pick_ranges",
    )(pick, got)
    block = jnp.stack([own] + [lax.ppermute(own, "tp", x_shift(k)) for k in SHIFTS])
    near = {k: lax.ppermute(block, "tp", y_shift(k)) for k in (1, SIDE - 1)}

    pair = 2 * HEAD_DIM
    size = SIDE * groups * ranges
    partial_type = jax.ShapeDtypeStruct((tp_count, ranges, wide), bf16)
    plan_type = pltpu.SMEM(plan.shape, jnp.int32)
    row_scratch = [pltpu.VMEM((size, HEAD_DIM), f32)] * 2
    partial = pl.pallas_call(
        functools.partial(attend_own, groups),
        in_specs=[hbm] * 3,
        out_specs=hbm,
        out_shape=partial_type,
        scratch_shapes=[
            plan_type,
            pltpu.VMEM((SIDE, ranges, groups * HEAD_DIM), bf16),
            pltpu.VMEM((2, pages, slice_tokens, pair), bf16),
            pltpu.VMEM((SIDE, ranges, wide), bf16),
            pltpu.VMEM((size, HEAD_DIM), f32),
        ]
        + row_scratch
        + [dma((5,))],
        compiler_params=whole,
        cost_estimate=pl.CostEstimate(flops=10**9, bytes_accessed=2**23, transcendentals=0),
        name="attend_own",
    )(plan, block, page_cache)
    passed, partial = lax.optimization_barrier((near[1], partial))
    far = lax.ppermute(passed, "tp", y_shift(1))
    for given in ({1: passed, SIDE - 1: near[SIDE - 1]}, {2: far}):
        count = len(given)
        partial = pl.pallas_call(
            functools.partial(attend_others, groups, list(given)),
            in_specs=[hbm] * (count + 3),
            out_specs=hbm,
            out_shape=partial_type,
            scratch_shapes=[
                plan_type,
                pltpu.VMEM((count, SIDE, ranges, groups * HEAD_DIM), bf16),
                pltpu.VMEM((count, 2, pages, slice_tokens, pair), bf16),
                pltpu.VMEM((count, SIDE, ranges, wide), bf16),
                pltpu.VMEM((count * size, HEAD_DIM), f32),
            ]
            + row_scratch
            + [dma((1 + 4 * count,))],
            input_output_aliases={count + 2: 0},
            compiler_params=whole,
            cost_estimate=pl.CostEstimate(
                flops=count * 10**9, bytes_accessed=count * 2**22, transcendentals=0
            ),
            name="attend_others",
        )(plan, *given.values(), page_cache, partial)

    parts = lax.all_to_all(partial, "tp", split_axis=0, concat_axis=0, tiled=True)
    lent = pl.pallas_call(
        functools.partial(merge_sources, groups),
        in_specs=[vmem] * 2,
        out_specs=vmem,
        out_shape=jax.ShapeDtypeStruct((slots * PAD, HEAD_DIM), bf16),
        scratch_shapes=[pltpu.VMEM((slots * PAD, HEAD_DIM), f32)],
        compiler_params=params,
        name="merge_sources",
    )(put, parts)
    back = lax.all_to_all(lent, "inst", split_axis=0, concat_axis=0, tiled=True)
    return pl.pallas_call(
        functools.partial(finish, steps, heads),
        in_specs=[vmem] * 5,
        out_specs=vmem,
        out_shape=jax.ShapeDtypeStruct((steps, requests, columns), bf16),
        scratch_shapes=[pltpu.VMEM((slots * PAD, HEAD_DIM), f32)],
        compiler_params=params,
        name="finish",
    )(back, slot_owner, queries, fresh[:, :, 0], fresh[:, :, 1])


def solution(mesh):
    placed = (
        P(None, "inst", "tp"),
        P(None, "inst", None, None),
        P("inst", None, "tp", None),
        P(),
        P(),
        P(),
    )
    return jax.shard_map(
        on_device, mesh=mesh, in_specs=placed, out_specs=P(None, "inst", "tp"), check_vma=False
    )
```

time: 87 us -> 83.4 us (0.959)
  local copies, waits for them, and re-layouts: 6.39 us -> 1.59 us
  starting transfers between devices: 31.8 us -> 29.4 us
  waiting for transfers between devices: 28.2 us -> 29.7 us
  Pallas kernels: 19.9 us -> 21.2 us
    unnamed x14 -> x8, local copies, waits for them, and re-layouts: 5.51 us -> 0.71 us
    all_to_all x1, starting transfers between devices: 9.02 us -> 7.02 us  [on_device(): back = lax.all_to_all(lent, 'inst', split_axis=0, concat_axis=0, tiled=True)]
    ppermute x6, starting transfers between devices: 8.75 us -> 7.13 us  [the longest x3 4.29 us: on_device(): lax.ppermute(own, 'tp', x_shift(k))]
    all_to_all x1, waiting for transfers between devices: 11 us -> 12.4 us  [on_device(): lax.all_to_all(partial, 'tp', split_axis=0, concat_axis=0, tiled=True)]
    pallas_call x5 -> x6, Pallas kernels: 16.3 us -> 17.6 us  [the longest x2 10.2 us: on_device(): pl.pallas_call(functools.partial(attend_others, groups, list(given)), in_...]
    all_to_all x1, starting transfers between devices: 4.04 us -> 5.27 us  [on_device(): lax.all_to_all(partial, 'tp', split_axis=0, concat_axis=0, tiled=True)]
  transfers between devices with their start and end apart: 9 -> 9, of which waited for: 5 -> 5; matrix products, arithmetic and copies ran while one was open for 1% -> 1% of each run, Pallas kernels for 7% -> 15%
where the time goes in v3:
time: 83.4 us; the launch traced here: 82.8 us
  waiting for transfers between devices  29.7 us (36%)
  starting transfers between devices  29.4 us (35%)
  Pallas kernels  21.2 us (25%)
  local copies, waits for them, and re-layouts  1.59 us (2%)
    all_to_all x1, waiting for transfers between devices, on_device(): lax.all_to_all(partial, 'tp', split_axis=0, concat_axis=0, tiled=True)  12.4 us
    pallas_call x2, Pallas kernels, on_device(): pl.pallas_call(functools.partial(attend_others, groups, list(given)), in_...  10.2 us
    all_to_all x1, starting transfers between devices, on_device(): got = lax.all_to_all(sent, 'inst', split_axis=0, concat_axis=0, tiled=True)  9.99 us
    all_to_all x1, waiting for transfers between devices, on_device(): back = lax.all_to_all(lent, 'inst', split_axis=0, concat_axis=0, tiled=True)  8.33 us
    all_to_all x1, starting transfers between devices, on_device(): back = lax.all_to_all(lent, 'inst', split_axis=0, concat_axis=0, tiled=True)  7.02 us
    all_to_all x1, waiting for transfers between devices, on_device(): got = lax.all_to_all(sent, 'inst', split_axis=0, concat_axis=0, tiled=True)  6.03 us
    all_to_all x1, starting transfers between devices, on_device(): lax.all_to_all(partial, 'tp', split_axis=0, concat_axis=0, tiled=True)  5.27 us
    ppermute x3, starting transfers between devices, on_device(): lax.ppermute(own, 'tp', x_shift(k))  4.29 us
  transfers between devices with their start and end apart: 9, of which 5 were waited for; matrix products, arithmetic and copies ran while one was open for 1% of the time, Pallas kernels for 15%

profile of v3, /device:TPU:1, one launch (start us, length us, event | category | flops | bytes accessed | tf_op | source)
XLA Modules:
  0.0 82.8 jit_solution(16337977508106701005)
XLA Ops:
  0.0 1.7 %prepare.1 = (bf16[384,128]{1,0:T(8,128)(2,1)}, f32[8,32]{1,0:T(8,128)}) custom-call(bf16[3,8,512]{2,1,0:T(8,128)(2,1)} %q_ref.1, s32[16,16]{1,0:T(8,128)} %owner_hbm.1), custom_call_target="tpu_custom_call" | custom-call | tf_op jit(solution)/shard_map/prepare/pallas_call | solution.py:405
  1.7 10.0 %all-to-all-start = ((bf16[16,24,128]{2,1,0:T(8,128)(2,1)}), bf16[16,24,128]{2,1,0:T(8,128)(2,1)S(1)}, u32[]{:S(2)}, u32[]{:S(2)}) async-start(bf16[16,24,128]{2,1,0:T(8,128)(2,1)} %bitcast.15), calls=%async_computation | async-start | bytes 196608 | tf_op jit(solution)/shard_map/all_to_all | solution.py:422
  11.7 2.4 %make_plan.1 = (s32[8,16]{1,0:T(8,128)}, f32[16,32]{1,0:T(8,128)}, f32[32,16]{1,0:T(8,128)}) custom-call(s32[16,16]{1,0:T(8,128)} %owner_hbm.1, s32[16,16]{1,0:T(8,128)} %start_ref.1, s32[16,16]{1,0:T(8,128)} %tokens_ref.1), custom_call_target="tpu_custom_call" | custom-call | tf_op jit(solution)/shard_map/make_plan/pallas_call | solution.py:424
  14.2 6.0 %all-to-all-done = bf16[16,24,128]{2,1,0:T(8,128)(2,1)S(1)} async-done(((bf16[16,24,128]{2,1,0:T(8,128)(2,1)}), bf16[16,24,128]{2,1,0:T(8,128)(2,1)S(1)}, u32[]{:S(2)}, u32[]{:S(2)}) %all-to-all-start) | async-done | bytes 98336 | tf_op jit(solution)/shard_map/all_to_all | solution.py:422
  20.2 0.0 copy-start.2
  20.2 0.7 copy-done.2
  20.9 0.2 pick_ranges.1
  21.1 1.3 %collective-permute-start = (bf16[16,1536]{1,0:T(8,128)(2,1)S(1)}, bf16[16,1536]{1,0:T(8,128)(2,1)S(1)}, u32[]{:S(2)}, u32[]{:S(2)}) collective-permute-start(bf16[16,1536]{1,0:T(8,128)(2,1)S(1)} %pick_ranges.1), channel_id=1, source_target_pairs={{0,1},{1,2},{2,3},{3,0},{4,5},{5,6},{6,7},{7,4},{8,9},{9,10},{10,1... | collective-permute-start | bytes 147464 | tf_op jit(solution)/shard_map/ppermute | solution.py:447
  22.4 1.5 %collective-permute-start.1 = (bf16[16,1536]{1,0:T(8,128)(2,1)S(1)}, bf16[16,1536]{1,0:T(8,128)(2,1)S(1)}, u32[]{:S(2)}, u32[]{:S(2)}) collective-permute-start(bf16[16,1536]{1,0:T(8,128)(2,1)S(1)} %pick_ranges.1), channel_id=1, source_target_pairs={{0,3},{1,0},{2,1},{3,2},{4,7},{5,4},{6,5},{7,6},{8,11},{9,8},{10,9... | collective-permute-start | bytes 147464 | tf_op jit(solution)/shard_map/ppermute | solution.py:447
  23.8 1.5 %collective-permute-start.2 = (bf16[16,1536]{1,0:T(8,128)(2,1)S(1)}, bf16[16,1536]{1,0:T(8,128)(2,1)S(1)}, u32[]{:S(2)}, u32[]{:S(2)}) collective-permute-start(bf16[16,1536]{1,0:T(8,128)(2,1)S(1)} %pick_ranges.1), channel_id=1, source_target_pairs={{0,2},{1,3},{2,0},{3,1},{4,6},{5,7},{6,4},{7,5},{8,10},{9,11},{10,... | collective-permute-start | bytes 147464 | tf_op jit(solution)/shard_map/ppermute | solution.py:447
  25.4 0.5 collective-permute-done
  25.8 0.0 collective-permute-done.1
  25.8 2.4 %collective-permute-done.2 = bf16[16,1536]{1,0:T(8,128)(2,1)S(1)} collective-permute-done((bf16[16,1536]{1,0:T(8,128)(2,1)S(1)}, bf16[16,1536]{1,0:T(8,128)(2,1)S(1)}, u32[]{:S(2)}, u32[]{:S(2)}) %collective-permute-start.2) | collective-permute-done | bytes 49184 | tf_op jit(solution)/shard_map/ppermute | solution.py:447
  28.3 0.7 pad_maximum_fusion.block
  29.0 1.3 %collective-permute-start.3 = (bf16[4,16,1536]{2,1,0:T(8,128)(2,1)}, bf16[4,16,1536]{2,1,0:T(8,128)(2,1)}, u32[]{:S(2)}, u32[]{:S(2)}) collective-permute-start(bf16[4,16,1536]{2,1,0:T(8,128)(2,1)} %pad_maximum_fusion.block), channel_id=1, source_target_pairs={{0,4},{1,5},{2,6},{3,7},{4,8},{5,9},{6,10},{7,11},{8,12},{9,13},{1... | collective-permute-start | bytes 589832 | tf_op jit(solution)/shard_map/ppermute | solution.py:448
  30.3 1.4 %collective-permute-start.5 = (bf16[4,16,1536]{2,1,0:T(8,128)(2,1)}, bf16[4,16,1536]{2,1,0:T(8,128)(2,1)}, u32[]{:S(2)}, u32[]{:S(2)}) collective-permute-start(bf16[4,16,1536]{2,1,0:T(8,128)(2,1)} %pad_maximum_fusion.block), channel_id=1, source_target_pairs={{0,12},{1,13},{2,14},{3,15},{4,0},{5,1},{6,2},{7,3},{8,4},{9,5},{1... | collective-permute-start | bytes 589832 | tf_op jit(solution)/shard_map/ppermute | solution.py:448
  31.7 4.0 %attend_own.1.refs_3_ = bf16[16,16,1664]{2,1,0:T(8,128)(2,1)} custom-call(s32[8,16]{1,0:T(8,128)} %get-tuple-element.13.plan_hbm, bf16[4,16,1536]{2,1,0:T(8,128)(2,1)} %pad_maximum_fusion.block, bf16[128,2,16,1024]{3,2,1,0:T(8,128)(2,1)} %refs_1_.1), custom_call_target="tpu_custom_call" | custom-call | flops 1000000000 | bytes 8388608 | tf_op jit(solution)/shard_map/attend_own/pallas_call | solution.py:455
  35.7 0.0 collective-permute-done.3.refs_0_
  35.8 0.1 collective-permute-start.4
  35.9 0.0 collective-permute-done.5.refs_1_
  35.9 6.2 %attend_others.2.refs_2_ = bf16[16,16,1664]{2,1,0:T(8,128)(2,1)} custom-call(s32[8,16]{1,0:T(8,128)} %get-tuple-element.13.plan_hbm, bf16[4,16,1536]{2,1,0:T(8,128)(2,1)} %collective-permute-done.3.refs_0_, bf16[4,16,1536]{2,1,0:T(8,128)(2,1)} %collective-permute-done.5.refs_1_, bf16[128,2,16,1024]{3,2,1,0:T(8,128)(2,1)} %refs_1_.1, ...), custom_call_target="tpu_custom_call", output_to_operand_aliasing={{}: (4, {})} | custom-call | flops 2000000000 | bytes 8388608 | tf_op jit(solution)/shard_map/attend_others/pallas_call | solution.py:477
  42.0 0.0 copy-start.1
  42.0 0.0 copy-start
  42.1 0.0 copy-start.3
  42.1 0.0 collective-permute-done.4.refs_0_
  42.1 4.1 %attend_others.3 = bf16[16,16,1664]{2,1,0:T(8,128)(2,1)} custom-call(s32[8,16]{1,0:T(8,128)} %get-tuple-element.13.plan_hbm, bf16[4,16,1536]{2,1,0:T(8,128)(2,1)} %collective-permute-done.4.refs_0_, bf16[128,2,16,1024]{3,2,1,0:T(8,128)(2,1)} %refs_1_.1, bf16[16,16,1664]{2,1,0:T(8,128)(2,1)} %attend_others.2.refs_2_), custom_call_target="tpu_custom_call", output_to_operand_aliasing={{}: (3, {})} | custom-call | flops 1000000000 | bytes 4194304 | tf_op jit(solution)/shard_map/attend_others/pallas_call | solution.py:477
  46.1 5.3 %all-to-all-start.1 = ((bf16[16,16,1664]{2,1,0:T(8,128)(2,1)}), bf16[16,16,1664]{2,1,0:T(8,128)(2,1)S(1)}, u32[]{:S(2)}, u32[]{:S(2)}) async-start(bf16[16,16,1664]{2,1,0:T(8,128)(2,1)} %attend_others.3), calls=%async_computation.1 | async-start | bytes 1703936 | tf_op jit(solution)/shard_map/all_to_all | solution.py:499
  51.4 12.4 %all-to-all-done.1.in_ref = bf16[16,16,1664]{2,1,0:T(8,128)(2,1)S(1)} async-done(((bf16[16,16,1664]{2,1,0:T(8,128)(2,1)}), bf16[16,16,1664]{2,1,0:T(8,128)(2,1)S(1)}, u32[]{:S(2)}, u32[]{:S(2)}) %all-to-all-start.1) | async-done | bytes 852000 | tf_op jit(solution)/shard_map/all_to_all | solution.py:499
  63.9 0.0 copy-done.1
  63.9 1.5 %merge_sources.1 = bf16[512,128]{1,0:T(8,128)(2,1)} custom-call(f32[32,16]{1,0:T(8,128)S(1)} %copy-done.1, bf16[16,16,1664]{2,1,0:T(8,128)(2,1)S(1)} %all-to-all-done.1.in_ref), custom_call_target="tpu_custom_call" | custom-call | tf_op jit(solution)/shard_map/merge_sources/pallas_call | solution.py:500
  65.4 7.0 %all-to-all-start.2 = ((bf16[16,32,128]{2,1,0:T(8,128)(2,1)}), bf16[16,32,128]{2,1,0:T(8,128)(2,1)S(1)}, u32[]{:S(2)}, u32[]{:S(2)}) async-start(bf16[16,32,128]{2,1,0:T(8,128)(2,1)} %bitcast.6), calls=%async_computation.2 | async-start | bytes 262144 | tf_op jit(solution)/shard_map/all_to_all | solution.py:509
  72.4 0.9 %constant_dynamic-slice_fusion.1 = (bf16[3,8,1,128]{3,2,1,0:T(2,128)(2,1)S(1)}, bf16[3,8,1,128]{3,2,1,0:T(2,128)(2,1)S(1)}) fusion(bf16[3,8,2,1024]{3,2,1,0:T(2,128)(2,1)} %param.7, s32[]{:T(128)S(6)} %add.5, s32[]{:T(128)S(6)} %select_n.9), kind=kLoop, calls=%fused_computation.4 | loop fusion | bytes 24584 | tf_op jit(solution)/shard_map/slice | solution.py:518
  73.3 8.3 %all-to-all-done.2 = bf16[16,32,128]{2,1,0:T(8,128)(2,1)S(1)} async-done(((bf16[16,32,128]{2,1,0:T(8,128)(2,1)}), bf16[16,32,128]{2,1,0:T(8,128)(2,1)S(1)}, u32[]{:S(2)}, u32[]{:S(2)}) %all-to-all-start.2) | async-done | bytes 131104 | tf_op jit(solution)/shard_map/all_to_all | solution.py:509
  81.6 0.0 copy-done
  81.6 0.0 copy-done.3
  81.6 1.2 %finish.1 = bf16[3,8,512]{2,1,0:T(8,128)(2,1)} custom-call(bf16[512,128]{1,0:T(8,128)(2,1)S(1)} %bitcast.12, f32[8,32]{1,0:T(8,128)S(1)} %copy-done.3, bf16[3,8,512]{2,1,0:T(8,128)(2,1)S(1)} %copy-done, bf16[3,8,128]{2,1,0:T(8,128)(2,1)S(1)} %get-tuple-element.22.k_ref, bf16[3,8,128]{2,1,0:T(8,128)(2,1)S(1)} %get-tuple-element.21.v_ref), custom_call_target="tpu_custom_call" | custom-call | tf_op jit(solution)/shard_map/finish/pallas_call | solution.py:510
  (1 shorter events, 0.0 us)
Async XLA Ops:
  1.7 18.5 %all-to-all-start = ((bf16[16,24,128]{2,1,0:T(8,128)(2,1)}), bf16[16,24,128]{2,1,0:T(8,128)(2,1)S(1)}, u32[]{:S(2)}, u32[]{:S(2)}) async-start(bf16[16,24,128]{2,1,0:T(8,128)(2,1)} %bitcast.15), calls=%async_computation | async-start | bytes 196608 | tf_op jit(solution)/shard_map/all_to_all | solution.py:422
  20.2 0.7 copy-start.2
  21.1 4.7 %collective-permute-start = (bf16[16,1536]{1,0:T(8,128)(2,1)S(1)}, bf16[16,1536]{1,0:T(8,128)(2,1)S(1)}, u32[]{:S(2)}, u32[]{:S(2)}) collective-permute-start(bf16[16,1536]{1,0:T(8,128)(2,1)S(1)} %pick_ranges.1), channel_id=1, source_target_pairs={{0,1},{1,2},{2,3},{3,0},{4,5},{5,6},{6,7},{7,4},{8,9},{9,10},{10,1... | collective-permute-start | bytes 147464 | tf_op jit(solution)/shard_map/ppermute | solution.py:447
  22.4 3.5 %collective-permute-start.1 = (bf16[16,1536]{1,0:T(8,128)(2,1)S(1)}, bf16[16,1536]{1,0:T(8,128)(2,1)S(1)}, u32[]{:S(2)}, u32[]{:S(2)}) collective-permute-start(bf16[16,1536]{1,0:T(8,128)(2,1)S(1)} %pick_ranges.1), channel_id=1, source_target_pairs={{0,3},{1,0},{2,1},{3,2},{4,7},{5,4},{6,5},{7,6},{8,11},{9,8},{10,9... | collective-permute-start | bytes 147464 | tf_op jit(solution)/shard_map/ppermute | solution.py:447
  23.8 4.4 %collective-permute-start.2 = (bf16[16,1536]{1,0:T(8,128)(2,1)S(1)}, bf16[16,1536]{1,0:T(8,128)(2,1)S(1)}, u32[]{:S(2)}, u32[]{:S(2)}) collective-permute-start(bf16[16,1536]{1,0:T(8,128)(2,1)S(1)} %pick_ranges.1), channel_id=1, source_target_pairs={{0,2},{1,3},{2,0},{3,1},{4,6},{5,7},{6,4},{7,5},{8,10},{9,11},{10,... | collective-permute-start | bytes 147464 | tf_op jit(solution)/shard_map/ppermute | solution.py:447
  29.0 6.8 %collective-permute-start.3 = (bf16[4,16,1536]{2,1,0:T(8,128)(2,1)}, bf16[4,16,1536]{2,1,0:T(8,128)(2,1)}, u32[]{:S(2)}, u32[]{:S(2)}) collective-permute-start(bf16[4,16,1536]{2,1,0:T(8,128)(2,1)} %pad_maximum_fusion.block), channel_id=1, source_target_pairs={{0,4},{1,5},{2,6},{3,7},{4,8},{5,9},{6,10},{7,11},{8,12},{9,13},{1... | collective-permute-start | bytes 589832 | tf_op jit(solution)/shard_map/ppermute | solution.py:448
  30.3 5.6 %collective-permute-start.5 = (bf16[4,16,1536]{2,1,0:T(8,128)(2,1)}, bf16[4,16,1536]{2,1,0:T(8,128)(2,1)}, u32[]{:S(2)}, u32[]{:S(2)}) collective-permute-start(bf16[4,16,1536]{2,1,0:T(8,128)(2,1)} %pad_maximum_fusion.block), channel_id=1, source_target_pairs={{0,12},{1,13},{2,14},{3,15},{4,0},{5,1},{6,2},{7,3},{8,4},{9,5},{1... | collective-permute-start | bytes 589832 | tf_op jit(solution)/shard_map/ppermute | solution.py:448
  35.8 6.3 %collective-permute-start.4 = (bf16[4,16,1536]{2,1,0:T(8,128)(2,1)}, bf16[4,16,1536]{2,1,0:T(8,128)(2,1)}, u32[]{:S(2)}, u32[]{:S(2)}) collective-permute-start(bf16[4,16,1536]{2,1,0:T(8,128)(2,1)} %collective-permute-done.3.refs_0_), channel_id=1, source_target_pairs={{0,4},{1,5},{2,6},{3,7},{4,8},{5,9},{6,10},{7,11},{8,12},{9,13},{1... | collective-permute-start | bytes 589832 | tf_op jit(solution)/shard_map/ppermute | solution.py:474
  42.0 21.8 %copy-start.1 = (f32[32,16]{1,0:T(8,128)S(1)}, f32[32,16]{1,0:T(8,128)}, u32[]{:S(2)}) copy-start(f32[32,16]{1,0:T(8,128)} %get-tuple-element.12.put_ref) | copy-start | bytes 6148
  42.0 39.6 %copy-start = (bf16[3,8,512]{2,1,0:T(8,128)(2,1)S(1)}, bf16[3,8,512]{2,1,0:T(8,128)(2,1)}, u32[]{:S(2)}) copy-start(bf16[3,8,512]{2,1,0:T(8,128)(2,1)} %q_ref.1) | copy-start | bytes 73732
  42.1 39.5 %copy-start.3 = (f32[8,32]{1,0:T(8,128)S(1)}, f32[8,32]{1,0:T(8,128)}, u32[]{:S(2)}) copy-start(f32[8,32]{1,0:T(8,128)} %get-tuple-element.18.owner_ref) | copy-start | bytes 3076
  46.1 17.7 %all-to-all-start.1 = ((bf16[16,16,1664]{2,1,0:T(8,128)(2,1)}), bf16[16,16,1664]{2,1,0:T(8,128)(2,1)S(1)}, u32[]{:S(2)}, u32[]{:S(2)}) async-start(bf16[16,16,1664]{2,1,0:T(8,128)(2,1)} %attend_others.3), calls=%async_computation.1 | async-start | bytes 1703936 | tf_op jit(solution)/shard_map/all_to_all | solution.py:499
  65.4 16.2 %all-to-all-start.2 = ((bf16[16,32,128]{2,1,0:T(8,128)(2,1)}), bf16[16,32,128]{2,1,0:T(8,128)(2,1)S(1)}, u32[]{:S(2)}, u32[]{:S(2)}) async-start(bf16[16,32,128]{2,1,0:T(8,128)(2,1)} %bitcast.6), calls=%async_computation.2 | async-start | bytes 262144 | tf_op jit(solution)/shard_map/all_to_all | solution.py:509

commit v4 on v3

--- a/solution.py
+++ b/solution.py
@@ -17,6 +17,7 @@
 FIRST = 8
 CHUNK = 16
 MORE = 8
+FEW = 2
 VERY_LOW = -1e30
 FLOOR = -1e29
 PAD = 16
@@ -204,10 +205,10 @@
         of[place(w[0]), :] = o
         lf[place(w[0]), :] = lse
 
-    def more(b, carry):
+    def more(size, done, b, carry):
         work = []
-        for j in range(MORE):
-            e = b * MORE + j
+        for j in range(size):
+            e = done + b * size + j
             work.append((plan[RANGE_ROW, e], plan[PAGE_ROW, e], plan[LOW_ROW, e], plan[HIGH_ROW, e]))
         for w, (o, lse) in zip(work, many(CHUNK, work)):
             at = place(w[0])
@@ -220,7 +221,12 @@
             lf[at, :] = high + jnp.log(total)
         return carry
 
-    lax.fori_loop(0, (plan[COUNT_ROW, 0] + MORE - 1) // MORE, more, 0)
+    count = plan[COUNT_ROW, 0]
+    large = (count + MORE // 2) // MORE
+    done = large * MORE
+    lax.fori_loop(0, large, functools.partial(more, MORE, 0), 0)
+    rest = (jnp.maximum(count - done, 0) + FEW - 1) // FEW
+    lax.fori_loop(0, rest, functools.partial(more, FEW, done), 0)
 
     lanes = iota((ranges, HEAD_DIM), 1)
     for x in range(SIDE):
@@ -277,7 +283,7 @@
     rows = [
         cache_copies(cache, kv.at[i], k, sems, 1 + count + 2 * i) for i, k in enumerate(shifts)
     ]
-    for copy in small + sum(rows, []):
+    for copy in small + rows[0]:
         copy.start()
     for copy in small:
         copy.wait()
@@ -292,6 +298,9 @@
                 @pl.when(i == k)
                 def _():
                     rows[k][w].wait()
+                    if w == 0 and k + 1 < count:
+                        for copy in rows[k + 1]:
+                            copy.start()
 
         wait_k, wait_v = functools.partial(wait, 0), functools.partial(wait, 1)
         keys, values = kv.at[i, 0], kv.at[i, 1]
@@ -318,7 +327,6 @@
     inverse = 1.0 / total
     shares = [s * inverse for s in shares]
     put = put_ref[...].astype(bf16)
-    stats = jnp.zeros((ranges, HEAD_DIM), f32)
     for g in range(groups):
         cols = slice(g * HEAD_DIM, (g + 1) * HEAD_DIM)
         acc = jnp.zeros((ranges, HEAD_DIM), f32)
@@ -327,8 +335,8 @@
         stage[pl.ds(g, slots, stride=PAD), :] = jnp.dot(
             put, acc.astype(bf16), preferred_element_type=f32
         )
-        mine = (lane == g) | (lane == g + groups) | (lane == g + 2 * groups)
-        stats = jnp.where(mine, jnp.broadcast_to(lse[:, g : g + 1], stats.shape), stats)
+    second, third = pltpu.roll(lse, groups, 1), pltpu.roll(lse, 2 * groups, 1)
+    stats = jnp.where(lane < groups, lse, jnp.where(lane < 2 * groups, second, third))
     parts = split3(stats, lane, groups)
     stage[pl.ds(groups, slots, stride=PAD), :] = jnp.dot(put, parts, preferred_element_type=f32)
     for g in range(groups + 1, PAD):
@@ -364,9 +372,10 @@
             top = jnp.maximum(top, jnp.max(lent, axis=1, keepdims=True))
             share = jnp.where(owned, jnp.exp(lent - top), 0.0)
             total = jnp.sum(share, axis=1, keepdims=True)
-            acc = jnp.dot(
-                share, group(g), preferred_element_type=f32, precision=lax.Precision.HIGHEST
-            )
+            high = share.astype(bf16).astype(f32)
+            parts = jnp.concatenate([high, share - high], axis=0).astype(bf16)
+            sums = jnp.dot(parts, group(g).astype(bf16), preferred_element_type=f32)
+            acc = sums[: len(share)] + sums[len(share) :]
             for t in range(s + 1):
                 weight = jnp.exp(scores[t] - top)
                 total = total + weight
@@ -399,6 +408,7 @@
     smem = pl.BlockSpec(memory_space=pltpu.SMEM)
     hbm = pl.BlockSpec(memory_space=pltpu.HBM)
     params = pltpu.CompilerParams(vmem_limit_bytes=24 * 2**20)
+    grant = pltpu.CompilerParams(vmem_limit_bytes=57 * 2**20)
     whole = pltpu.CompilerParams(vmem_limit_bytes=64 * 2**20 - 2**17)
     dma = pltpu.SemaphoreType.DMA
 
@@ -430,6 +440,7 @@
             jax.ShapeDtypeStruct((ranges, slots), f32),
             jax.ShapeDtypeStruct((slots, ranges), f32),
         ],
+        compiler_params=params,
         name="make_plan",
     )(range_owner, range_start, range_tokens)
     head = my_tp * heads // group_size
@@ -466,7 +477,7 @@
         ]
         + row_scratch
         + [dma((5,))],
-        compiler_params=whole,
+        compiler_params=grant,
         cost_estimate=pl.CostEstimate(flops=10**9, bytes_accessed=2**23, transcendentals=0),
         name="attend_own",
     )(plan, block, page_cache)

time: 83.4 us -> 82.3 us (0.987)
  waiting for transfers between devices: 29.7 us -> 27.2 us
  local copies, waits for them, and re-layouts: 1.59 us -> 3.56 us
    all_to_all x1, waiting for transfers between devices: 6.03 us -> 3.42 us  [on_device(): got = lax.all_to_all(sent, 'inst', split_axis=0, concat_axis=0, tiled=True)]
    unnamed x8 -> x14, local copies, waits for them, and re-layouts: 0.71 us -> 2.69 us
  transfers between devices with their start and end apart: 9 -> 9, of which waited for: 5 -> 5; matrix products, arithmetic and copies ran while one was open for 1% -> 1% of each run, Pallas kernels for 15% -> 16%
where the time goes in v4:
time: 82.3 us; the launch traced here: 81.6 us
  starting transfers between devices  29.5 us (36%)
  waiting for transfers between devices  27.2 us (33%)
  Pallas kernels  21.2 us (26%)
  local copies, waits for them, and re-layouts  3.56 us (4%)
    all_to_all x1, waiting for transfers between devices, on_device(): lax.all_to_all(partial, 'tp', split_axis=0, concat_axis=0, tiled=True)  12.6 us
    pallas_call x2, Pallas kernels, on_device(): pl.pallas_call(functools.partial(attend_others, groups, list(given)), in_...  10.3 us
    all_to_all x1, starting transfers between devices, on_device(): got = lax.all_to_all(sent, 'inst', split_axis=0, concat_axis=0, tiled=True)  9.99 us
    all_to_all x1, waiting for transfers between devices, on_device(): back = lax.all_to_all(lent, 'inst', split_axis=0, concat_axis=0, tiled=True)  8.28 us
    all_to_all x1, starting transfers between devices, on_device(): back = lax.all_to_all(lent, 'inst', split_axis=0, concat_axis=0, tiled=True)  6.94 us
    all_to_all x1, starting transfers between devices, on_device(): lax.all_to_all(partial, 'tp', split_axis=0, concat_axis=0, tiled=True)  5.26 us
    ppermute x3, starting transfers between devices, on_device(): lax.ppermute(own, 'tp', x_shift(k))  4.29 us
    pallas_call x1, Pallas kernels, on_device(): pl.pallas_call(functools.partial(attend_own, groups), in_specs=[hbm] * 3,...  4.07 us
  transfers between devices with their start and end apart: 9, of which 5 were waited for; matrix products, arithmetic and copies ran while one was open for 1% of the time, Pallas kernels for 16%

profile of v4, /device:TPU:1, one launch (start us, length us, event | category | flops | bytes accessed | tf_op | source)
XLA Modules:
  0.0 81.6 jit_solution(14430626253053409432)
XLA Ops:
  0.0 1.7 %prepare.1 = (bf16[384,128]{1,0:T(8,128)(2,1)}, f32[8,32]{1,0:T(8,128)}) custom-call(bf16[3,8,512]{2,1,0:T(8,128)(2,1)} %q_ref.1, s32[16,16]{1,0:T(8,128)} %owner_hbm.1), custom_call_target="tpu_custom_call" | custom-call | tf_op jit(solution)/shard_map/prepare/pallas_call | solution.py:415
  1.7 10.0 %all-to-all-start = ((bf16[16,24,128]{2,1,0:T(8,128)(2,1)}), bf16[16,24,128]{2,1,0:T(8,128)(2,1)S(1)}, u32[]{:S(2)}, u32[]{:S(2)}) async-start(bf16[16,24,128]{2,1,0:T(8,128)(2,1)} %bitcast.15), calls=%async_computation | async-start | bytes 196608 | tf_op jit(solution)/shard_map/all_to_all | solution.py:432
  11.7 0.0 copy-start.2
  11.7 0.7 copy-done.2
  12.4 0.0 copy-start.3
  12.4 0.7 copy-done.3
  13.1 0.0 copy-start.4
  13.1 0.7 copy-done.4
  13.8 2.4 %make_plan.1 = (s32[8,16]{1,0:T(8,128)S(1)}, f32[16,32]{1,0:T(8,128)S(1)}, f32[32,16]{1,0:T(8,128)S(1)}) custom-call(s32[16,16]{1,0:T(8,128)S(1)} %copy-done.2, s32[16,16]{1,0:T(8,128)S(1)} %copy-done.3, s32[16,16]{1,0:T(8,128)S(1)} %copy-done.4), custom_call_target="tpu_custom_call" | custom-call | tf_op jit(solution)/shard_map/make_plan/pallas_call | solution.py:434
  16.2 0.0 copy-start.1
  16.2 0.6 copy-done.1
  16.8 3.4 %all-to-all-done = bf16[16,24,128]{2,1,0:T(8,128)(2,1)S(1)} async-done(((bf16[16,24,128]{2,1,0:T(8,128)(2,1)}), bf16[16,24,128]{2,1,0:T(8,128)(2,1)S(1)}, u32[]{:S(2)}, u32[]{:S(2)}) %all-to-all-start) | async-done | bytes 98336 | tf_op jit(solution)/shard_map/all_to_all | solution.py:432
  20.2 0.2 pick_ranges.1
  20.4 1.3 %collective-permute-start = (bf16[16,1536]{1,0:T(8,128)(2,1)S(1)}, bf16[16,1536]{1,0:T(8,128)(2,1)S(1)}, u32[]{:S(2)}, u32[]{:S(2)}) collective-permute-start(bf16[16,1536]{1,0:T(8,128)(2,1)S(1)} %pick_ranges.1), channel_id=1, source_target_pairs={{0,1},{1,2},{2,3},{3,0},{4,5},{5,6},{6,7},{7,4},{8,9},{9,10},{10,1... | collective-permute-start | bytes 147464 | tf_op jit(solution)/shard_map/ppermute | solution.py:458
  21.7 1.5 %collective-permute-start.1 = (bf16[16,1536]{1,0:T(8,128)(2,1)S(1)}, bf16[16,1536]{1,0:T(8,128)(2,1)S(1)}, u32[]{:S(2)}, u32[]{:S(2)}) collective-permute-start(bf16[16,1536]{1,0:T(8,128)(2,1)S(1)} %pick_ranges.1), channel_id=1, source_target_pairs={{0,3},{1,0},{2,1},{3,2},{4,7},{5,4},{6,5},{7,6},{8,11},{9,8},{10,9... | collective-permute-start | bytes 147464 | tf_op jit(solution)/shard_map/ppermute | solution.py:458
  23.1 1.5 %collective-permute-start.2 = (bf16[16,1536]{1,0:T(8,128)(2,1)S(1)}, bf16[16,1536]{1,0:T(8,128)(2,1)S(1)}, u32[]{:S(2)}, u32[]{:S(2)}) collective-permute-start(bf16[16,1536]{1,0:T(8,128)(2,1)S(1)} %pick_ranges.1), channel_id=1, source_target_pairs={{0,2},{1,3},{2,0},{3,1},{4,6},{5,7},{6,4},{7,5},{8,10},{9,11},{10,... | collective-permute-start | bytes 147464 | tf_op jit(solution)/shard_map/ppermute | solution.py:458
  24.7 0.5 collective-permute-done
  25.1 0.0 collective-permute-done.1
  25.1 2.4 %collective-permute-done.2 = bf16[16,1536]{1,0:T(8,128)(2,1)S(1)} collective-permute-done((bf16[16,1536]{1,0:T(8,128)(2,1)S(1)}, bf16[16,1536]{1,0:T(8,128)(2,1)S(1)}, u32[]{:S(2)}, u32[]{:S(2)}) %collective-permute-start.2) | collective-permute-done | bytes 49184 | tf_op jit(solution)/shard_map/ppermute | solution.py:458
  27.6 0.0 copy-start.6
  27.6 1.4 %collective-permute-start.3 = (bf16[4,16,1536]{2,1,0:T(8,128)(2,1)S(1)}, bf16[4,16,1536]{2,1,0:T(8,128)(2,1)}, u32[]{:S(2)}, u32[]{:S(2)}) collective-permute-start(bf16[4,16,1536]{2,1,0:T(8,128)(2,1)S(1)} %pad_maximum_fusion.block), channel_id=1, source_target_pairs={{0,4},{1,5},{2,6},{3,7},{4,8},{5,9},{6,10},{7,11},{8,12},{9,13},{1... | collective-permute-start | bytes 589832 | tf_op jit(solution)/shard_map/ppermute | solution.py:459
  29.0 1.5 %collective-permute-start.5 = (bf16[4,16,1536]{2,1,0:T(8,128)(2,1)S(1)}, bf16[4,16,1536]{2,1,0:T(8,128)(2,1)}, u32[]{:S(2)}, u32[]{:S(2)}) collective-permute-start(bf16[4,16,1536]{2,1,0:T(8,128)(2,1)S(1)} %pad_maximum_fusion.block), channel_id=1, source_target_pairs={{0,12},{1,13},{2,14},{3,15},{4,0},{5,1},{6,2},{7,3},{8,4},{9,5},{1... | collective-permute-start | bytes 589832 | tf_op jit(solution)/shard_map/ppermute | solution.py:459
  30.5 0.0 copy-done.6
  30.5 4.1 %attend_own.1.refs_3_ = bf16[16,16,1664]{2,1,0:T(8,128)(2,1)} custom-call(s32[8,16]{1,0:T(8,128)} %copy-done.1, bf16[4,16,1536]{2,1,0:T(8,128)(2,1)} %copy-done.6, bf16[128,2,16,1024]{3,2,1,0:T(8,128)(2,1)} %refs_1_.1), custom_call_target="tpu_custom_call" | custom-call | flops 1000000000 | bytes 8388608 | tf_op jit(solution)/shard_map/attend_own/pallas_call | solution.py:466
  34.6 0.0 collective-permute-done.3.refs_0_
  34.6 0.1 collective-permute-start.4
  34.7 0.0 collective-permute-done.5.refs_1_
  34.7 6.2 %attend_others.2.refs_2_ = bf16[16,16,1664]{2,1,0:T(8,128)(2,1)} custom-call(s32[8,16]{1,0:T(8,128)} %copy-done.1, bf16[4,16,1536]{2,1,0:T(8,128)(2,1)} %collective-permute-done.3.refs_0_, bf16[4,16,1536]{2,1,0:T(8,128)(2,1)} %collective-permute-done.5.refs_1_, bf16[128,2,16,1024]{3,2,1,0:T(8,128)(2,1)} %refs_1_.1, ...), custom_call_target="tpu_custom_call", output_to_operand_aliasing={{}: (4, {})} | custom-call | flops 2000000000 | bytes 8388608 | tf_op jit(solution)/shard_map/attend_others/pallas_call | solution.py:488
  41.0 0.0 copy-start
  41.0 0.0 copy-start.5
  41.0 0.0 collective-permute-done.4.refs_0_
  41.0 4.1 %attend_others.3 = bf16[16,16,1664]{2,1,0:T(8,128)(2,1)} custom-call(s32[8,16]{1,0:T(8,128)} %copy-done.1, bf16[4,16,1536]{2,1,0:T(8,128)(2,1)} %collective-permute-done.4.refs_0_, bf16[128,2,16,1024]{3,2,1,0:T(8,128)(2,1)} %refs_1_.1, bf16[16,16,1664]{2,1,0:T(8,128)(2,1)} %attend_others.2.refs_2_), custom_call_target="tpu_custom_call", output_to_operand_aliasing={{}: (3, {})} | custom-call | flops 1000000000 | bytes 4194304 | tf_op jit(solution)/shard_map/attend_others/pallas_call | solution.py:488
  45.1 5.3 %all-to-all-start.1 = ((bf16[16,16,1664]{2,1,0:T(8,128)(2,1)}), bf16[16,16,1664]{2,1,0:T(8,128)(2,1)S(1)}, u32[]{:S(2)}, u32[]{:S(2)}) async-start(bf16[16,16,1664]{2,1,0:T(8,128)(2,1)} %attend_others.3), calls=%async_computation.1 | async-start | bytes 1703936 | tf_op jit(solution)/shard_map/all_to_all | solution.py:510
  50.4 12.6 %all-to-all-done.1.in_ref = bf16[16,16,1664]{2,1,0:T(8,128)(2,1)S(1)} async-done(((bf16[16,16,1664]{2,1,0:T(8,128)(2,1)}), bf16[16,16,1664]{2,1,0:T(8,128)(2,1)S(1)}, u32[]{:S(2)}, u32[]{:S(2)}) %all-to-all-start.1) | async-done | bytes 852000 | tf_op jit(solution)/shard_map/all_to_all | solution.py:510
  62.9 1.5 %merge_sources.1 = bf16[512,128]{1,0:T(8,128)(2,1)} custom-call(f32[32,16]{1,0:T(8,128)S(1)} %get-tuple-element.12.put_ref, bf16[16,16,1664]{2,1,0:T(8,128)(2,1)S(1)} %all-to-all-done.1.in_ref), custom_call_target="tpu_custom_call" | custom-call | tf_op jit(solution)/shard_map/merge_sources/pallas_call | solution.py:511
  64.4 6.9 %all-to-all-start.2 = ((bf16[16,32,128]{2,1,0:T(8,128)(2,1)}), bf16[16,32,128]{2,1,0:T(8,128)(2,1)S(1)}, u32[]{:S(2)}, u32[]{:S(2)}) async-start(bf16[16,32,128]{2,1,0:T(8,128)(2,1)} %bitcast.6), calls=%async_computation.2 | async-start | bytes 262144 | tf_op jit(solution)/shard_map/all_to_all | solution.py:520
  71.3 0.9 %constant_dynamic-slice_fusion.1 = (bf16[3,8,1,128]{3,2,1,0:T(2,128)(2,1)S(1)}, bf16[3,8,1,128]{3,2,1,0:T(2,128)(2,1)S(1)}) fusion(bf16[3,8,2,1024]{3,2,1,0:T(2,128)(2,1)} %param.7, s32[]{:T(128)S(6)} %add.5, s32[]{:T(128)S(6)} %select_n.9), kind=kLoop, calls=%fused_computation.4 | loop fusion | bytes 24584 | tf_op jit(solution)/shard_map/slice | solution.py:529
  72.2 8.3 %all-to-all-done.2 = bf16[16,32,128]{2,1,0:T(8,128)(2,1)S(1)} async-done(((bf16[16,32,128]{2,1,0:T(8,128)(2,1)}), bf16[16,32,128]{2,1,0:T(8,128)(2,1)S(1)}, u32[]{:S(2)}, u32[]{:S(2)}) %all-to-all-start.2) | async-done | bytes 131104 | tf_op jit(solution)/shard_map/all_to_all | solution.py:520
  80.5 0.0 copy-done
  80.5 0.0 copy-done.5
  80.5 1.0 %finish.1 = bf16[3,8,512]{2,1,0:T(8,128)(2,1)} custom-call(bf16[512,128]{1,0:T(8,128)(2,1)S(1)} %bitcast.12, f32[8,32]{1,0:T(8,128)S(1)} %copy-done.5, bf16[3,8,512]{2,1,0:T(8,128)(2,1)S(1)} %copy-done, bf16[3,8,128]{2,1,0:T(8,128)(2,1)S(1)} %get-tuple-element.22.k_ref, bf16[3,8,128]{2,1,0:T(8,128)(2,1)S(1)} %get-tuple-element.21.v_ref), custom_call_target="tpu_custom_call" | custom-call | tf_op jit(solution)/shard_map/finish/pallas_call | solution.py:521
  (2 shorter events, 0.0 us)
Async XLA Ops:
  1.7 18.5 %all-to-all-start = ((bf16[16,24,128]{2,1,0:T(8,128)(2,1)}), bf16[16,24,128]{2,1,0:T(8,128)(2,1)S(1)}, u32[]{:S(2)}, u32[]{:S(2)}) async-start(bf16[16,24,128]{2,1,0:T(8,128)(2,1)} %bitcast.15), calls=%async_computation | async-start | bytes 196608 | tf_op jit(solution)/shard_map/all_to_all | solution.py:432
  11.7 0.7 copy-start.2
  12.4 0.7 copy-start.3
  13.1 0.7 copy-start.4
  16.2 0.6 copy-start.1
  20.4 4.7 %collective-permute-start = (bf16[16,1536]{1,0:T(8,128)(2,1)S(1)}, bf16[16,1536]{1,0:T(8,128)(2,1)S(1)}, u32[]{:S(2)}, u32[]{:S(2)}) collective-permute-start(bf16[16,1536]{1,0:T(8,128)(2,1)S(1)} %pick_ranges.1), channel_id=1, source_target_pairs={{0,1},{1,2},{2,3},{3,0},{4,5},{5,6},{6,7},{7,4},{8,9},{9,10},{10,1... | collective-permute-start | bytes 147464 | tf_op jit(solution)/shard_map/ppermute | solution.py:458
  21.7 3.5 %collective-permute-start.1 = (bf16[16,1536]{1,0:T(8,128)(2,1)S(1)}, bf16[16,1536]{1,0:T(8,128)(2,1)S(1)}, u32[]{:S(2)}, u32[]{:S(2)}) collective-permute-start(bf16[16,1536]{1,0:T(8,128)(2,1)S(1)} %pick_ranges.1), channel_id=1, source_target_pairs={{0,3},{1,0},{2,1},{3,2},{4,7},{5,4},{6,5},{7,6},{8,11},{9,8},{10,9... | collective-permute-start | bytes 147464 | tf_op jit(solution)/shard_map/ppermute | solution.py:458
  23.1 4.4 %collective-permute-start.2 = (bf16[16,1536]{1,0:T(8,128)(2,1)S(1)}, bf16[16,1536]{1,0:T(8,128)(2,1)S(1)}, u32[]{:S(2)}, u32[]{:S(2)}) collective-permute-start(bf16[16,1536]{1,0:T(8,128)(2,1)S(1)} %pick_ranges.1), channel_id=1, source_target_pairs={{0,2},{1,3},{2,0},{3,1},{4,6},{5,7},{6,4},{7,5},{8,10},{9,11},{10,... | collective-permute-start | bytes 147464 | tf_op jit(solution)/shard_map/ppermute | solution.py:458
  27.6 2.9 %copy-start.6 = (bf16[4,16,1536]{2,1,0:T(8,128)(2,1)}, bf16[4,16,1536]{2,1,0:T(8,128)(2,1)S(1)}, u32[]{:S(2)}) copy-start(bf16[4,16,1536]{2,1,0:T(8,128)(2,1)S(1)} %pad_maximum_fusion.block) | copy-start | bytes 589828
  27.6 7.0 %collective-permute-start.3 = (bf16[4,16,1536]{2,1,0:T(8,128)(2,1)S(1)}, bf16[4,16,1536]{2,1,0:T(8,128)(2,1)}, u32[]{:S(2)}, u32[]{:S(2)}) collective-permute-start(bf16[4,16,1536]{2,1,0:T(8,128)(2,1)S(1)} %pad_maximum_fusion.block), channel_id=1, source_target_pairs={{0,4},{1,5},{2,6},{3,7},{4,8},{5,9},{6,10},{7,11},{8,12},{9,13},{1... | collective-permute-start | bytes 589832 | tf_op jit(solution)/shard_map/ppermute | solution.py:459
  29.0 5.7 %collective-permute-start.5 = (bf16[4,16,1536]{2,1,0:T(8,128)(2,1)S(1)}, bf16[4,16,1536]{2,1,0:T(8,128)(2,1)}, u32[]{:S(2)}, u32[]{:S(2)}) collective-permute-start(bf16[4,16,1536]{2,1,0:T(8,128)(2,1)S(1)} %pad_maximum_fusion.block), channel_id=1, source_target_pairs={{0,12},{1,13},{2,14},{3,15},{4,0},{5,1},{6,2},{7,3},{8,4},{9,5},{1... | collective-permute-start | bytes 589832 | tf_op jit(solution)/shard_map/ppermute | solution.py:459
  34.6 6.4 %collective-permute-start.4 = (bf16[4,16,1536]{2,1,0:T(8,128)(2,1)}, bf16[4,16,1536]{2,1,0:T(8,128)(2,1)}, u32[]{:S(2)}, u32[]{:S(2)}) collective-permute-start(bf16[4,16,1536]{2,1,0:T(8,128)(2,1)} %collective-permute-done.3.refs_0_), channel_id=1, source_target_pairs={{0,4},{1,5},{2,6},{3,7},{4,8},{5,9},{6,10},{7,11},{8,12},{9,13},{1... | collective-permute-start | bytes 589832 | tf_op jit(solution)/shard_map/ppermute | solution.py:485
  41.0 39.5 %copy-start = (bf16[3,8,512]{2,1,0:T(8,128)(2,1)S(1)}, bf16[3,8,512]{2,1,0:T(8,128)(2,1)}, u32[]{:S(2)}) copy-start(bf16[3,8,512]{2,1,0:T(8,128)(2,1)} %q_ref.1) | copy-start | bytes 73732
  41.0 39.5 %copy-start.5 = (f32[8,32]{1,0:T(8,128)S(1)}, f32[8,32]{1,0:T(8,128)}, u32[]{:S(2)}) copy-start(f32[8,32]{1,0:T(8,128)} %get-tuple-element.18.owner_ref) | copy-start | bytes 3076
  45.1 17.8 %all-to-all-start.1 = ((bf16[16,16,1664]{2,1,0:T(8,128)(2,1)}), bf16[16,16,1664]{2,1,0:T(8,128)(2,1)S(1)}, u32[]{:S(2)}, u32[]{:S(2)}) async-start(bf16[16,16,1664]{2,1,0:T(8,128)(2,1)} %attend_others.3), calls=%async_computation.1 | async-start | bytes 1703936 | tf_op jit(solution)/shard_map/all_to_all | solution.py:510
  64.4 16.1 %all-to-all-start.2 = ((bf16[16,32,128]{2,1,0:T(8,128)(2,1)}), bf16[16,32,128]{2,1,0:T(8,128)(2,1)S(1)}, u32[]{:S(2)}, u32[]{:S(2)}) async-start(bf16[16,32,128]{2,1,0:T(8,128)(2,1)} %bitcast.6), calls=%async_computation.2 | async-start | bytes 262144 | tf_op jit(solution)/shard_map/all_to_all | solution.py:520

commit v5 on v4

--- a/solution.py
+++ b/solution.py
@@ -184,49 +184,50 @@
         o = jnp.dot(p, load(v_ref, page, span), preferred_element_type=f32)
         return jnp.where(top, o[:, :HEAD_DIM], o[:, HEAD_DIM:]) * inverse
 
-    def many(span, work, wait=None):
-        s = [scores(span, *w) for w in work]
-        s = [softmax(one) for one in s]
-        if wait is not None:
-            wait()
-        o = [values(span, w[1], one[0], one[1]) for one, w in zip(s, work)]
-        return [(one, lse) for one, (_, _, lse) in zip(o, s)]
-
     def place(r):
         return pl.ds(pl.multiple_of(r * rows, 8), rows)
+
+    def later(e):
+        return plan[RANGE_ROW, e], plan[PAGE_ROW, e], plan[LOW_ROW, e], plan[HIGH_ROW, e]
+
+    def join(r, o, lse):
+        at = place(r)
+        old = lf[at, :]
+        high = jnp.maximum(old, lse)
+        share_old = jnp.exp(old - high)
+        share = jnp.exp(lse - high)
+        total = share_old + share
+        of[at, :] = (of[at, :] * share_old + o * share) / total
+        lf[at, :] = high + jnp.log(total)
 
     work = []
     for r in range(ranges):
         start = plan[START_ROW, r]
         page = jnp.minimum(start, pages - FIRST)
-        work.append((r, page, start * slice_tokens, plan[END_ROW, r]))
+        work.append((FIRST, r, page, start * slice_tokens, plan[END_ROW, r]))
+    for e in range(MORE):
+        work.append((CHUNK, *later(e)))
     wait_k()
-    for w, (o, lse) in zip(work, many(FIRST, work, wait_v)):
-        of[place(w[0]), :] = o
-        lf[place(w[0]), :] = lse
-
-    def more(size, done, b, carry):
-        work = []
-        for j in range(size):
-            e = done + b * size + j
-            work.append((plan[RANGE_ROW, e], plan[PAGE_ROW, e], plan[LOW_ROW, e], plan[HIGH_ROW, e]))
-        for w, (o, lse) in zip(work, many(CHUNK, work)):
-            at = place(w[0])
-            old = lf[at, :]
-            high = jnp.maximum(old, lse)
-            share_old = jnp.exp(old - high)
-            share = jnp.exp(lse - high)
-            total = share_old + share
-            of[at, :] = (of[at, :] * share_old + o * share) / total
-            lf[at, :] = high + jnp.log(total)
+    parts = [scores(*w) for w in work]
+    parts = [softmax(one) for one in parts]
+    wait_v()
+    outs = [values(w[0], w[2], p[0], p[1]) for p, w in zip(parts, work)]
+
+    for w, (_, _, lse), o in zip(work[:ranges], parts, outs):
+        of[place(w[1]), :] = o
+        lf[place(w[1]), :] = lse
+    for w, (_, _, lse), o in zip(work[ranges:], parts[ranges:], outs[ranges:]):
+        join(w[1], o, lse)
+
+    def few(b, carry):
+        work = [later(MORE + b * FEW + j) for j in range(FEW)]
+        parts = [softmax(scores(CHUNK, *w)) for w in work]
+        outs = [values(CHUNK, w[1], p[0], p[1]) for p, w in zip(parts, work)]
+        for w, (_, _, lse), o in zip(work, parts, outs):
+            join(w[0], o, lse)
         return carry
 
-    count = plan[COUNT_ROW, 0]
-    large = (count + MORE // 2) // MORE
-    done = large * MORE
-    lax.fori_loop(0, large, functools.partial(more, MORE, 0), 0)
-    rest = (jnp.maximum(count - done, 0) + FEW - 1) // FEW
-    lax.fori_loop(0, rest, functools.partial(more, FEW, done), 0)
+    lax.fori_loop(0, (jnp.maximum(plan[COUNT_ROW, 0] - MORE, 0) + FEW - 1) // FEW, few, 0)
 
     lanes = iota((ranges, HEAD_DIM), 1)
     for x in range(SIDE):

time: 82.3 us -> 81.6 us (level)
  transfers between devices with their start and end apart: 9 -> 9, of which waited for: 5 -> 6; matrix products, arithmetic and copies ran while one was open for 1% -> 1% of each run, Pallas kernels for 16% -> 15%
where the time goes in v5:
time: 81.6 us; the launch traced here: 80.9 us
  starting transfers between devices  29.4 us (36%)
  waiting for transfers between devices  27.3 us (33%)
  Pallas kernels  20.4 us (25%)
  local copies, waits for them, and re-layouts  3.56 us (4%)
    all_to_all x1, waiting for transfers between devices, on_device(): lax.all_to_all(partial, 'tp', split_axis=0, concat_axis=0, tiled=True)  12.5 us
    all_to_all x1, starting transfers between devices, on_device(): got = lax.all_to_all(sent, 'inst', split_axis=0, concat_axis=0, tiled=True)  9.99 us
    pallas_call x2, Pallas kernels, on_device(): pl.pallas_call(functools.partial(attend_others, groups, list(given)), in_...  9.79 us
    all_to_all x1, waiting for transfers between devices, on_device(): back = lax.all_to_all(lent, 'inst', split_axis=0, concat_axis=0, tiled=True)  8.28 us
    all_to_all x1, starting transfers between devices, on_device(): back = lax.all_to_all(lent, 'inst', split_axis=0, concat_axis=0, tiled=True)  7.01 us
    all_to_all x1, starting transfers between devices, on_device(): lax.all_to_all(partial, 'tp', split_axis=0, concat_axis=0, tiled=True)  5.16 us
    ppermute x3, starting transfers between devices, on_device(): lax.ppermute(own, 'tp', x_shift(k))  4.29 us
    pallas_call x1, Pallas kernels, on_device(): pl.pallas_call(functools.partial(attend_own, groups), in_specs=[hbm] * 3,...  3.89 us
  transfers between devices with their start and end apart: 9, of which 6 were waited for; matrix products, arithmetic and copies ran while one was open for 1% of the time, Pallas kernels for 15%

profile of v5, /device:TPU:1, one launch (start us, length us, event | category | flops | bytes accessed | tf_op | source)
XLA Modules:
  0.0 80.9 jit_solution(15153564461853212269)
XLA Ops:
  0.0 1.7 %prepare.1 = (bf16[384,128]{1,0:T(8,128)(2,1)}, f32[8,32]{1,0:T(8,128)}) custom-call(bf16[3,8,512]{2,1,0:T(8,128)(2,1)} %q_ref.1, s32[16,16]{1,0:T(8,128)} %owner_hbm.1), custom_call_target="tpu_custom_call" | custom-call | tf_op jit(solution)/shard_map/prepare/pallas_call | solution.py:416
  1.7 10.0 %all-to-all-start = ((bf16[16,24,128]{2,1,0:T(8,128)(2,1)}), bf16[16,24,128]{2,1,0:T(8,128)(2,1)S(1)}, u32[]{:S(2)}, u32[]{:S(2)}) async-start(bf16[16,24,128]{2,1,0:T(8,128)(2,1)} %bitcast.15), calls=%async_computation | async-start | bytes 196608 | tf_op jit(solution)/shard_map/all_to_all | solution.py:433
  11.7 0.0 copy-start.2
  11.7 0.7 copy-done.2
  12.4 0.0 copy-start.3
  12.4 0.7 copy-done.3
  13.1 0.0 copy-start.4
  13.1 0.7 copy-done.4
  13.8 2.4 %make_plan.1 = (s32[8,16]{1,0:T(8,128)S(1)}, f32[16,32]{1,0:T(8,128)S(1)}, f32[32,16]{1,0:T(8,128)S(1)}) custom-call(s32[16,16]{1,0:T(8,128)S(1)} %copy-done.2, s32[16,16]{1,0:T(8,128)S(1)} %copy-done.3, s32[16,16]{1,0:T(8,128)S(1)} %copy-done.4), custom_call_target="tpu_custom_call" | custom-call | tf_op jit(solution)/shard_map/make_plan/pallas_call | solution.py:435
  16.2 0.0 copy-start.1
  16.2 0.6 copy-done.1
  16.8 3.4 %all-to-all-done = bf16[16,24,128]{2,1,0:T(8,128)(2,1)S(1)} async-done(((bf16[16,24,128]{2,1,0:T(8,128)(2,1)}), bf16[16,24,128]{2,1,0:T(8,128)(2,1)S(1)}, u32[]{:S(2)}, u32[]{:S(2)}) %all-to-all-start) | async-done | bytes 98336 | tf_op jit(solution)/shard_map/all_to_all | solution.py:433
  20.2 0.2 pick_ranges.1
  20.4 1.3 %collective-permute-start = (bf16[16,1536]{1,0:T(8,128)(2,1)S(1)}, bf16[16,1536]{1,0:T(8,128)(2,1)S(1)}, u32[]{:S(2)}, u32[]{:S(2)}) collective-permute-start(bf16[16,1536]{1,0:T(8,128)(2,1)S(1)} %pick_ranges.1), channel_id=1, source_target_pairs={{0,1},{1,2},{2,3},{3,0},{4,5},{5,6},{6,7},{7,4},{8,9},{9,10},{10,1... | collective-permute-start | bytes 147464 | tf_op jit(solution)/shard_map/ppermute | solution.py:459
  21.7 1.5 %collective-permute-start.1 = (bf16[16,1536]{1,0:T(8,128)(2,1)S(1)}, bf16[16,1536]{1,0:T(8,128)(2,1)S(1)}, u32[]{:S(2)}, u32[]{:S(2)}) collective-permute-start(bf16[16,1536]{1,0:T(8,128)(2,1)S(1)} %pick_ranges.1), channel_id=1, source_target_pairs={{0,3},{1,0},{2,1},{3,2},{4,7},{5,4},{6,5},{7,6},{8,11},{9,8},{10,9... | collective-permute-start | bytes 147464 | tf_op jit(solution)/shard_map/ppermute | solution.py:459
  23.1 1.5 %collective-permute-start.2 = (bf16[16,1536]{1,0:T(8,128)(2,1)S(1)}, bf16[16,1536]{1,0:T(8,128)(2,1)S(1)}, u32[]{:S(2)}, u32[]{:S(2)}) collective-permute-start(bf16[16,1536]{1,0:T(8,128)(2,1)S(1)} %pick_ranges.1), channel_id=1, source_target_pairs={{0,2},{1,3},{2,0},{3,1},{4,6},{5,7},{6,4},{7,5},{8,10},{9,11},{10,... | collective-permute-start | bytes 147464 | tf_op jit(solution)/shard_map/ppermute | solution.py:459
  24.7 0.5 collective-permute-done
  25.1 0.0 collective-permute-done.1
  25.1 2.4 %collective-permute-done.2 = bf16[16,1536]{1,0:T(8,128)(2,1)S(1)} collective-permute-done((bf16[16,1536]{1,0:T(8,128)(2,1)S(1)}, bf16[16,1536]{1,0:T(8,128)(2,1)S(1)}, u32[]{:S(2)}, u32[]{:S(2)}) %collective-permute-start.2) | collective-permute-done | bytes 49184 | tf_op jit(solution)/shard_map/ppermute | solution.py:459
  27.6 0.0 copy-start.6
  27.6 1.4 %collective-permute-start.3 = (bf16[4,16,1536]{2,1,0:T(8,128)(2,1)S(1)}, bf16[4,16,1536]{2,1,0:T(8,128)(2,1)}, u32[]{:S(2)}, u32[]{:S(2)}) collective-permute-start(bf16[4,16,1536]{2,1,0:T(8,128)(2,1)S(1)} %pad_maximum_fusion.block), channel_id=1, source_target_pairs={{0,4},{1,5},{2,6},{3,7},{4,8},{5,9},{6,10},{7,11},{8,12},{9,13},{1... | collective-permute-start | bytes 589832 | tf_op jit(solution)/shard_map/ppermute | solution.py:460
  29.0 1.5 %collective-permute-start.5 = (bf16[4,16,1536]{2,1,0:T(8,128)(2,1)S(1)}, bf16[4,16,1536]{2,1,0:T(8,128)(2,1)}, u32[]{:S(2)}, u32[]{:S(2)}) collective-permute-start(bf16[4,16,1536]{2,1,0:T(8,128)(2,1)S(1)} %pad_maximum_fusion.block), channel_id=1, source_target_pairs={{0,12},{1,13},{2,14},{3,15},{4,0},{5,1},{6,2},{7,3},{8,4},{9,5},{1... | collective-permute-start | bytes 589832 | tf_op jit(solution)/shard_map/ppermute | solution.py:460
  30.5 0.0 copy-done.6
  30.5 3.9 %attend_own.1.refs_3_ = bf16[16,16,1664]{2,1,0:T(8,128)(2,1)} custom-call(s32[8,16]{1,0:T(8,128)} %copy-done.1, bf16[4,16,1536]{2,1,0:T(8,128)(2,1)} %copy-done.6, bf16[128,2,16,1024]{3,2,1,0:T(8,128)(2,1)} %refs_1_.1), custom_call_target="tpu_custom_call" | custom-call | flops 1000000000 | bytes 8388608 | tf_op jit(solution)/shard_map/attend_own/pallas_call | solution.py:467
  34.4 0.0 collective-permute-done.3.refs_0_
  34.4 0.1 collective-permute-start.4
  34.5 0.0 collective-permute-done.5.refs_1_
  34.5 5.9 %attend_others.2.refs_2_ = bf16[16,16,1664]{2,1,0:T(8,128)(2,1)} custom-call(s32[8,16]{1,0:T(8,128)} %copy-done.1, bf16[4,16,1536]{2,1,0:T(8,128)(2,1)} %collective-permute-done.3.refs_0_, bf16[4,16,1536]{2,1,0:T(8,128)(2,1)} %collective-permute-done.5.refs_1_, bf16[128,2,16,1024]{3,2,1,0:T(8,128)(2,1)} %refs_1_.1, ...), custom_call_target="tpu_custom_call", output_to_operand_aliasing={{}: (4, {})} | custom-call | flops 2000000000 | bytes 8388608 | tf_op jit(solution)/shard_map/attend_others/pallas_call | solution.py:489
  40.4 0.0 copy-start
  40.4 0.0 copy-start.5
  40.5 0.1 collective-permute-done.4.refs_0_
  40.6 3.9 %attend_others.3 = bf16[16,16,1664]{2,1,0:T(8,128)(2,1)} custom-call(s32[8,16]{1,0:T(8,128)} %copy-done.1, bf16[4,16,1536]{2,1,0:T(8,128)(2,1)} %collective-permute-done.4.refs_0_, bf16[128,2,16,1024]{3,2,1,0:T(8,128)(2,1)} %refs_1_.1, bf16[16,16,1664]{2,1,0:T(8,128)(2,1)} %attend_others.2.refs_2_), custom_call_target="tpu_custom_call", output_to_operand_aliasing={{}: (3, {})} | custom-call | flops 1000000000 | bytes 4194304 | tf_op jit(solution)/shard_map/attend_others/pallas_call | solution.py:489
  44.5 5.2 %all-to-all-start.1 = ((bf16[16,16,1664]{2,1,0:T(8,128)(2,1)}), bf16[16,16,1664]{2,1,0:T(8,128)(2,1)S(1)}, u32[]{:S(2)}, u32[]{:S(2)}) async-start(bf16[16,16,1664]{2,1,0:T(8,128)(2,1)} %attend_others.3), calls=%async_computation.1 | async-start | bytes 1703936 | tf_op jit(solution)/shard_map/all_to_all | solution.py:511
  49.7 12.5 %all-to-all-done.1.in_ref = bf16[16,16,1664]{2,1,0:T(8,128)(2,1)S(1)} async-done(((bf16[16,16,1664]{2,1,0:T(8,128)(2,1)}), bf16[16,16,1664]{2,1,0:T(8,128)(2,1)S(1)}, u32[]{:S(2)}, u32[]{:S(2)}) %all-to-all-start.1) | async-done | bytes 852000 | tf_op jit(solution)/shard_map/all_to_all | solution.py:511
  62.2 1.5 %merge_sources.1 = bf16[512,128]{1,0:T(8,128)(2,1)} custom-call(f32[32,16]{1,0:T(8,128)S(1)} %get-tuple-element.12.put_ref, bf16[16,16,1664]{2,1,0:T(8,128)(2,1)S(1)} %all-to-all-done.1.in_ref), custom_call_target="tpu_custom_call" | custom-call | tf_op jit(solution)/shard_map/merge_sources/pallas_call | solution.py:512
  63.7 7.0 %all-to-all-start.2 = ((bf16[16,32,128]{2,1,0:T(8,128)(2,1)}), bf16[16,32,128]{2,1,0:T(8,128)(2,1)S(1)}, u32[]{:S(2)}, u32[]{:S(2)}) async-start(bf16[16,32,128]{2,1,0:T(8,128)(2,1)} %bitcast.6), calls=%async_computation.2 | async-start | bytes 262144 | tf_op jit(solution)/shard_map/all_to_all | solution.py:521
  70.7 0.9 %constant_dynamic-slice_fusion.1 = (bf16[3,8,1,128]{3,2,1,0:T(2,128)(2,1)S(1)}, bf16[3,8,1,128]{3,2,1,0:T(2,128)(2,1)S(1)}) fusion(bf16[3,8,2,1024]{3,2,1,0:T(2,128)(2,1)} %param.7, s32[]{:T(128)S(6)} %add.5, s32[]{:T(128)S(6)} %select_n.9), kind=kLoop, calls=%fused_computation.4 | loop fusion | bytes 24584 | tf_op jit(solution)/shard_map/slice | solution.py:530
  71.6 8.3 %all-to-all-done.2 = bf16[16,32,128]{2,1,0:T(8,128)(2,1)S(1)} async-done(((bf16[16,32,128]{2,1,0:T(8,128)(2,1)}), bf16[16,32,128]{2,1,0:T(8,128)(2,1)S(1)}, u32[]{:S(2)}, u32[]{:S(2)}) %all-to-all-start.2) | async-done | bytes 131104 | tf_op jit(solution)/shard_map/all_to_all | solution.py:521
  79.8 0.0 copy-done
  79.8 0.0 copy-done.5
  79.8 1.0 %finish.1 = bf16[3,8,512]{2,1,0:T(8,128)(2,1)} custom-call(bf16[512,128]{1,0:T(8,128)(2,1)S(1)} %bitcast.12, f32[8,32]{1,0:T(8,128)S(1)} %copy-done.5, bf16[3,8,512]{2,1,0:T(8,128)(2,1)S(1)} %copy-done, bf16[3,8,128]{2,1,0:T(8,128)(2,1)S(1)} %get-tuple-element.22.k_ref, bf16[3,8,128]{2,1,0:T(8,128)(2,1)S(1)} %get-tuple-element.21.v_ref), custom_call_target="tpu_custom_call" | custom-call | tf_op jit(solution)/shard_map/finish/pallas_call | solution.py:522
  (2 shorter events, 0.0 us)
Async XLA Ops:
  1.7 18.5 %all-to-all-start = ((bf16[16,24,128]{2,1,0:T(8,128)(2,1)}), bf16[16,24,128]{2,1,0:T(8,128)(2,1)S(1)}, u32[]{:S(2)}, u32[]{:S(2)}) async-start(bf16[16,24,128]{2,1,0:T(8,128)(2,1)} %bitcast.15), calls=%async_computation | async-start | bytes 196608 | tf_op jit(solution)/shard_map/all_to_all | solution.py:433
  11.7 0.7 copy-start.2
  12.4 0.7 copy-start.3
  13.1 0.7 copy-start.4
  16.2 0.6 copy-start.1
  20.4 4.7 %collective-permute-start = (bf16[16,1536]{1,0:T(8,128)(2,1)S(1)}, bf16[16,1536]{1,0:T(8,128)(2,1)S(1)}, u32[]{:S(2)}, u32[]{:S(2)}) collective-permute-start(bf16[16,1536]{1,0:T(8,128)(2,1)S(1)} %pick_ranges.1), channel_id=1, source_target_pairs={{0,1},{1,2},{2,3},{3,0},{4,5},{5,6},{6,7},{7,4},{8,9},{9,10},{10,1... | collective-permute-start | bytes 147464 | tf_op jit(solution)/shard_map/ppermute | solution.py:459
  21.7 3.5 %collective-permute-start.1 = (bf16[16,1536]{1,0:T(8,128)(2,1)S(1)}, bf16[16,1536]{1,0:T(8,128)(2,1)S(1)}, u32[]{:S(2)}, u32[]{:S(2)}) collective-permute-start(bf16[16,1536]{1,0:T(8,128)(2,1)S(1)} %pick_ranges.1), channel_id=1, source_target_pairs={{0,3},{1,0},{2,1},{3,2},{4,7},{5,4},{6,5},{7,6},{8,11},{9,8},{10,9... | collective-permute-start | bytes 147464 | tf_op jit(solution)/shard_map/ppermute | solution.py:459
  23.1 4.4 %collective-permute-start.2 = (bf16[16,1536]{1,0:T(8,128)(2,1)S(1)}, bf16[16,1536]{1,0:T(8,128)(2,1)S(1)}, u32[]{:S(2)}, u32[]{:S(2)}) collective-permute-start(bf16[16,1536]{1,0:T(8,128)(2,1)S(1)} %pick_ranges.1), channel_id=1, source_target_pairs={{0,2},{1,3},{2,0},{3,1},{4,6},{5,7},{6,4},{7,5},{8,10},{9,11},{10,... | collective-permute-start | bytes 147464 | tf_op jit(solution)/shard_map/ppermute | solution.py:459
  27.6 2.9 %copy-start.6 = (bf16[4,16,1536]{2,1,0:T(8,128)(2,1)}, bf16[4,16,1536]{2,1,0:T(8,128)(2,1)S(1)}, u32[]{:S(2)}) copy-start(bf16[4,16,1536]{2,1,0:T(8,128)(2,1)S(1)} %pad_maximum_fusion.block) | copy-start | bytes 589828
  27.6 6.8 %collective-permute-start.3 = (bf16[4,16,1536]{2,1,0:T(8,128)(2,1)S(1)}, bf16[4,16,1536]{2,1,0:T(8,128)(2,1)}, u32[]{:S(2)}, u32[]{:S(2)}) collective-permute-start(bf16[4,16,1536]{2,1,0:T(8,128)(2,1)S(1)} %pad_maximum_fusion.block), channel_id=1, source_target_pairs={{0,4},{1,5},{2,6},{3,7},{4,8},{5,9},{6,10},{7,11},{8,12},{9,13},{1... | collective-permute-start | bytes 589832 | tf_op jit(solution)/shard_map/ppermute | solution.py:460
  29.0 5.5 %collective-permute-start.5 = (bf16[4,16,1536]{2,1,0:T(8,128)(2,1)S(1)}, bf16[4,16,1536]{2,1,0:T(8,128)(2,1)}, u32[]{:S(2)}, u32[]{:S(2)}) collective-permute-start(bf16[4,16,1536]{2,1,0:T(8,128)(2,1)S(1)} %pad_maximum_fusion.block), channel_id=1, source_target_pairs={{0,12},{1,13},{2,14},{3,15},{4,0},{5,1},{6,2},{7,3},{8,4},{9,5},{1... | collective-permute-start | bytes 589832 | tf_op jit(solution)/shard_map/ppermute | solution.py:460
  34.4 6.1 %collective-permute-start.4 = (bf16[4,16,1536]{2,1,0:T(8,128)(2,1)}, bf16[4,16,1536]{2,1,0:T(8,128)(2,1)}, u32[]{:S(2)}, u32[]{:S(2)}) collective-permute-start(bf16[4,16,1536]{2,1,0:T(8,128)(2,1)} %collective-permute-done.3.refs_0_), channel_id=1, source_target_pairs={{0,4},{1,5},{2,6},{3,7},{4,8},{5,9},{6,10},{7,11},{8,12},{9,13},{1... | collective-permute-start | bytes 589832 | tf_op jit(solution)/shard_map/ppermute | solution.py:486
  40.4 39.4 %copy-start = (bf16[3,8,512]{2,1,0:T(8,128)(2,1)S(1)}, bf16[3,8,512]{2,1,0:T(8,128)(2,1)}, u32[]{:S(2)}) copy-start(bf16[3,8,512]{2,1,0:T(8,128)(2,1)} %q_ref.1) | copy-start | bytes 73732
  40.4 39.4 %copy-start.5 = (f32[8,32]{1,0:T(8,128)S(1)}, f32[8,32]{1,0:T(8,128)}, u32[]{:S(2)}) copy-start(f32[8,32]{1,0:T(8,128)} %get-tuple-element.18.owner_ref) | copy-start | bytes 3076
  44.5 17.7 %all-to-all-start.1 = ((bf16[16,16,1664]{2,1,0:T(8,128)(2,1)}), bf16[16,16,1664]{2,1,0:T(8,128)(2,1)S(1)}, u32[]{:S(2)}, u32[]{:S(2)}) async-start(bf16[16,16,1664]{2,1,0:T(8,128)(2,1)} %attend_others.3), calls=%async_computation.1 | async-start | bytes 1703936 | tf_op jit(solution)/shard_map/all_to_all | solution.py:511
  63.7 16.2 %all-to-all-start.2 = ((bf16[16,32,128]{2,1,0:T(8,128)(2,1)}), bf16[16,32,128]{2,1,0:T(8,128)(2,1)S(1)}, u32[]{:S(2)}, u32[]{:S(2)}) async-start(bf16[16,32,128]{2,1,0:T(8,128)(2,1)} %bitcast.6), calls=%async_computation.2 | async-start | bytes 262144 | tf_op jit(solution)/shard_map/all_to_all | solution.py:521

commit v6 on v5

--- a/solution.py
+++ b/solution.py
@@ -474,7 +474,7 @@
             pltpu.VMEM((SIDE, ranges, groups * HEAD_DIM), bf16),
             pltpu.VMEM((2, pages, slice_tokens, pair), bf16),
             pltpu.VMEM((SIDE, ranges, wide), bf16),
-            pltpu.VMEM((size, HEAD_DIM), f32),
+            pltpu.VMEM((size + ranges, HEAD_DIM), f32),
         ]
         + row_scratch
         + [dma((5,))],
@@ -496,7 +496,7 @@
                 pltpu.VMEM((count, SIDE, ranges, groups * HEAD_DIM), bf16),
                 pltpu.VMEM((count, 2, pages, slice_tokens, pair), bf16),
                 pltpu.VMEM((count, SIDE, ranges, wide), bf16),
-                pltpu.VMEM((count * size, HEAD_DIM), f32),
+                pltpu.VMEM((count * size + ranges, HEAD_DIM), f32),
             ]
             + row_scratch
             + [dma((1 + 4 * count,))],

time: 81.6 us -> 81.7 us (level)
  no operation moved by 1% of the time
where the time goes in v6:
time: 81.7 us; the launch traced here: 81 us
  starting transfers between devices  29.6 us (36%)
  waiting for transfers between devices  27.2 us (33%)
  Pallas kernels  20.4 us (25%)
  local copies, waits for them, and re-layouts  3.56 us (4%)
    all_to_all x1, waiting for transfers between devices, on_device(): lax.all_to_all(partial, 'tp', split_axis=0, concat_axis=0, tiled=True)  12.5 us
    all_to_all x1, starting transfers between devices, on_device(): got = lax.all_to_all(sent, 'inst', split_axis=0, concat_axis=0, tiled=True)  9.99 us
    pallas_call x2, Pallas kernels, on_device(): pl.pallas_call(functools.partial(attend_others, groups, list(given)), in_...  9.8 us
    all_to_all x1, waiting for transfers between devices, on_device(): back = lax.all_to_all(lent, 'inst', split_axis=0, concat_axis=0, tiled=True)  8.28 us
    all_to_all x1, starting transfers between devices, on_device(): back = lax.all_to_all(lent, 'inst', split_axis=0, concat_axis=0, tiled=True)  7.12 us
    all_to_all x1, starting transfers between devices, on_device(): lax.all_to_all(partial, 'tp', split_axis=0, concat_axis=0, tiled=True)  5.18 us
    ppermute x3, starting transfers between devices, on_device(): lax.ppermute(own, 'tp', x_shift(k))  4.29 us
    pallas_call x1, Pallas kernels, on_device(): pl.pallas_call(functools.partial(attend_own, groups), in_specs=[hbm] * 3,...  3.88 us
  transfers between devices with their start and end apart: 9, of which 6 were waited for; matrix products, arithmetic and copies ran while one was open for 1% of the time, Pallas kernels for 15%

profile of v6, /device:TPU:1, one launch (start us, length us, event | category | flops | bytes accessed | tf_op | source)
XLA Modules:
  0.0 81.0 jit_solution(489883184054959777)
XLA Ops:
  0.0 1.7 %prepare.1 = (bf16[384,128]{1,0:T(8,128)(2,1)}, f32[8,32]{1,0:T(8,128)}) custom-call(bf16[3,8,512]{2,1,0:T(8,128)(2,1)} %q_ref.1, s32[16,16]{1,0:T(8,128)} %owner_hbm.1), custom_call_target="tpu_custom_call" | custom-call | tf_op jit(solution)/shard_map/prepare/pallas_call | solution.py:416
  1.7 10.0 %all-to-all-start = ((bf16[16,24,128]{2,1,0:T(8,128)(2,1)}), bf16[16,24,128]{2,1,0:T(8,128)(2,1)S(1)}, u32[]{:S(2)}, u32[]{:S(2)}) async-start(bf16[16,24,128]{2,1,0:T(8,128)(2,1)} %bitcast.15), calls=%async_computation | async-start | bytes 196608 | tf_op jit(solution)/shard_map/all_to_all | solution.py:433
  11.7 0.0 copy-start.2
  11.7 0.7 copy-done.2
  12.4 0.0 copy-start.3
  12.4 0.7 copy-done.3
  13.1 0.0 copy-start.4
  13.1 0.7 copy-done.4
  13.8 2.4 %make_plan.1 = (s32[8,16]{1,0:T(8,128)S(1)}, f32[16,32]{1,0:T(8,128)S(1)}, f32[32,16]{1,0:T(8,128)S(1)}) custom-call(s32[16,16]{1,0:T(8,128)S(1)} %copy-done.2, s32[16,16]{1,0:T(8,128)S(1)} %copy-done.3, s32[16,16]{1,0:T(8,128)S(1)} %copy-done.4), custom_call_target="tpu_custom_call" | custom-call | tf_op jit(solution)/shard_map/make_plan/pallas_call | solution.py:435
  16.2 0.0 copy-start.1
  16.2 0.6 copy-done.1
  16.8 3.4 %all-to-all-done = bf16[16,24,128]{2,1,0:T(8,128)(2,1)S(1)} async-done(((bf16[16,24,128]{2,1,0:T(8,128)(2,1)}), bf16[16,24,128]{2,1,0:T(8,128)(2,1)S(1)}, u32[]{:S(2)}, u32[]{:S(2)}) %all-to-all-start) | async-done | bytes 98336 | tf_op jit(solution)/shard_map/all_to_all | solution.py:433
  20.2 0.2 pick_ranges.1
  20.4 1.3 %collective-permute-start = (bf16[16,1536]{1,0:T(8,128)(2,1)S(1)}, bf16[16,1536]{1,0:T(8,128)(2,1)S(1)}, u32[]{:S(2)}, u32[]{:S(2)}) collective-permute-start(bf16[16,1536]{1,0:T(8,128)(2,1)S(1)} %pick_ranges.1), channel_id=1, source_target_pairs={{0,1},{1,2},{2,3},{3,0},{4,5},{5,6},{6,7},{7,4},{8,9},{9,10},{10,1... | collective-permute-start | bytes 147464 | tf_op jit(solution)/shard_map/ppermute | solution.py:459
  21.7 1.5 %collective-permute-start.1 = (bf16[16,1536]{1,0:T(8,128)(2,1)S(1)}, bf16[16,1536]{1,0:T(8,128)(2,1)S(1)}, u32[]{:S(2)}, u32[]{:S(2)}) collective-permute-start(bf16[16,1536]{1,0:T(8,128)(2,1)S(1)} %pick_ranges.1), channel_id=1, source_target_pairs={{0,3},{1,0},{2,1},{3,2},{4,7},{5,4},{6,5},{7,6},{8,11},{9,8},{10,9... | collective-permute-start | bytes 147464 | tf_op jit(solution)/shard_map/ppermute | solution.py:459
  23.1 1.5 %collective-permute-start.2 = (bf16[16,1536]{1,0:T(8,128)(2,1)S(1)}, bf16[16,1536]{1,0:T(8,128)(2,1)S(1)}, u32[]{:S(2)}, u32[]{:S(2)}) collective-permute-start(bf16[16,1536]{1,0:T(8,128)(2,1)S(1)} %pick_ranges.1), channel_id=1, source_target_pairs={{0,2},{1,3},{2,0},{3,1},{4,6},{5,7},{6,4},{7,5},{8,10},{9,11},{10,... | collective-permute-start | bytes 147464 | tf_op jit(solution)/shard_map/ppermute | solution.py:459
  24.7 0.5 collective-permute-done
  25.1 0.0 collective-permute-done.1
  25.1 2.4 %collective-permute-done.2 = bf16[16,1536]{1,0:T(8,128)(2,1)S(1)} collective-permute-done((bf16[16,1536]{1,0:T(8,128)(2,1)S(1)}, bf16[16,1536]{1,0:T(8,128)(2,1)S(1)}, u32[]{:S(2)}, u32[]{:S(2)}) %collective-permute-start.2) | collective-permute-done | bytes 49184 | tf_op jit(solution)/shard_map/ppermute | solution.py:459
  27.6 0.0 copy-start.6
  27.6 1.4 %collective-permute-start.3 = (bf16[4,16,1536]{2,1,0:T(8,128)(2,1)S(1)}, bf16[4,16,1536]{2,1,0:T(8,128)(2,1)}, u32[]{:S(2)}, u32[]{:S(2)}) collective-permute-start(bf16[4,16,1536]{2,1,0:T(8,128)(2,1)S(1)} %pad_maximum_fusion.block), channel_id=1, source_target_pairs={{0,4},{1,5},{2,6},{3,7},{4,8},{5,9},{6,10},{7,11},{8,12},{9,13},{1... | collective-permute-start | bytes 589832 | tf_op jit(solution)/shard_map/ppermute | solution.py:460
  29.0 1.5 %collective-permute-start.5 = (bf16[4,16,1536]{2,1,0:T(8,128)(2,1)S(1)}, bf16[4,16,1536]{2,1,0:T(8,128)(2,1)}, u32[]{:S(2)}, u32[]{:S(2)}) collective-permute-start(bf16[4,16,1536]{2,1,0:T(8,128)(2,1)S(1)} %pad_maximum_fusion.block), channel_id=1, source_target_pairs={{0,12},{1,13},{2,14},{3,15},{4,0},{5,1},{6,2},{7,3},{8,4},{9,5},{1... | collective-permute-start | bytes 589832 | tf_op jit(solution)/shard_map/ppermute | solution.py:460
  30.5 0.0 copy-done.6
  30.5 3.9 %attend_own.1.refs_3_ = bf16[16,16,1664]{2,1,0:T(8,128)(2,1)} custom-call(s32[8,16]{1,0:T(8,128)} %copy-done.1, bf16[4,16,1536]{2,1,0:T(8,128)(2,1)} %copy-done.6, bf16[128,2,16,1024]{3,2,1,0:T(8,128)(2,1)} %refs_1_.1), custom_call_target="tpu_custom_call" | custom-call | flops 1000000000 | bytes 8388608 | tf_op jit(solution)/shard_map/attend_own/pallas_call | solution.py:467
  34.4 0.0 collective-permute-done.3.refs_0_
  34.4 0.1 collective-permute-start.4
  34.5 0.0 collective-permute-done.5.refs_1_
  34.5 5.9 %attend_others.2.refs_2_ = bf16[16,16,1664]{2,1,0:T(8,128)(2,1)} custom-call(s32[8,16]{1,0:T(8,128)} %copy-done.1, bf16[4,16,1536]{2,1,0:T(8,128)(2,1)} %collective-permute-done.3.refs_0_, bf16[4,16,1536]{2,1,0:T(8,128)(2,1)} %collective-permute-done.5.refs_1_, bf16[128,2,16,1024]{3,2,1,0:T(8,128)(2,1)} %refs_1_.1, ...), custom_call_target="tpu_custom_call", output_to_operand_aliasing={{}: (4, {})} | custom-call | flops 2000000000 | bytes 8388608 | tf_op jit(solution)/shard_map/attend_others/pallas_call | solution.py:489
  40.4 0.0 copy-start
  40.5 0.0 copy-start.5
  40.5 0.1 collective-permute-done.4.refs_0_
  40.6 3.9 %attend_others.3 = bf16[16,16,1664]{2,1,0:T(8,128)(2,1)} custom-call(s32[8,16]{1,0:T(8,128)} %copy-done.1, bf16[4,16,1536]{2,1,0:T(8,128)(2,1)} %collective-permute-done.4.refs_0_, bf16[128,2,16,1024]{3,2,1,0:T(8,128)(2,1)} %refs_1_.1, bf16[16,16,1664]{2,1,0:T(8,128)(2,1)} %attend_others.2.refs_2_), custom_call_target="tpu_custom_call", output_to_operand_aliasing={{}: (3, {})} | custom-call | flops 1000000000 | bytes 4194304 | tf_op jit(solution)/shard_map/attend_others/pallas_call | solution.py:489
  44.5 5.2 %all-to-all-start.1 = ((bf16[16,16,1664]{2,1,0:T(8,128)(2,1)}), bf16[16,16,1664]{2,1,0:T(8,128)(2,1)S(1)}, u32[]{:S(2)}, u32[]{:S(2)}) async-start(bf16[16,16,1664]{2,1,0:T(8,128)(2,1)} %attend_others.3), calls=%async_computation.1 | async-start | bytes 1703936 | tf_op jit(solution)/shard_map/all_to_all | solution.py:511
  49.7 12.5 %all-to-all-done.1.in_ref = bf16[16,16,1664]{2,1,0:T(8,128)(2,1)S(1)} async-done(((bf16[16,16,1664]{2,1,0:T(8,128)(2,1)}), bf16[16,16,1664]{2,1,0:T(8,128)(2,1)S(1)}, u32[]{:S(2)}, u32[]{:S(2)}) %all-to-all-start.1) | async-done | bytes 852000 | tf_op jit(solution)/shard_map/all_to_all | solution.py:511
  62.2 1.5 %merge_sources.1 = bf16[512,128]{1,0:T(8,128)(2,1)} custom-call(f32[32,16]{1,0:T(8,128)S(1)} %get-tuple-element.12.put_ref, bf16[16,16,1664]{2,1,0:T(8,128)(2,1)S(1)} %all-to-all-done.1.in_ref), custom_call_target="tpu_custom_call" | custom-call | tf_op jit(solution)/shard_map/merge_sources/pallas_call | solution.py:512
  63.7 7.1 %all-to-all-start.2 = ((bf16[16,32,128]{2,1,0:T(8,128)(2,1)}), bf16[16,32,128]{2,1,0:T(8,128)(2,1)S(1)}, u32[]{:S(2)}, u32[]{:S(2)}) async-start(bf16[16,32,128]{2,1,0:T(8,128)(2,1)} %bitcast.6), calls=%async_computation.2 | async-start | bytes 262144 | tf_op jit(solution)/shard_map/all_to_all | solution.py:521
  70.8 0.9 %constant_dynamic-slice_fusion.1 = (bf16[3,8,1,128]{3,2,1,0:T(2,128)(2,1)S(1)}, bf16[3,8,1,128]{3,2,1,0:T(2,128)(2,1)S(1)}) fusion(bf16[3,8,2,1024]{3,2,1,0:T(2,128)(2,1)} %param.7, s32[]{:T(128)S(6)} %add.5, s32[]{:T(128)S(6)} %select_n.9), kind=kLoop, calls=%fused_computation.4 | loop fusion | bytes 24584 | tf_op jit(solution)/shard_map/slice | solution.py:530
  71.7 8.3 %all-to-all-done.2 = bf16[16,32,128]{2,1,0:T(8,128)(2,1)S(1)} async-done(((bf16[16,32,128]{2,1,0:T(8,128)(2,1)}), bf16[16,32,128]{2,1,0:T(8,128)(2,1)S(1)}, u32[]{:S(2)}, u32[]{:S(2)}) %all-to-all-start.2) | async-done | bytes 131104 | tf_op jit(solution)/shard_map/all_to_all | solution.py:521
  80.0 0.0 copy-done
  80.0 0.0 copy-done.5
  80.0 1.0 %finish.1 = bf16[3,8,512]{2,1,0:T(8,128)(2,1)} custom-call(bf16[512,128]{1,0:T(8,128)(2,1)S(1)} %bitcast.12, f32[8,32]{1,0:T(8,128)S(1)} %copy-done.5, bf16[3,8,512]{2,1,0:T(8,128)(2,1)S(1)} %copy-done, bf16[3,8,128]{2,1,0:T(8,128)(2,1)S(1)} %get-tuple-element.22.k_ref, bf16[3,8,128]{2,1,0:T(8,128)(2,1)S(1)} %get-tuple-element.21.v_ref), custom_call_target="tpu_custom_call" | custom-call | tf_op jit(solution)/shard_map/finish/pallas_call | solution.py:522
  (2 shorter events, 0.0 us)
Async XLA Ops:
  1.7 18.5 %all-to-all-start = ((bf16[16,24,128]{2,1,0:T(8,128)(2,1)}), bf16[16,24,128]{2,1,0:T(8,128)(2,1)S(1)}, u32[]{:S(2)}, u32[]{:S(2)}) async-start(bf16[16,24,128]{2,1,0:T(8,128)(2,1)} %bitcast.15), calls=%async_computation | async-start | bytes 196608 | tf_op jit(solution)/shard_map/all_to_all | solution.py:433
  11.7 0.7 copy-start.2
  12.4 0.7 copy-start.3
  13.1 0.7 copy-start.4
  16.2 0.6 copy-start.1
  20.4 4.7 %collective-permute-start = (bf16[16,1536]{1,0:T(8,128)(2,1)S(1)}, bf16[16,1536]{1,0:T(8,128)(2,1)S(1)}, u32[]{:S(2)}, u32[]{:S(2)}) collective-permute-start(bf16[16,1536]{1,0:T(8,128)(2,1)S(1)} %pick_ranges.1), channel_id=1, source_target_pairs={{0,1},{1,2},{2,3},{3,0},{4,5},{5,6},{6,7},{7,4},{8,9},{9,10},{10,1... | collective-permute-start | bytes 147464 | tf_op jit(solution)/shard_map/ppermute | solution.py:459
  21.7 3.5 %collective-permute-start.1 = (bf16[16,1536]{1,0:T(8,128)(2,1)S(1)}, bf16[16,1536]{1,0:T(8,128)(2,1)S(1)}, u32[]{:S(2)}, u32[]{:S(2)}) collective-permute-start(bf16[16,1536]{1,0:T(8,128)(2,1)S(1)} %pick_ranges.1), channel_id=1, source_target_pairs={{0,3},{1,0},{2,1},{3,2},{4,7},{5,4},{6,5},{7,6},{8,11},{9,8},{10,9... | collective-permute-start | bytes 147464 | tf_op jit(solution)/shard_map/ppermute | solution.py:459
  23.1 4.4 %collective-permute-start.2 = (bf16[16,1536]{1,0:T(8,128)(2,1)S(1)}, bf16[16,1536]{1,0:T(8,128)(2,1)S(1)}, u32[]{:S(2)}, u32[]{:S(2)}) collective-permute-start(bf16[16,1536]{1,0:T(8,128)(2,1)S(1)} %pick_ranges.1), channel_id=1, source_target_pairs={{0,2},{1,3},{2,0},{3,1},{4,6},{5,7},{6,4},{7,5},{8,10},{9,11},{10,... | collective-permute-start | bytes 147464 | tf_op jit(solution)/shard_map/ppermute | solution.py:459
  27.6 2.9 %copy-start.6 = (bf16[4,16,1536]{2,1,0:T(8,128)(2,1)}, bf16[4,16,1536]{2,1,0:T(8,128)(2,1)S(1)}, u32[]{:S(2)}) copy-start(bf16[4,16,1536]{2,1,0:T(8,128)(2,1)S(1)} %pad_maximum_fusion.block) | copy-start | bytes 589828
  27.6 6.8 %collective-permute-start.3 = (bf16[4,16,1536]{2,1,0:T(8,128)(2,1)S(1)}, bf16[4,16,1536]{2,1,0:T(8,128)(2,1)}, u32[]{:S(2)}, u32[]{:S(2)}) collective-permute-start(bf16[4,16,1536]{2,1,0:T(8,128)(2,1)S(1)} %pad_maximum_fusion.block), channel_id=1, source_target_pairs={{0,4},{1,5},{2,6},{3,7},{4,8},{5,9},{6,10},{7,11},{8,12},{9,13},{1... | collective-permute-start | bytes 589832 | tf_op jit(solution)/shard_map/ppermute | solution.py:460
  29.0 5.5 %collective-permute-start.5 = (bf16[4,16,1536]{2,1,0:T(8,128)(2,1)S(1)}, bf16[4,16,1536]{2,1,0:T(8,128)(2,1)}, u32[]{:S(2)}, u32[]{:S(2)}) collective-permute-start(bf16[4,16,1536]{2,1,0:T(8,128)(2,1)S(1)} %pad_maximum_fusion.block), channel_id=1, source_target_pairs={{0,12},{1,13},{2,14},{3,15},{4,0},{5,1},{6,2},{7,3},{8,4},{9,5},{1... | collective-permute-start | bytes 589832 | tf_op jit(solution)/shard_map/ppermute | solution.py:460
  34.4 6.1 %collective-permute-start.4 = (bf16[4,16,1536]{2,1,0:T(8,128)(2,1)}, bf16[4,16,1536]{2,1,0:T(8,128)(2,1)}, u32[]{:S(2)}, u32[]{:S(2)}) collective-permute-start(bf16[4,16,1536]{2,1,0:T(8,128)(2,1)} %collective-permute-done.3.refs_0_), channel_id=1, source_target_pairs={{0,4},{1,5},{2,6},{3,7},{4,8},{5,9},{6,10},{7,11},{8,12},{9,13},{1... | collective-permute-start | bytes 589832 | tf_op jit(solution)/shard_map/ppermute | solution.py:486
  40.4 39.5 %copy-start = (bf16[3,8,512]{2,1,0:T(8,128)(2,1)S(1)}, bf16[3,8,512]{2,1,0:T(8,128)(2,1)}, u32[]{:S(2)}) copy-start(bf16[3,8,512]{2,1,0:T(8,128)(2,1)} %q_ref.1) | copy-start | bytes 73732
  40.5 39.5 %copy-start.5 = (f32[8,32]{1,0:T(8,128)S(1)}, f32[8,32]{1,0:T(8,128)}, u32[]{:S(2)}) copy-start(f32[8,32]{1,0:T(8,128)} %get-tuple-element.18.owner_ref) | copy-start | bytes 3076
  44.5 17.7 %all-to-all-start.1 = ((bf16[16,16,1664]{2,1,0:T(8,128)(2,1)}), bf16[16,16,1664]{2,1,0:T(8,128)(2,1)S(1)}, u32[]{:S(2)}, u32[]{:S(2)}) async-start(bf16[16,16,1664]{2,1,0:T(8,128)(2,1)} %attend_others.3), calls=%async_computation.1 | async-start | bytes 1703936 | tf_op jit(solution)/shard_map/all_to_all | solution.py:511
  63.7 16.3 %all-to-all-start.2 = ((bf16[16,32,128]{2,1,0:T(8,128)(2,1)}), bf16[16,32,128]{2,1,0:T(8,128)(2,1)S(1)}, u32[]{:S(2)}, u32[]{:S(2)}) async-start(bf16[16,32,128]{2,1,0:T(8,128)(2,1)} %bitcast.6), calls=%async_computation.2 | async-start | bytes 262144 | tf_op jit(solution)/shard_map/all_to_all | solution.py:521

commit v7 on v6

--- a/solution.py
+++ b/solution.py
@@ -48,7 +48,20 @@
     )
 
 
-def prepare(q_hbm, owner_hbm, sent_ref, mine_ref, q_ref, owner_ref, stage, sems):
+def slot_owners(owner):
+    lenders, ranges = owner.shape
+    hit = owner // REQ_INST == lax.axis_index("inst")
+    earlier = (iota((ranges, ranges), 0) < iota((ranges, ranges), 1)).astype(f32)
+    rank = jnp.dot(hit.astype(f32), earlier, preferred_element_type=f32)
+    local = (owner % REQ_INST + 1).astype(f32)
+    owners = []
+    for c in range(CAP):
+        chosen = jnp.where(hit & (jnp.abs(rank - c) < 0.5), local, 0.0)
+        owners.append(jnp.sum(chosen, axis=1, keepdims=True) - 1.0)
+    return owners
+
+
+def prepare(q_hbm, owner_hbm, sent_ref, q_ref, owner_ref, stage, sems):
     copies = [
         pltpu.make_async_copy(owner_hbm, owner_ref, sems.at[0]),
         pltpu.make_async_copy(q_hbm, q_ref, sems.at[1]),
@@ -59,16 +72,8 @@
     heads = columns // HEAD_DIM
     groups = steps * heads
     lenders, ranges = owner_ref.shape
-    earlier = (iota((ranges, ranges), 0) < iota((ranges, ranges), 1)).astype(f32)
     copies[0].wait()
-    owner = owner_ref[...]
-    hit = owner // REQ_INST == lax.axis_index("inst")
-    rank = jnp.dot(hit.astype(f32), earlier, preferred_element_type=f32)
-    local = (owner % REQ_INST + 1).astype(f32)
-    owners = []
-    for c in range(CAP):
-        chosen = jnp.where(hit & (jnp.abs(rank - c) < 0.5), local, 0.0)
-        owners.append(jnp.sum(chosen, axis=1, keepdims=True) - 1.0)
+    owners = slot_owners(owner_ref[...])
     copies[1].wait()
     for c in range(CAP):
         pick = (owners[c].astype(jnp.int32) == iota((lenders, requests), 1)).astype(f32)
@@ -78,8 +83,6 @@
                 at = pl.ds(c * groups + s * heads + h, lenders, stride=CAP * groups)
                 stage[at, :] = value[:, h * HEAD_DIM : (h + 1) * HEAD_DIM]
     sent_ref[...] = stage[...].astype(bf16)
-    spread = [jnp.broadcast_to(mine, (lenders, HEAD_DIM)) for mine in owners]
-    mine_ref[...] = jnp.transpose(jnp.concatenate(spread, axis=0), (1, 0))[: mine_ref.shape[0], :]
 
 
 def make_plan(slice_tokens, pages, owner_ref, start_ref, tokens_ref, plan, pick_ref, put_ref):
@@ -345,6 +348,12 @@
     out_ref[...] = stage[...].astype(bf16)
 
 
+def slot_table(owner_ref, mine_ref):
+    lenders = owner_ref.shape[0]
+    spread = [jnp.broadcast_to(mine, (lenders, HEAD_DIM)) for mine in slot_owners(owner_ref[...])]
+    mine_ref[...] = jnp.transpose(jnp.concatenate(spread, axis=0), (1, 0))[: mine_ref.shape[0], :]
+
+
 def finish(steps, heads, in_ref, owner_ref, q_ref, k_ref, v_ref, out_ref, stage):
     groups = steps * heads
     lenders = in_ref.shape[0] // (CAP * PAD)
@@ -413,14 +422,11 @@
     whole = pltpu.CompilerParams(vmem_limit_bytes=64 * 2**20 - 2**17)
     dma = pltpu.SemaphoreType.DMA
 
-    sent, slot_owner = pl.pallas_call(
+    sent = pl.pallas_call(
         prepare,
         in_specs=[hbm] * 2,
-        out_specs=[vmem] * 2,
-        out_shape=[
-            jax.ShapeDtypeStruct((slots * groups, HEAD_DIM), bf16),
-            jax.ShapeDtypeStruct((requests, slots), f32),
-        ],
+        out_specs=vmem,
+        out_shape=jax.ShapeDtypeStruct((slots * groups, HEAD_DIM), bf16),
         scratch_shapes=[
             pltpu.VMEM(queries.shape, bf16),
             pltpu.VMEM(range_owner.shape, jnp.int32),
@@ -444,9 +450,6 @@
         compiler_params=params,
         name="make_plan",
     )(range_owner, range_start, range_tokens)
-    head = my_tp * heads // group_size
-    fresh = lax.dynamic_slice_in_dim(new_kv, head * HEAD_DIM, HEAD_DIM, axis=3)
-
     own = pl.pallas_call(
         functools.partial(pick_ranges, groups),
         in_specs=[vmem] * 2,
@@ -519,6 +522,17 @@
         name="merge_sources",
     )(put, parts)
     back = lax.all_to_all(lent, "inst", split_axis=0, concat_axis=0, tiled=True)
+    lent, new_kv, owners = lax.optimization_barrier((lent, new_kv, range_owner))
+    head = my_tp * heads // group_size
+    fresh = lax.dynamic_slice_in_dim(new_kv, head * HEAD_DIM, HEAD_DIM, axis=3)
+    slot_owner = pl.pallas_call(
+        slot_table,
+        in_specs=[vmem],
+        out_specs=vmem,
+        out_shape=jax.ShapeDtypeStruct((requests, slots), f32),
+        compiler_params=params,
+        name="slot_table",
+    )(owners)
     return pl.pallas_call(
         functools.partial(finish, steps, heads),
         in_specs=[vmem] * 5,

time: 81.7 us -> 81.5 us (level)
  blocking collectives: 0 us -> 17.8 us
  waiting for transfers between devices: 27.2 us -> 14.4 us
  starting transfers between devices: 29.6 us -> 24.2 us
    all_to_all x0 -> x1, blocking collectives: none -> 17.8 us  [on_device(): lax.all_to_all(partial, 'tp', split_axis=0, concat_axis=0, tiled=True)]
    all_to_all x1 -> x0, waiting for transfers between devices: 12.5 us -> none  [on_device(): lax.all_to_all(partial, 'tp', split_axis=0, concat_axis=0, tiled=True)]
    all_to_all x1 -> x0, starting transfers between devices: 5.18 us -> none  [on_device(): lax.all_to_all(partial, 'tp', split_axis=0, concat_axis=0, tiled=True)]
    optimization_barrier x0 -> x1, local copies, waits for them, and re-layouts: none -> 0.91 us  [on_device(): lent, new_kv, owners = lax.optimization_barrier((lent, new_kv, range_owner))]
    slice x1 -> x0, local copies, waits for them, and re-layouts: 0.87 us -> none  [on_device(): fresh[:, :, 1]]
    pallas_call x1 -> x2, Pallas kernels: 1.73 us -> 2 us  [the longest x1 1.73 us: on_device(): pl.pallas_call(prepare, in_specs=[hbm] * 2, out_specs=vmem, out_shape=jax...]
  transfers between devices with their start and end apart: 9 -> 8, of which waited for: 6 -> 5; matrix products, arithmetic and copies ran while one was open for 1% -> 1% of each run, Pallas kernels for 15% -> 15%
where the time goes in v7:
time: 81.5 us; the launch traced here: 80.9 us
  starting transfers between devices  24.2 us (30%)
  Pallas kernels  20.7 us (25%)
  blocking collectives  17.8 us (22%)
  waiting for transfers between devices  14.4 us (18%)
  local copies, waits for them, and re-layouts  3.6 us (4%)
    all_to_all x1, blocking collectives, on_device(): lax.all_to_all(partial, 'tp', split_axis=0, concat_axis=0, tiled=True)  17.8 us
    all_to_all x1, starting transfers between devices, on_device(): got = lax.all_to_all(sent, 'inst', split_axis=0, concat_axis=0, tiled=True)  9.99 us
    pallas_call x2, Pallas kernels, on_device(): pl.pallas_call(functools.partial(attend_others, groups, list(given)), in_...  9.8 us
    all_to_all x1, waiting for transfers between devices, on_device(): back = lax.all_to_all(lent, 'inst', split_axis=0, concat_axis=0, tiled=True)  7.97 us
    all_to_all x1, starting transfers between devices, on_device(): back = lax.all_to_all(lent, 'inst', split_axis=0, concat_axis=0, tiled=True)  6.94 us
    ppermute x3, starting transfers between devices, on_device(): lax.ppermute(own, 'tp', x_shift(k))  4.29 us
    pallas_call x1, Pallas kernels, on_device(): pl.pallas_call(functools.partial(attend_own, groups), in_specs=[hbm] * 3,...  3.9 us
    all_to_all x1, waiting for transfers between devices, on_device(): got = lax.all_to_all(sent, 'inst', split_axis=0, concat_axis=0, tiled=True)  3.43 us
  transfers between devices with their start and end apart: 8, of which 5 were waited for; matrix products, arithmetic and copies ran while one was open for 1% of the time, Pallas kernels for 15%

profile of v7, /device:TPU:1, one launch (start us, length us, event | category | flops | bytes accessed | tf_op | source)
XLA Modules:
  0.0 80.9 jit_solution(9755257460165733091)
XLA Ops:
  0.0 1.7 %prepare.1 = bf16[384,128]{1,0:T(8,128)(2,1)} custom-call(bf16[3,8,512]{2,1,0:T(8,128)(2,1)} %q_ref.1, s32[16,16]{1,0:T(8,128)} %owner_ref.2), custom_call_target="tpu_custom_call" | custom-call | tf_op jit(solution)/shard_map/prepare/pallas_call | solution.py:425
  1.7 10.0 %all-to-all-start = ((bf16[16,24,128]{2,1,0:T(8,128)(2,1)}), bf16[16,24,128]{2,1,0:T(8,128)(2,1)S(1)}, u32[]{:S(2)}, u32[]{:S(2)}) async-start(bf16[16,24,128]{2,1,0:T(8,128)(2,1)} %bitcast.15), calls=%async_computation | async-start | bytes 196608 | tf_op jit(solution)/shard_map/all_to_all | solution.py:439
  11.7 0.0 copy-start.1
  11.7 0.7 copy-done.1
  12.4 0.0 copy-start.4
  12.4 0.7 copy-done.4
  13.1 0.0 copy-start.5
  13.1 0.7 copy-done.5
  13.8 2.4 %make_plan.1 = (s32[8,16]{1,0:T(8,128)S(1)}, f32[16,32]{1,0:T(8,128)S(1)}, f32[32,16]{1,0:T(8,128)S(1)}) custom-call(s32[16,16]{1,0:T(8,128)S(1)} %copy-done.1, s32[16,16]{1,0:T(8,128)S(1)} %copy-done.4, s32[16,16]{1,0:T(8,128)S(1)} %copy-done.5), custom_call_target="tpu_custom_call" | custom-call | tf_op jit(solution)/shard_map/make_plan/pallas_call | solution.py:441
  16.2 0.0 copy-start.3
  16.2 0.6 copy-done.3
  16.8 3.4 %all-to-all-done = bf16[16,24,128]{2,1,0:T(8,128)(2,1)S(1)} async-done(((bf16[16,24,128]{2,1,0:T(8,128)(2,1)}), bf16[16,24,128]{2,1,0:T(8,128)(2,1)S(1)}, u32[]{:S(2)}, u32[]{:S(2)}) %all-to-all-start) | async-done | bytes 98336 | tf_op jit(solution)/shard_map/all_to_all | solution.py:439
  20.2 0.2 pick_ranges.1
  20.4 1.3 %collective-permute-start = (bf16[16,1536]{1,0:T(8,128)(2,1)S(1)}, bf16[16,1536]{1,0:T(8,128)(2,1)S(1)}, u32[]{:S(2)}, u32[]{:S(2)}) collective-permute-start(bf16[16,1536]{1,0:T(8,128)(2,1)S(1)} %pick_ranges.1), channel_id=1, source_target_pairs={{0,1},{1,2},{2,3},{3,0},{4,5},{5,6},{6,7},{7,4},{8,9},{9,10},{10,1... | collective-permute-start | bytes 147464 | tf_op jit(solution)/shard_map/ppermute | solution.py:462
  21.7 1.5 %collective-permute-start.1 = (bf16[16,1536]{1,0:T(8,128)(2,1)S(1)}, bf16[16,1536]{1,0:T(8,128)(2,1)S(1)}, u32[]{:S(2)}, u32[]{:S(2)}) collective-permute-start(bf16[16,1536]{1,0:T(8,128)(2,1)S(1)} %pick_ranges.1), channel_id=1, source_target_pairs={{0,3},{1,0},{2,1},{3,2},{4,7},{5,4},{6,5},{7,6},{8,11},{9,8},{10,9... | collective-permute-start | bytes 147464 | tf_op jit(solution)/shard_map/ppermute | solution.py:462
  23.1 1.5 %collective-permute-start.2 = (bf16[16,1536]{1,0:T(8,128)(2,1)S(1)}, bf16[16,1536]{1,0:T(8,128)(2,1)S(1)}, u32[]{:S(2)}, u32[]{:S(2)}) collective-permute-start(bf16[16,1536]{1,0:T(8,128)(2,1)S(1)} %pick_ranges.1), channel_id=1, source_target_pairs={{0,2},{1,3},{2,0},{3,1},{4,6},{5,7},{6,4},{7,5},{8,10},{9,11},{10,... | collective-permute-start | bytes 147464 | tf_op jit(solution)/shard_map/ppermute | solution.py:462
  24.7 0.5 collective-permute-done
  25.1 0.0 collective-permute-done.1
  25.1 2.4 %collective-permute-done.2 = bf16[16,1536]{1,0:T(8,128)(2,1)S(1)} collective-permute-done((bf16[16,1536]{1,0:T(8,128)(2,1)S(1)}, bf16[16,1536]{1,0:T(8,128)(2,1)S(1)}, u32[]{:S(2)}, u32[]{:S(2)}) %collective-permute-start.2) | collective-permute-done | bytes 49184 | tf_op jit(solution)/shard_map/ppermute | solution.py:462
  27.6 0.0 copy-start.6
  27.6 1.4 %collective-permute-start.3 = (bf16[4,16,1536]{2,1,0:T(8,128)(2,1)S(1)}, bf16[4,16,1536]{2,1,0:T(8,128)(2,1)}, u32[]{:S(2)}, u32[]{:S(2)}) collective-permute-start(bf16[4,16,1536]{2,1,0:T(8,128)(2,1)S(1)} %pad_maximum_fusion.block), channel_id=1, source_target_pairs={{0,4},{1,5},{2,6},{3,7},{4,8},{5,9},{6,10},{7,11},{8,12},{9,13},{1... | collective-permute-start | bytes 589832 | tf_op jit(solution)/shard_map/ppermute | solution.py:463
  29.0 1.5 %collective-permute-start.5 = (bf16[4,16,1536]{2,1,0:T(8,128)(2,1)S(1)}, bf16[4,16,1536]{2,1,0:T(8,128)(2,1)}, u32[]{:S(2)}, u32[]{:S(2)}) collective-permute-start(bf16[4,16,1536]{2,1,0:T(8,128)(2,1)S(1)} %pad_maximum_fusion.block), channel_id=1, source_target_pairs={{0,12},{1,13},{2,14},{3,15},{4,0},{5,1},{6,2},{7,3},{8,4},{9,5},{1... | collective-permute-start | bytes 589832 | tf_op jit(solution)/shard_map/ppermute | solution.py:463
  30.5 0.0 copy-done.6
  30.5 3.9 %attend_own.1.refs_3_ = bf16[16,16,1664]{2,1,0:T(8,128)(2,1)} custom-call(s32[8,16]{1,0:T(8,128)} %copy-done.3, bf16[4,16,1536]{2,1,0:T(8,128)(2,1)} %copy-done.6, bf16[128,2,16,1024]{3,2,1,0:T(8,128)(2,1)} %refs_1_.1), custom_call_target="tpu_custom_call" | custom-call | flops 1000000000 | bytes 8388608 | tf_op jit(solution)/shard_map/attend_own/pallas_call | solution.py:470
  34.4 0.0 collective-permute-done.3.refs_0_
  34.4 0.1 collective-permute-start.4
  34.5 0.0 collective-permute-done.5.refs_1_
  34.6 5.9 %attend_others.2.refs_2_ = bf16[16,16,1664]{2,1,0:T(8,128)(2,1)} custom-call(s32[8,16]{1,0:T(8,128)} %copy-done.3, bf16[4,16,1536]{2,1,0:T(8,128)(2,1)} %collective-permute-done.3.refs_0_, bf16[4,16,1536]{2,1,0:T(8,128)(2,1)} %collective-permute-done.5.refs_1_, bf16[128,2,16,1024]{3,2,1,0:T(8,128)(2,1)} %refs_1_.1, ...), custom_call_target="tpu_custom_call", output_to_operand_aliasing={{}: (4, {})} | custom-call | flops 2000000000 | bytes 8388608 | tf_op jit(solution)/shard_map/attend_others/pallas_call | solution.py:492
  40.5 0.0 copy-start.2
  40.5 0.0 copy-start
  40.5 0.1 collective-permute-done.4.refs_0_
  40.6 3.9 %attend_others.3 = bf16[16,16,1664]{2,1,0:T(8,128)(2,1)} custom-call(s32[8,16]{1,0:T(8,128)} %copy-done.3, bf16[4,16,1536]{2,1,0:T(8,128)(2,1)} %collective-permute-done.4.refs_0_, bf16[128,2,16,1024]{3,2,1,0:T(8,128)(2,1)} %refs_1_.1, bf16[16,16,1664]{2,1,0:T(8,128)(2,1)} %attend_others.2.refs_2_), custom_call_target="tpu_custom_call", output_to_operand_aliasing={{}: (3, {})} | custom-call | flops 1000000000 | bytes 4194304 | tf_op jit(solution)/shard_map/attend_others/pallas_call | solution.py:492
  44.5 17.8 %all_to_all.27.in_ref = bf16[16,16,1664]{2,1,0:T(8,128)(2,1)S(1)} all-to-all(bf16[16,16,1664]{2,1,0:T(8,128)(2,1)} %attend_others.3), channel_id=1, replica_groups=mesh['inst'=16,'tp'=16] {'tp'}, dimensions={0} | all-to-all | bytes 1703936 | tf_op jit(solution)/shard_map/all_to_all | solution.py:514
  62.3 1.5 %merge_sources.1 = bf16[512,128]{1,0:T(8,128)(2,1)} custom-call(f32[32,16]{1,0:T(8,128)S(1)} %get-tuple-element.12.put_ref, bf16[16,16,1664]{2,1,0:T(8,128)(2,1)S(1)} %all_to_all.27.in_ref), custom_call_target="tpu_custom_call" | custom-call | tf_op jit(solution)/shard_map/merge_sources/pallas_call | solution.py:515
  63.8 6.9 %all-to-all-start.2 = ((bf16[16,32,128]{2,1,0:T(8,128)(2,1)}), bf16[16,32,128]{2,1,0:T(8,128)(2,1)S(1)}, u32[]{:S(2)}, u32[]{:S(2)}) async-start(bf16[16,32,128]{2,1,0:T(8,128)(2,1)} %bitcast.6), calls=%async_computation.2 | async-start | bytes 262144 | tf_op jit(solution)/shard_map/all_to_all | solution.py:524
  70.7 0.9 %copy.9 = bf16[3,8,2,1024]{3,1,0,2:T(8,128)(2,1)S(1)} copy(bf16[3,8,2,1024]{3,2,1,0:T(2,128)(2,1)} %param.7) | data formatting | bytes 196608 | tf_op jit(solution)/shard_map/optimization_barrier | solution.py:525
  71.6 0.0 copy-done.2
  71.6 0.3 slot_table.1.owner_ref
  71.9 8.0 %all-to-all-done.2 = bf16[16,32,128]{2,1,0:T(8,128)(2,1)S(1)} async-done(((bf16[16,32,128]{2,1,0:T(8,128)(2,1)}), bf16[16,32,128]{2,1,0:T(8,128)(2,1)S(1)}, u32[]{:S(2)}, u32[]{:S(2)}) %all-to-all-start.2) | async-done | bytes 131104 | tf_op jit(solution)/shard_map/all_to_all | solution.py:524
  79.9 0.0 copy-done
  79.9 1.0 %finish.1 = bf16[3,8,512]{2,1,0:T(8,128)(2,1)} custom-call(bf16[512,128]{1,0:T(8,128)(2,1)S(1)} %bitcast.12, f32[8,32]{1,0:T(8,128)S(1)} %slot_table.1.owner_ref, bf16[3,8,512]{2,1,0:T(8,128)(2,1)S(1)} %copy-done, bf16[3,8,128]{2,1,0:T(8,128)(2,1)S(1)} %get-tuple-element.20.k_ref, bf16[3,8,128]{2,1,0:T(8,128)(2,1)S(1)} %get-tuple-element.19.v_ref), custom_call_target="tpu_custom_call" | custom-call | tf_op jit(solution)/shard_map/finish/pallas_call | solution.py:536
  (2 shorter events, 0.0 us)
Async XLA Ops:
  1.7 18.5 %all-to-all-start = ((bf16[16,24,128]{2,1,0:T(8,128)(2,1)}), bf16[16,24,128]{2,1,0:T(8,128)(2,1)S(1)}, u32[]{:S(2)}, u32[]{:S(2)}) async-start(bf16[16,24,128]{2,1,0:T(8,128)(2,1)} %bitcast.15), calls=%async_computation | async-start | bytes 196608 | tf_op jit(solution)/shard_map/all_to_all | solution.py:439
  11.7 0.7 copy-start.1
  12.4 0.7 copy-start.4
  13.1 0.7 copy-start.5
  16.2 0.6 copy-start.3
  20.4 4.7 %collective-permute-start = (bf16[16,1536]{1,0:T(8,128)(2,1)S(1)}, bf16[16,1536]{1,0:T(8,128)(2,1)S(1)}, u32[]{:S(2)}, u32[]{:S(2)}) collective-permute-start(bf16[16,1536]{1,0:T(8,128)(2,1)S(1)} %pick_ranges.1), channel_id=1, source_target_pairs={{0,1},{1,2},{2,3},{3,0},{4,5},{5,6},{6,7},{7,4},{8,9},{9,10},{10,1... | collective-permute-start | bytes 147464 | tf_op jit(solution)/shard_map/ppermute | solution.py:462
  21.7 3.5 %collective-permute-start.1 = (bf16[16,1536]{1,0:T(8,128)(2,1)S(1)}, bf16[16,1536]{1,0:T(8,128)(2,1)S(1)}, u32[]{:S(2)}, u32[]{:S(2)}) collective-permute-start(bf16[16,1536]{1,0:T(8,128)(2,1)S(1)} %pick_ranges.1), channel_id=1, source_target_pairs={{0,3},{1,0},{2,1},{3,2},{4,7},{5,4},{6,5},{7,6},{8,11},{9,8},{10,9... | collective-permute-start | bytes 147464 | tf_op jit(solution)/shard_map/ppermute | solution.py:462
  23.1 4.4 %collective-permute-start.2 = (bf16[16,1536]{1,0:T(8,128)(2,1)S(1)}, bf16[16,1536]{1,0:T(8,128)(2,1)S(1)}, u32[]{:S(2)}, u32[]{:S(2)}) collective-permute-start(bf16[16,1536]{1,0:T(8,128)(2,1)S(1)} %pick_ranges.1), channel_id=1, source_target_pairs={{0,2},{1,3},{2,0},{3,1},{4,6},{5,7},{6,4},{7,5},{8,10},{9,11},{10,... | collective-permute-start | bytes 147464 | tf_op jit(solution)/shard_map/ppermute | solution.py:462
  27.6 2.9 %copy-start.6 = (bf16[4,16,1536]{2,1,0:T(8,128)(2,1)}, bf16[4,16,1536]{2,1,0:T(8,128)(2,1)S(1)}, u32[]{:S(2)}) copy-start(bf16[4,16,1536]{2,1,0:T(8,128)(2,1)S(1)} %pad_maximum_fusion.block) | copy-start | bytes 589828
  27.6 6.8 %collective-permute-start.3 = (bf16[4,16,1536]{2,1,0:T(8,128)(2,1)S(1)}, bf16[4,16,1536]{2,1,0:T(8,128)(2,1)}, u32[]{:S(2)}, u32[]{:S(2)}) collective-permute-start(bf16[4,16,1536]{2,1,0:T(8,128)(2,1)S(1)} %pad_maximum_fusion.block), channel_id=1, source_target_pairs={{0,4},{1,5},{2,6},{3,7},{4,8},{5,9},{6,10},{7,11},{8,12},{9,13},{1... | collective-permute-start | bytes 589832 | tf_op jit(solution)/shard_map/ppermute | solution.py:463
  29.0 5.5 %collective-permute-start.5 = (bf16[4,16,1536]{2,1,0:T(8,128)(2,1)S(1)}, bf16[4,16,1536]{2,1,0:T(8,128)(2,1)}, u32[]{:S(2)}, u32[]{:S(2)}) collective-permute-start(bf16[4,16,1536]{2,1,0:T(8,128)(2,1)S(1)} %pad_maximum_fusion.block), channel_id=1, source_target_pairs={{0,12},{1,13},{2,14},{3,15},{4,0},{5,1},{6,2},{7,3},{8,4},{9,5},{1... | collective-permute-start | bytes 589832 | tf_op jit(solution)/shard_map/ppermute | solution.py:463
  34.4 6.1 %collective-permute-start.4 = (bf16[4,16,1536]{2,1,0:T(8,128)(2,1)}, bf16[4,16,1536]{2,1,0:T(8,128)(2,1)}, u32[]{:S(2)}, u32[]{:S(2)}) collective-permute-start(bf16[4,16,1536]{2,1,0:T(8,128)(2,1)} %collective-permute-done.3.refs_0_), channel_id=1, source_target_pairs={{0,4},{1,5},{2,6},{3,7},{4,8},{5,9},{6,10},{7,11},{8,12},{9,13},{1... | collective-permute-start | bytes 589832 | tf_op jit(solution)/shard_map/ppermute | solution.py:489
  40.5 31.1 %copy-start.2 = (s32[16,16]{1,0:T(8,128)S(1)}, s32[16,16]{1,0:T(8,128)}, u32[]{:S(2)}) copy-start(s32[16,16]{1,0:T(8,128)} %owner_ref.2) | copy-start | bytes 3076
  40.5 39.4 %copy-start = (bf16[3,8,512]{2,1,0:T(8,128)(2,1)S(1)}, bf16[3,8,512]{2,1,0:T(8,128)(2,1)}, u32[]{:S(2)}) copy-start(bf16[3,8,512]{2,1,0:T(8,128)(2,1)} %q_ref.1) | copy-start | bytes 73732
  63.8 16.1 %all-to-all-start.2 = ((bf16[16,32,128]{2,1,0:T(8,128)(2,1)}), bf16[16,32,128]{2,1,0:T(8,128)(2,1)S(1)}, u32[]{:S(2)}, u32[]{:S(2)}) async-start(bf16[16,32,128]{2,1,0:T(8,128)(2,1)} %bitcast.6), calls=%async_computation.2 | async-start | bytes 262144 | tf_op jit(solution)/shard_map/all_to_all | solution.py:524

commit v8 on v6

--- a/solution.py
+++ b/solution.py
@@ -456,7 +456,8 @@
         compiler_params=params,
         name="pick_ranges",
     )(pick, got)
-    block = jnp.stack([own] + [lax.ppermute(own, "tp", x_shift(k)) for k in SHIFTS])
+    before, after = (lax.ppermute(own, "tp", x_shift(k)) for k in (1, SIDE - 1))
+    block = jnp.stack([own, before, after, lax.ppermute(before, "tp", x_shift(1))])
     near = {k: lax.ppermute(block, "tp", y_shift(k)) for k in (1, SIDE - 1)}
 
     pair = 2 * HEAD_DIM

time: 81.7 us -> 82 us (level)
  waiting for transfers between devices: 27.2 us -> 30.2 us
  starting transfers between devices: 29.6 us -> 27 us
    ppermute x3, waiting for transfers between devices: 2.91 us -> 6.14 us  [the longest x1 4.14 us: on_device(): lax.ppermute(before, 'tp', x_shift(1))]
    ppermute x3, starting transfers between devices: 4.29 us -> 2.76 us  [the longest x2 2.75 us: on_device(): before, after = (lax.ppermute(own, 'tp', x_shift(k)) for k in (1, SIDE - 1))]
    all_to_all x1, starting transfers between devices: 5.18 us -> 3.98 us  [on_device(): lax.all_to_all(partial, 'tp', split_axis=0, concat_axis=0, tiled=True)]
where the time goes in v8:
time: 82 us; the launch traced here: 81.4 us
  waiting for transfers between devices  30.2 us (37%)
  starting transfers between devices  27 us (33%)
  Pallas kernels  20.5 us (25%)
  local copies, waits for them, and re-layouts  3.56 us (4%)
    all_to_all x1, waiting for transfers between devices, on_device(): lax.all_to_all(partial, 'tp', split_axis=0, concat_axis=0, tiled=True)  12.2 us
    all_to_all x1, starting transfers between devices, on_device(): got = lax.all_to_all(sent, 'inst', split_axis=0, concat_axis=0, tiled=True)  9.99 us
    pallas_call x2, Pallas kernels, on_device(): pl.pallas_call(functools.partial(attend_others, groups, list(given)), in_...  9.81 us
    all_to_all x1, waiting for transfers between devices, on_device(): back = lax.all_to_all(lent, 'inst', split_axis=0, concat_axis=0, tiled=True)  8.33 us
    all_to_all x1, starting transfers between devices, on_device(): back = lax.all_to_all(lent, 'inst', split_axis=0, concat_axis=0, tiled=True)  7.24 us
    ppermute x1, waiting for transfers between devices, on_device(): lax.ppermute(before, 'tp', x_shift(1))  4.14 us
    all_to_all x1, starting transfers between devices, on_device(): lax.all_to_all(partial, 'tp', split_axis=0, concat_axis=0, tiled=True)  3.98 us
    pallas_call x1, Pallas kernels, on_device(): pl.pallas_call(functools.partial(attend_own, groups), in_specs=[hbm] * 3,...  3.89 us
  transfers between devices with their start and end apart: 9, of which 6 were waited for; matrix products, arithmetic and copies ran while one was open for 1% of the time, Pallas kernels for 15%

profile of v8, /device:TPU:1, one launch (start us, length us, event | category | flops | bytes accessed | tf_op | source)
XLA Modules:
  0.0 81.4 jit_solution(16280031112316058545)
XLA Ops:
  0.0 1.7 %prepare.1 = (bf16[384,128]{1,0:T(8,128)(2,1)}, f32[8,32]{1,0:T(8,128)}) custom-call(bf16[3,8,512]{2,1,0:T(8,128)(2,1)} %q_ref.1, s32[16,16]{1,0:T(8,128)} %owner_hbm.1), custom_call_target="tpu_custom_call" | custom-call | tf_op jit(solution)/shard_map/prepare/pallas_call | solution.py:416
  1.7 10.0 %all-to-all-start = ((bf16[16,24,128]{2,1,0:T(8,128)(2,1)}), bf16[16,24,128]{2,1,0:T(8,128)(2,1)S(1)}, u32[]{:S(2)}, u32[]{:S(2)}) async-start(bf16[16,24,128]{2,1,0:T(8,128)(2,1)} %bitcast.15), calls=%async_computation | async-start | bytes 196608 | tf_op jit(solution)/shard_map/all_to_all | solution.py:433
  11.7 0.0 copy-start.2
  11.7 0.7 copy-done.2
  12.4 0.0 copy-start.3
  12.4 0.7 copy-done.3
  13.1 0.0 copy-start.4
  13.1 0.7 copy-done.4
  13.8 2.4 %make_plan.1 = (s32[8,16]{1,0:T(8,128)S(1)}, f32[16,32]{1,0:T(8,128)S(1)}, f32[32,16]{1,0:T(8,128)S(1)}) custom-call(s32[16,16]{1,0:T(8,128)S(1)} %copy-done.2, s32[16,16]{1,0:T(8,128)S(1)} %copy-done.3, s32[16,16]{1,0:T(8,128)S(1)} %copy-done.4), custom_call_target="tpu_custom_call" | custom-call | tf_op jit(solution)/shard_map/make_plan/pallas_call | solution.py:435
  16.2 0.0 copy-start.1
  16.2 0.6 copy-done.1
  16.8 3.4 %all-to-all-done = bf16[16,24,128]{2,1,0:T(8,128)(2,1)S(1)} async-done(((bf16[16,24,128]{2,1,0:T(8,128)(2,1)}), bf16[16,24,128]{2,1,0:T(8,128)(2,1)S(1)}, u32[]{:S(2)}, u32[]{:S(2)}) %all-to-all-start) | async-done | bytes 98336 | tf_op jit(solution)/shard_map/all_to_all | solution.py:433
  20.2 0.2 pick_ranges.1
  20.4 1.3 %collective-permute-start = (bf16[16,1536]{1,0:T(8,128)(2,1)S(1)}, bf16[16,1536]{1,0:T(8,128)(2,1)S(1)}, u32[]{:S(2)}, u32[]{:S(2)}) collective-permute-start(bf16[16,1536]{1,0:T(8,128)(2,1)S(1)} %pick_ranges.1), channel_id=1, source_target_pairs={{0,1},{1,2},{2,3},{3,0},{4,5},{5,6},{6,7},{7,4},{8,9},{9,10},{10,1... | collective-permute-start | bytes 147464 | tf_op jit(solution)/shard_map/ppermute | solution.py:459
  21.7 1.5 %collective-permute-start.1 = (bf16[16,1536]{1,0:T(8,128)(2,1)S(1)}, bf16[16,1536]{1,0:T(8,128)(2,1)S(1)}, u32[]{:S(2)}, u32[]{:S(2)}) collective-permute-start(bf16[16,1536]{1,0:T(8,128)(2,1)S(1)} %pick_ranges.1), channel_id=1, source_target_pairs={{0,3},{1,0},{2,1},{3,2},{4,7},{5,4},{6,5},{7,6},{8,11},{9,8},{10,9... | collective-permute-start | bytes 147464 | tf_op jit(solution)/shard_map/ppermute | solution.py:459
  23.1 2.0 %collective-permute-done = bf16[16,1536]{1,0:T(8,128)(2,1)S(1)} collective-permute-done((bf16[16,1536]{1,0:T(8,128)(2,1)S(1)}, bf16[16,1536]{1,0:T(8,128)(2,1)S(1)}, u32[]{:S(2)}, u32[]{:S(2)}) %collective-permute-start) | collective-permute-done | bytes 49184 | tf_op jit(solution)/shard_map/ppermute | solution.py:459
  25.1 0.0 collective-permute-start.2
  25.1 0.0 collective-permute-done.1
  25.1 4.1 %collective-permute-done.2 = bf16[16,1536]{1,0:T(8,128)(2,1)S(1)} collective-permute-done((bf16[16,1536]{1,0:T(8,128)(2,1)S(1)}, bf16[16,1536]{1,0:T(8,128)(2,1)S(1)}, u32[]{:S(2)}, u32[]{:S(2)}) %collective-permute-start.2) | collective-permute-done | bytes 49184 | tf_op jit(solution)/shard_map/ppermute | solution.py:460
  29.3 0.0 copy-start.6
  29.3 1.4 %collective-permute-start.3 = (bf16[4,16,1536]{2,1,0:T(8,128)(2,1)S(1)}, bf16[4,16,1536]{2,1,0:T(8,128)(2,1)}, u32[]{:S(2)}, u32[]{:S(2)}) collective-permute-start(bf16[4,16,1536]{2,1,0:T(8,128)(2,1)S(1)} %pad_maximum_fusion.block), channel_id=1, source_target_pairs={{0,4},{1,5},{2,6},{3,7},{4,8},{5,9},{6,10},{7,11},{8,12},{9,13},{1... | collective-permute-start | bytes 589832 | tf_op jit(solution)/shard_map/ppermute | solution.py:461
  30.7 1.5 %collective-permute-start.5 = (bf16[4,16,1536]{2,1,0:T(8,128)(2,1)S(1)}, bf16[4,16,1536]{2,1,0:T(8,128)(2,1)}, u32[]{:S(2)}, u32[]{:S(2)}) collective-permute-start(bf16[4,16,1536]{2,1,0:T(8,128)(2,1)S(1)} %pad_maximum_fusion.block), channel_id=1, source_target_pairs={{0,12},{1,13},{2,14},{3,15},{4,0},{5,1},{6,2},{7,3},{8,4},{9,5},{1... | collective-permute-start | bytes 589832 | tf_op jit(solution)/shard_map/ppermute | solution.py:461
  32.2 0.0 copy-done.6
  32.2 3.9 %attend_own.1.refs_3_ = bf16[16,16,1664]{2,1,0:T(8,128)(2,1)} custom-call(s32[8,16]{1,0:T(8,128)} %copy-done.1, bf16[4,16,1536]{2,1,0:T(8,128)(2,1)} %copy-done.6, bf16[128,2,16,1024]{3,2,1,0:T(8,128)(2,1)} %refs_1_.1), custom_call_target="tpu_custom_call" | custom-call | flops 1000000000 | bytes 8388608 | tf_op jit(solution)/shard_map/attend_own/pallas_call | solution.py:468
  36.1 0.0 collective-permute-done.3.refs_0_
  36.1 0.1 collective-permute-start.4
  36.2 0.0 collective-permute-done.5.refs_1_
  36.2 5.9 %attend_others.2.refs_2_ = bf16[16,16,1664]{2,1,0:T(8,128)(2,1)} custom-call(s32[8,16]{1,0:T(8,128)} %copy-done.1, bf16[4,16,1536]{2,1,0:T(8,128)(2,1)} %collective-permute-done.3.refs_0_, bf16[4,16,1536]{2,1,0:T(8,128)(2,1)} %collective-permute-done.5.refs_1_, bf16[128,2,16,1024]{3,2,1,0:T(8,128)(2,1)} %refs_1_.1, ...), custom_call_target="tpu_custom_call", output_to_operand_aliasing={{}: (4, {})} | custom-call | flops 2000000000 | bytes 8388608 | tf_op jit(solution)/shard_map/attend_others/pallas_call | solution.py:490
  42.2 0.0 copy-start
  42.2 0.0 copy-start.5
  42.2 0.1 collective-permute-done.4.refs_0_
  42.3 3.9 %attend_others.3 = bf16[16,16,1664]{2,1,0:T(8,128)(2,1)} custom-call(s32[8,16]{1,0:T(8,128)} %copy-done.1, bf16[4,16,1536]{2,1,0:T(8,128)(2,1)} %collective-permute-done.4.refs_0_, bf16[128,2,16,1024]{3,2,1,0:T(8,128)(2,1)} %refs_1_.1, bf16[16,16,1664]{2,1,0:T(8,128)(2,1)} %attend_others.2.refs_2_), custom_call_target="tpu_custom_call", output_to_operand_aliasing={{}: (3, {})} | custom-call | flops 1000000000 | bytes 4194304 | tf_op jit(solution)/shard_map/attend_others/pallas_call | solution.py:490
  46.2 4.0 %all-to-all-start.1 = ((bf16[16,16,1664]{2,1,0:T(8,128)(2,1)}), bf16[16,16,1664]{2,1,0:T(8,128)(2,1)S(1)}, u32[]{:S(2)}, u32[]{:S(2)}) async-start(bf16[16,16,1664]{2,1,0:T(8,128)(2,1)} %attend_others.3), calls=%async_computation.1 | async-start | bytes 1703936 | tf_op jit(solution)/shard_map/all_to_all | solution.py:512
  50.2 12.2 %all-to-all-done.1.in_ref = bf16[16,16,1664]{2,1,0:T(8,128)(2,1)S(1)} async-done(((bf16[16,16,1664]{2,1,0:T(8,128)(2,1)}), bf16[16,16,1664]{2,1,0:T(8,128)(2,1)S(1)}, u32[]{:S(2)}, u32[]{:S(2)}) %all-to-all-start.1) | async-done | bytes 852000 | tf_op jit(solution)/shard_map/all_to_all | solution.py:512
  62.4 1.5 %merge_sources.1 = bf16[512,128]{1,0:T(8,128)(2,1)} custom-call(f32[32,16]{1,0:T(8,128)S(1)} %get-tuple-element.12.put_ref, bf16[16,16,1664]{2,1,0:T(8,128)(2,1)S(1)} %all-to-all-done.1.in_ref), custom_call_target="tpu_custom_call" | custom-call | tf_op jit(solution)/shard_map/merge_sources/pallas_call | solution.py:513
  63.9 7.2 %all-to-all-start.2 = ((bf16[16,32,128]{2,1,0:T(8,128)(2,1)}), bf16[16,32,128]{2,1,0:T(8,128)(2,1)S(1)}, u32[]{:S(2)}, u32[]{:S(2)}) async-start(bf16[16,32,128]{2,1,0:T(8,128)(2,1)} %bitcast.6), calls=%async_computation.2 | async-start | bytes 262144 | tf_op jit(solution)/shard_map/all_to_all | solution.py:522
  71.1 0.9 %constant_dynamic-slice_fusion.1 = (bf16[3,8,1,128]{3,2,1,0:T(2,128)(2,1)S(1)}, bf16[3,8,1,128]{3,2,1,0:T(2,128)(2,1)S(1)}) fusion(bf16[3,8,2,1024]{3,2,1,0:T(2,128)(2,1)} %param.7, s32[]{:T(128)S(6)} %add.5, s32[]{:T(128)S(6)} %select_n.9), kind=kLoop, calls=%fused_computation.4 | loop fusion | bytes 24584 | tf_op jit(solution)/shard_map/slice | solution.py:531
  72.0 8.3 %all-to-all-done.2 = bf16[16,32,128]{2,1,0:T(8,128)(2,1)S(1)} async-done(((bf16[16,32,128]{2,1,0:T(8,128)(2,1)}), bf16[16,32,128]{2,1,0:T(8,128)(2,1)S(1)}, u32[]{:S(2)}, u32[]{:S(2)}) %all-to-all-start.2) | async-done | bytes 131104 | tf_op jit(solution)/shard_map/all_to_all | solution.py:522
  80.3 0.0 copy-done
  80.3 0.0 copy-done.5
  80.3 1.0 %finish.1 = bf16[3,8,512]{2,1,0:T(8,128)(2,1)} custom-call(bf16[512,128]{1,0:T(8,128)(2,1)S(1)} %bitcast.12, f32[8,32]{1,0:T(8,128)S(1)} %copy-done.5, bf16[3,8,512]{2,1,0:T(8,128)(2,1)S(1)} %copy-done, bf16[3,8,128]{2,1,0:T(8,128)(2,1)S(1)} %get-tuple-element.22.k_ref, bf16[3,8,128]{2,1,0:T(8,128)(2,1)S(1)} %get-tuple-element.21.v_ref), custom_call_target="tpu_custom_call" | custom-call | tf_op jit(solution)/shard_map/finish/pallas_call | solution.py:523
  (2 shorter events, 0.0 us)
Async XLA Ops:
  1.7 18.5 %all-to-all-start = ((bf16[16,24,128]{2,1,0:T(8,128)(2,1)}), bf16[16,24,128]{2,1,0:T(8,128)(2,1)S(1)}, u32[]{:S(2)}, u32[]{:S(2)}) async-start(bf16[16,24,128]{2,1,0:T(8,128)(2,1)} %bitcast.15), calls=%async_computation | async-start | bytes 196608 | tf_op jit(solution)/shard_map/all_to_all | solution.py:433
  11.7 0.7 copy-start.2
  12.4 0.7 copy-start.3
  13.1 0.7 copy-start.4
  16.2 0.6 copy-start.1
  20.4 4.7 %collective-permute-start = (bf16[16,1536]{1,0:T(8,128)(2,1)S(1)}, bf16[16,1536]{1,0:T(8,128)(2,1)S(1)}, u32[]{:S(2)}, u32[]{:S(2)}) collective-permute-start(bf16[16,1536]{1,0:T(8,128)(2,1)S(1)} %pick_ranges.1), channel_id=1, source_target_pairs={{0,1},{1,2},{2,3},{3,0},{4,5},{5,6},{6,7},{7,4},{8,9},{9,10},{10,1... | collective-permute-start | bytes 147464 | tf_op jit(solution)/shard_map/ppermute | solution.py:459
  21.7 3.5 %collective-permute-start.1 = (bf16[16,1536]{1,0:T(8,128)(2,1)S(1)}, bf16[16,1536]{1,0:T(8,128)(2,1)S(1)}, u32[]{:S(2)}, u32[]{:S(2)}) collective-permute-start(bf16[16,1536]{1,0:T(8,128)(2,1)S(1)} %pick_ranges.1), channel_id=1, source_target_pairs={{0,3},{1,0},{2,1},{3,2},{4,7},{5,4},{6,5},{7,6},{8,11},{9,8},{10,9... | collective-permute-start | bytes 147464 | tf_op jit(solution)/shard_map/ppermute | solution.py:459
  25.1 4.2 %collective-permute-start.2 = (bf16[16,1536]{1,0:T(8,128)(2,1)S(1)}, bf16[16,1536]{1,0:T(8,128)(2,1)S(1)}, u32[]{:S(2)}, u32[]{:S(2)}) collective-permute-start(bf16[16,1536]{1,0:T(8,128)(2,1)S(1)} %collective-permute-done), channel_id=1, source_target_pairs={{0,1},{1,2},{2,3},{3,0},{4,5},{5,6},{6,7},{7,4},{8,9},{9,10},{10,1... | collective-permute-start | bytes 147464 | tf_op jit(solution)/shard_map/ppermute | solution.py:460
  29.3 2.9 %copy-start.6 = (bf16[4,16,1536]{2,1,0:T(8,128)(2,1)}, bf16[4,16,1536]{2,1,0:T(8,128)(2,1)S(1)}, u32[]{:S(2)}) copy-start(bf16[4,16,1536]{2,1,0:T(8,128)(2,1)S(1)} %pad_maximum_fusion.block) | copy-start | bytes 589828
  29.3 6.8 %collective-permute-start.3 = (bf16[4,16,1536]{2,1,0:T(8,128)(2,1)S(1)}, bf16[4,16,1536]{2,1,0:T(8,128)(2,1)}, u32[]{:S(2)}, u32[]{:S(2)}) collective-permute-start(bf16[4,16,1536]{2,1,0:T(8,128)(2,1)S(1)} %pad_maximum_fusion.block), channel_id=1, source_target_pairs={{0,4},{1,5},{2,6},{3,7},{4,8},{5,9},{6,10},{7,11},{8,12},{9,13},{1... | collective-permute-start | bytes 589832 | tf_op jit(solution)/shard_map/ppermute | solution.py:461
  30.7 5.5 %collective-permute-start.5 = (bf16[4,16,1536]{2,1,0:T(8,128)(2,1)S(1)}, bf16[4,16,1536]{2,1,0:T(8,128)(2,1)}, u32[]{:S(2)}, u32[]{:S(2)}) collective-permute-start(bf16[4,16,1536]{2,1,0:T(8,128)(2,1)S(1)} %pad_maximum_fusion.block), channel_id=1, source_target_pairs={{0,12},{1,13},{2,14},{3,15},{4,0},{5,1},{6,2},{7,3},{8,4},{9,5},{1... | collective-permute-start | bytes 589832 | tf_op jit(solution)/shard_map/ppermute | solution.py:461
  36.1 6.1 %collective-permute-start.4 = (bf16[4,16,1536]{2,1,0:T(8,128)(2,1)}, bf16[4,16,1536]{2,1,0:T(8,128)(2,1)}, u32[]{:S(2)}, u32[]{:S(2)}) collective-permute-start(bf16[4,16,1536]{2,1,0:T(8,128)(2,1)} %collective-permute-done.3.refs_0_), channel_id=1, source_target_pairs={{0,4},{1,5},{2,6},{3,7},{4,8},{5,9},{6,10},{7,11},{8,12},{9,13},{1... | collective-permute-start | bytes 589832 | tf_op jit(solution)/shard_map/ppermute | solution.py:487
  42.2 38.2 %copy-start = (bf16[3,8,512]{2,1,0:T(8,128)(2,1)S(1)}, bf16[3,8,512]{2,1,0:T(8,128)(2,1)}, u32[]{:S(2)}) copy-start(bf16[3,8,512]{2,1,0:T(8,128)(2,1)} %q_ref.1) | copy-start | bytes 73732
  42.2 38.1 %copy-start.5 = (f32[8,32]{1,0:T(8,128)S(1)}, f32[8,32]{1,0:T(8,128)}, u32[]{:S(2)}) copy-start(f32[8,32]{1,0:T(8,128)} %get-tuple-element.18.owner_ref) | copy-start | bytes 3076
  46.2 16.2 %all-to-all-start.1 = ((bf16[16,16,1664]{2,1,0:T(8,128)(2,1)}), bf16[16,16,1664]{2,1,0:T(8,128)(2,1)S(1)}, u32[]{:S(2)}, u32[]{:S(2)}) async-start(bf16[16,16,1664]{2,1,0:T(8,128)(2,1)} %attend_others.3), calls=%async_computation.1 | async-start | bytes 1703936 | tf_op jit(solution)/shard_map/all_to_all | solution.py:512
  63.9 16.5 %all-to-all-start.2 = ((bf16[16,32,128]{2,1,0:T(8,128)(2,1)}), bf16[16,32,128]{2,1,0:T(8,128)(2,1)S(1)}, u32[]{:S(2)}, u32[]{:S(2)}) async-start(bf16[16,32,128]{2,1,0:T(8,128)(2,1)} %bitcast.6), calls=%async_computation.2 | async-start | bytes 262144 | tf_op jit(solution)/shard_map/all_to_all | solution.py:522
